TPU v7x, 32 devices: a whole 2x2x4 slice. The times are simulated.
32 devices in a mesh: bead: 16 (over z, y, x), slab: 2 (over core).
Axes of the slice: x: 2, y: 2, z: 4, core: 2. Of those that a mesh axis runs over, the one named last changes fastest.
Arguments:
- positions: float32 [3, 16, 256], P(None, 'bead', 'slab'), may hold values from -5 to 5
- velocities: float32 [3, 16, 256], P(None, 'bead', 'slab'), may hold values from -5 to 5
- atom_types: int32 [256], P('slab'), may hold values from 0 to 1
- live_atoms: int32 [2], P('slab'), may hold values from 16 to 128, as said below
- halo_rows: int32 [2, 128], P('slab'), may hold values from 0 to 127, as said below
- neighbours: int32 [256, 128], P('slab'), may hold values from -1 to 255, as said below
- type_scale: float32 [2, 25], replicated, may hold values from -4 to 4
- type_shift: float32 [2, 25], replicated, may hold values from -4 to 4
- embed_two: bfloat16 [25, 50], replicated, may hold values from -1.25 to 1.25
- embed_bias_two: float32 [50], replicated, may hold values from -3 to 3
- embed_three: bfloat16 [50, 100], replicated, may hold values from -0.875 to 0.875
- embed_bias_three: float32 [100], replicated, may hold values from -3 to 3
- fit_first: bfloat16 [1600, 240], replicated, may hold values from -0.625 to 0.625
- fit_bias_first: float32 [240], replicated, may hold values from -3 to 3
- fit_second: bfloat16 [240, 240], replicated, may hold values from -0.375 to 0.375
- fit_bias_second: float32 [240], replicated, may hold values from -3 to 3
- fit_third: bfloat16 [240, 240], replicated, may hold values from -0.375 to 0.375
- fit_bias_third: float32 [240], replicated, may hold values from -3 to 3
- fit_readout: float32 [2, 240], replicated, may hold values from -0.375 to 0.375
Outputs:
- positions_new: float32 [3, 16, 256], P(None, 'bead', 'slab')
- velocities_new: float32 [3, 16, 256], P(None, 'bead', 'slab')
- forces: float32 [3, 16, 256], P(None, 'bead', 'slab')
Inputs may be any that keep to these rules, and one draw needn't show every extreme that they name: Slab s holds atoms in its first live_atoms[s] rows; one slab is full. The system is a water film with vacuum on both sides, so slabs crossing the vacuum hold few atoms. `halo_rows`: each entry is an occupied row of its slab; the first 64 of a slab go to the slab one lower (cyclic), the other 64 to the slab one higher. `neighbours`: -1 marks an empty slot; entries below 128 are occupied own rows of the slab, never the atom itself; entries from 128 on index the extended list's halo part. Rows at or past a slab's live count are all empty; an occupied row has between 64 and 128 filled slots, first, and some row of each slab has 128.
All inputs are finite; a program needn't handle non-finite values.
Results may differ from a plain program's by a relative error of at most 0.014.
Values sent between devices are 32-bit elements; how exact they have to be, the bound alone decides.
No kernel may reach another device: no remote copies, remote signals or barrier semaphores. Data moves between devices by JAX's collectives and lax.ppermute only.
A program may use at most 64 MiB of HBM per device.

v0:
```python
import jax
import jax.numpy as jnp
from jax import lax
from jax.sharding import PartitionSpec as P

M2 = 16
BLOCK = 32


step_size = 0.25
phase_rate = 1.2
cutoff_sq = 16.0
softening = 0.25
heavy_mass = 16.0
highest = lax.Precision.HIGHEST


def padded_2(cells, sides, width):
    for axis, dim in sides:
        count = lax.axis_size(axis)
        head = lax.slice_in_dim(cells, 0, width, axis=dim)
        tail = lax.slice_in_dim(cells, cells.shape[dim] - width, cells.shape[dim], axis=dim)
        cells = jnp.concatenate(
            [
                lax.ppermute(tail, axis, [(i, (i + 1) % count) for i in range(count)]),
                cells,
                lax.ppermute(head, axis, [((i + 1) % count, i) for i in range(count)]),
            ],
            axis=dim,
        )
    return cells


def mode_tables(bead_count):
    indices = jnp.arange(bead_count)
    bead_rows = indices[:, None].astype(jnp.float32)
    mode_cols = indices[None, :]
    mode_float = mode_cols.astype(jnp.float32)
    angles = 2.0 * jnp.pi * bead_rows * mode_float / bead_count
    norm_scale = jnp.sqrt(2.0 / bead_count)
    middle = bead_count // 2
    edge_value = 1.0 / jnp.sqrt(1.0 * bead_count)
    mode_basis = jnp.where(
        mode_cols == 0,
        edge_value,
        jnp.where(
            mode_cols < middle,
            norm_scale * jnp.cos(angles),
            jnp.where(
                mode_cols == middle,
                jnp.cos(jnp.pi * bead_rows) * edge_value,
                norm_scale * jnp.sin(angles),
            ),
        ),
    )
    sine_part = jnp.sin(jnp.pi * indices.astype(jnp.float32) / bead_count)
    ratio = 2.0 * sine_part
    phases = phase_rate * bead_count * sine_part
    guarded = jnp.where(indices == 0, 1.0, ratio)
    cosine = jnp.cos(phases)
    travel = jnp.where(indices == 0, 1.0, jnp.sin(phases) / guarded)
    spring = ratio * jnp.sin(phases)
    return (mode_basis, cosine, travel, spring)


def block_energy(centre, beside_all, around_hydrogen, filled, centre_hydrogen, living, weights):
    (
        type_scale,
        type_shift,
        embed_two,
        embed_bias_two,
        embed_three,
        embed_bias_three,
        fit_first,
        fit_bias_first,
        fit_second,
        fit_bias_second,
        fit_third,
        fit_bias_third,
        fit_readout,
    ) = weights
    offsets = beside_all - centre[:, :, None]
    dist_sq = jnp.sum(offsets * offsets, axis=0)
    softened = jnp.sqrt(dist_sq + softening)
    switch = jnp.maximum(1.0 - dist_sq / cutoff_sq, 0.0)
    strength = filled * switch * switch / softened
    environ = jnp.concatenate([strength[None], strength[None] * offsets / softened[None]], axis=0)
    block_rows, slot_count = strength.shape
    input_scale = type_scale[0] + around_hydrogen[..., None] * (type_scale[1] - type_scale[0])
    input_shift = type_shift[0] + around_hydrogen[..., None] * (type_shift[1] - type_shift[0])
    layer_one = jnp.tanh(strength[..., None] * input_scale + input_shift).reshape(
        block_rows * slot_count, -1
    )
    layer_two = jnp.tanh(
        jnp.dot(layer_one.astype(jnp.bfloat16), embed_two, preferred_element_type=jnp.float32)
        + embed_bias_two
    )
    layer_two = layer_two + jnp.concatenate([layer_one, layer_one], axis=1)
    layer_three = jnp.tanh(
        jnp.dot(layer_two.astype(jnp.bfloat16), embed_three, preferred_element_type=jnp.float32)
        + embed_bias_three
    )
    layer_three = layer_three + jnp.concatenate([layer_two, layer_two], axis=1)
    layer_three = layer_three.reshape(block_rows, slot_count, -1)
    features = jnp.einsum("bke,cbk->bec", layer_three, environ, precision=highest) / slot_count
    descriptor = jnp.einsum("bec,bfc->bef", features, features[:, :M2], precision=highest).reshape(
        block_rows, -1
    )
    fit_one = jnp.tanh(
        jnp.dot(descriptor.astype(jnp.bfloat16), fit_first, preferred_element_type=jnp.float32)
        + fit_bias_first
    )
    fit_two = (
        jnp.tanh(
            jnp.dot(fit_one.astype(jnp.bfloat16), fit_second, preferred_element_type=jnp.float32)
            + fit_bias_second
        )
        + fit_one
    )
    fit_three = (
        jnp.tanh(
            jnp.dot(fit_two.astype(jnp.bfloat16), fit_third, preferred_element_type=jnp.float32)
            + fit_bias_third
        )
        + fit_two
    )
    readout = fit_readout[0] + centre_hydrogen[:, None] * (fit_readout[1] - fit_readout[0])
    return jnp.sum(living * jnp.sum(fit_three * readout, axis=1))


def block_gradient(gradient, extended, wide_hydrogen, listed, first_row, living, weights):
    centre = lax.dynamic_slice_in_dim(extended, first_row, BLOCK, 1)
    filled = (listed >= 0).astype(jnp.float32)
    flat_rows = jnp.where(listed >= 0, listed, 0).reshape(-1)
    beside_all = extended[:, flat_rows].reshape(3, BLOCK, -1)
    around_hydrogen = wide_hydrogen[flat_rows].reshape(BLOCK, -1)
    centre_hydrogen = lax.dynamic_slice_in_dim(wide_hydrogen, first_row, BLOCK, 0)

    def energy_of(centre_in, around_in):
        return block_energy(
            centre_in, around_in, around_hydrogen, filled, centre_hydrogen, living, weights
        )

    energy, backward = jax.vjp(energy_of, centre, beside_all)
    grad_centre, grad_around = backward(jnp.ones_like(energy))
    gradient = gradient.at[:, flat_rows].add(grad_around.reshape(3, -1))
    current = lax.dynamic_slice_in_dim(gradient, first_row, BLOCK, 1)
    return lax.dynamic_update_slice_in_dim(gradient, current + grad_centre, first_row, 1)


def slab_gradient(extended, wide_hydrogen, slab_lists, live_count, block_count, weights):

    def add_block(block_index, gradient):
        first_row = block_index * BLOCK
        listed = lax.dynamic_slice_in_dim(slab_lists, first_row, BLOCK, 0)
        row_numbers = first_row + jnp.arange(BLOCK)
        living = (row_numbers < live_count).astype(jnp.float32)
        return block_gradient(gradient, extended, wide_hydrogen, listed, first_row, living, weights)

    zeroed = jnp.zeros(extended.shape, jnp.float32)
    return lax.fori_loop(0, block_count, add_block, zeroed)


def own_slab_force(local_field, hydrogen, live_atoms, halo_rows, neighbours, weights):
    atom_count = local_field.shape[1]
    outgoing = halo_rows[0]
    halo_half = outgoing.shape[0] // 2
    sending = jnp.concatenate([local_field[:, outgoing], hydrogen[outgoing][None]], axis=0)
    padded = padded_2(sending, (("slab", 1),), halo_half)
    extended = jnp.concatenate(
        [local_field, padded[:3, :halo_half], padded[:3, 3 * halo_half :]], axis=1
    )
    wide_hydrogen = jnp.concatenate([hydrogen, padded[3, :halo_half], padded[3, 3 * halo_half :]])
    live_count = live_atoms[0]
    block_count = (live_count + BLOCK - 1) // BLOCK
    gradient = slab_gradient(extended, wide_hydrogen, neighbours, live_count, block_count, weights)
    returned = padded_2(gradient[:, atom_count:], (("slab", 1),), halo_half)
    own_force = gradient[:, :atom_count]
    own_force = own_force.at[:, outgoing[:halo_half]].add(returned[:, :halo_half])
    own_force = own_force.at[:, outgoing[halo_half:]].add(returned[:, 3 * halo_half :])
    return -own_force


def exchange_apply(bead_field, mode_basis, first_gain, second_gain):
    amplitudes = jnp.einsum(
        "jk,cja->cka",
        mode_basis,
        lax.all_to_all(bead_field[:, None, :], "bead", split_axis=2, concat_axis=1, tiled=True),
        precision=highest,
    )
    upper_part = jnp.einsum(
        "jk,cka->cja", mode_basis, amplitudes * first_gain[None, :, None], precision=highest
    )
    lower_part = jnp.einsum(
        "jk,cka->cja", mode_basis, amplitudes * second_gain[None, :, None], precision=highest
    )
    return (
        lax.all_to_all(upper_part, "bead", split_axis=1, concat_axis=2, tiled=True)[:, 0, :],
        lax.all_to_all(lower_part, "bead", split_axis=1, concat_axis=2, tiled=True)[:, 0, :],
    )


def local(
    positions,
    velocities,
    atom_types,
    live_atoms,
    halo_rows,
    neighbours,
    type_scale,
    type_shift,
    embed_two,
    embed_bias_two,
    embed_three,
    embed_bias_three,
    fit_first,
    fit_bias_first,
    fit_second,
    fit_bias_second,
    fit_third,
    fit_bias_third,
    fit_readout,
):
    weights = (
        type_scale,
        type_shift,
        embed_two,
        embed_bias_two,
        embed_three,
        embed_bias_three,
        fit_first,
        fit_bias_first,
        fit_second,
        fit_bias_second,
        fit_third,
        fit_bias_third,
        fit_readout,
    )
    hydrogen = (atom_types == 1).astype(jnp.float32)
    local_field = positions[:, 0, :]
    forces = own_slab_force(local_field, hydrogen, live_atoms, halo_rows, neighbours, weights)
    inverse_mass = jnp.where(atom_types == 1, 1.0, 1.0 / heavy_mass)
    kicked = velocities[:, 0, :] + step_size * inverse_mass[None, :] * forces
    bead_count = lax.axis_size("bead")
    mode_basis, cosine, travel, spring = mode_tables(bead_count)
    from_positions = exchange_apply(local_field, mode_basis, cosine, -spring)
    from_velocities = exchange_apply(kicked, mode_basis, travel, cosine)
    positions_new = from_positions[0] + from_velocities[0]
    velocities_new = from_positions[1] + from_velocities[1]
    return (positions_new[:, None, :], velocities_new[:, None, :], forces[:, None, :])


def solution(mesh):
    return jax.shard_map(
        local,
        mesh=mesh,
        in_specs=(
            P(None, "bead", "slab"),
            P(None, "bead", "slab"),
            P("slab"),
            P("slab"),
            P("slab", None),
            P("slab", None),
            P(),
            P(),
            P(),
            P(),
            P(),
            P(),
            P(),
            P(),
            P(),
            P(),
            P(),
            P(),
            P(),
        ),
        out_specs=(P(None, "bead", "slab"), P(None, "bead", "slab"), P(None, "bead", "slab")),
        check_vma=False,
    )
```

profile of v0, /device:TPU:0, one launch (start us, length us, event | category | flops | bytes accessed | tf_op | source)
XLA Modules:
  0.0 507.0 jit_solution(14615083480512017695)
XLA Ops:
  2.0 8.4 %all-to-all-start = ((f32[3,1,128]{0,1,2:T(1,128)}), f32[3,1,128]{0,1,2:T(1,128)}, u32[]{:S(2)}, u32[]{:S(2)}) async-start(f32[3,1,128]{0,1,2:T(1,128)} %copy.96), calls=%async_computation | async-start | bytes 131072 | tf_op jit(solution)/shard_map/all_to_all | solution.py:188
  24.8 212.4 %while.11 = (s32[]{:T(128)}, f32[3,256]{0,1:T(8,128)S(1)}, s32[]{:T(128)}, s32[128,128]{1,0:T(8,128)}, f32[3,256]{0,1:T(8,128)S(1)}, /*index=5*/s32[]{:T(128)}, ...) while((s32[]{:T(128)}, f32[3,256]{0,1:T(8,128)S(1)}, ...), condition=%wide.region_7.8_spmd, body=%wide.region_0.7_spmd.sunk | while | flops 241789632 | bytes 47924876 | solution.py:161
  26.2 10.8 %gather_fusion = f32[4096,3]{1,0:T(8,128)S(1)} fusion(f32[3,256]{0,1:T(8,128)S(1)} %get-tuple-element.566, s32[4096]{0:T(1024)S(1)} %broadcast_clamp_fusion.2), kind=kCustom, calls=%fused_computation.clone.1 | custom fusion | bytes 114688 | tf_op jit(solution)/shard_map/while/body/gather | solution.py:135
  38.9 25.7 %gather_fusion.1 = f32[4096]{0:T(1024)S(1)} fusion(f32[256]{0:T(256)S(1)} %get-tuple-element.569, s32[4096]{0:T(1024)S(1)} %broadcast_clamp_fusion.2), kind=kCustom, calls=%fused_computation.1.clone.1 | custom fusion | bytes 49152 | tf_op jit(solution)/shard_map/while/body/gather | solution.py:136
  69.3 4.2 fusion.266
  73.5 2.2 convolution_convert_fusion.8
  75.7 2.1 copy.150
  86.6 2.4 convolution_convert_fusion.9
  95.4 2.3 fusion.272
  97.9 2.9 fusion.273
  105.8 23.4 %scatter_fusion = f32[3,256]{0,1:T(8,128)S(1)} fusion(f32[3,256]{0,1:T(8,128)S(1)} %get-tuple-element.534, s32[4096]{0:T(1024)S(1)} %bitcast.236, f32[4096,3]{1,0:T(8,128)S(1)} %copy.155), kind=kCustom, calls=%fused_computation.4.clone.1 | custom fusion | flops 12288 | bytes 163840 | tf_op jit(solution)/shard_map/while/body/scatter-add | solution.py:146
  130.7 10.8 %gather_fusion = f32[4096,3]{1,0:T(8,128)S(1)} fusion(f32[3,256]{0,1:T(8,128)S(1)} %get-tuple-element.566, s32[4096]{0:T(1024)S(1)} %broadcast_clamp_fusion.2), kind=kCustom, calls=%fused_computation.clone.1 | custom fusion | bytes 114688 | tf_op jit(solution)/shard_map/while/body/gather | solution.py:135
  143.4 25.7 %gather_fusion.1 = f32[4096]{0:T(1024)S(1)} fusion(f32[256]{0:T(256)S(1)} %get-tuple-element.569, s32[4096]{0:T(1024)S(1)} %broadcast_clamp_fusion.2), kind=kCustom, calls=%fused_computation.1.clone.1 | custom fusion | bytes 49152 | tf_op jit(solution)/shard_map/while/body/gather | solution.py:136
  173.8 4.2 fusion.266
  178.0 2.2 convolution_convert_fusion.8
  180.2 2.1 copy.150
  191.1 2.4 convolution_convert_fusion.9
  195.3 2.1 copy.152
  199.8 2.3 fusion.272
  202.3 2.9 fusion.273
  210.2 26.7 %scatter_fusion = f32[3,256]{0,1:T(8,128)S(1)} fusion(f32[3,256]{0,1:T(8,128)S(1)} %get-tuple-element.534, s32[4096]{0:T(1024)S(1)} %bitcast.236, f32[4096,3]{1,0:T(8,128)S(1)} %copy.155), kind=kCustom, calls=%fused_computation.4.clone.1 | custom fusion | flops 12288 | bytes 163840 | tf_op jit(solution)/shard_map/while/body/scatter-add | solution.py:146
  237.3 205.6 %collective-permute-start.2 = (f32[3,64]{0,1:T(8,128)S(1)}, f32[3,64]{0,1:T(8,128)S(1)}, u32[]{:S(2)}, u32[]{:S(2)}) collective-permute-start(f32[3,64]{0,1:T(8,128)S(1)} %get-tuple-element.321), channel_id=1, source_target_pairs={{0,1},{1,0},{2,3},{3,2},{4,5},{5,4},{6,7},{7,6},{8,9},{9,8},{10,11... | collective-permute-start | bytes 2312 | tf_op jit(solution)/shard_map/ppermute | solution.py:25
  447.3 6.9 %all-to-all-start.2 = ((f32[3,1,128]{0,1,2:T(1,128)}), f32[3,1,128]{0,1,2:T(1,128)S(1)}, u32[]{:S(2)}, u32[]{:S(2)}) async-start(f32[3,1,128]{0,1,2:T(1,128)} %bitcast.45), calls=%async_computation.2 | async-start | bytes 131072 | tf_op jit(solution)/shard_map/all_to_all | solution.py:188
  459.4 2.4 all-to-all-done.2
  461.7 4.6 all-to-all-start.1
  467.4 6.3 %all-to-all-done.1 = f32[3,16,8]{2,0,1:T(4,128)S(1)} async-done(((f32[3,16,8]{2,0,1:T(4,128)}), f32[3,16,8]{2,0,1:T(4,128)S(1)}, u32[]{:S(2)}, u32[]{:S(2)}) %all-to-all-start.1) | async-done | bytes 1568 | tf_op jit(solution)/shard_map/all_to_all | solution.py:198
  473.7 3.5 all-to-all-start.4
  478.2 6.3 %all-to-all-done.4 = f32[3,16,8]{2,0,1:T(4,128)S(1)} async-done(((f32[3,16,8]{2,0,1:T(4,128)}), f32[3,16,8]{2,0,1:T(4,128)S(1)}, u32[]{:S(2)}, u32[]{:S(2)}) %all-to-all-start.4) | async-done | bytes 1568 | tf_op jit(solution)/shard_map/all_to_all | solution.py:199
  484.6 3.5 all-to-all-start.3
  489.0 6.4 %all-to-all-done.3 = f32[3,16,8]{2,0,1:T(4,128)S(1)} async-done(((f32[3,16,8]{2,0,1:T(4,128)}), f32[3,16,8]{2,0,1:T(4,128)S(1)}, u32[]{:S(2)}, u32[]{:S(2)}) %all-to-all-start.3) | async-done | bytes 1568 | tf_op jit(solution)/shard_map/all_to_all | solution.py:198
  495.4 3.5 all-to-all-start.5
  500.2 6.1 %all-to-all-done.5 = f32[3,16,8]{2,0,1:T(4,128)S(1)} async-done(((f32[3,16,8]{2,0,1:T(4,128)}), f32[3,16,8]{2,0,1:T(4,128)S(1)}, u32[]{:S(2)}, u32[]{:S(2)}) %all-to-all-start.5) | async-done | bytes 1568 | tf_op jit(solution)/shard_map/all_to_all | solution.py:199
  (284 shorter events, 83.6 us)
Async XLA Ops:
  2.0 445.3 %all-to-all-start = ((f32[3,1,128]{0,1,2:T(1,128)}), f32[3,1,128]{0,1,2:T(1,128)}, u32[]{:S(2)}, u32[]{:S(2)}) async-start(f32[3,1,128]{0,1,2:T(1,128)} %copy.96), calls=%async_computation | async-start | bytes 131072 | tf_op jit(solution)/shard_map/all_to_all | solution.py:188
  14.6 9.8 %collective-permute-start.1 = (f32[4,64]{1,0:T(4,128)S(1)}, f32[4,64]{1,0:T(4,128)S(1)}, u32[]{:S(2)}, u32[]{:S(2)}) collective-permute-start(f32[4,64]{1,0:T(4,128)S(1)} %get-tuple-element.325), channel_id=1, source_target_pairs={{1,0},{0,1},{3,2},{2,3},{5,4},{4,5},{7,6},{6,7},{9,8},{8,9},{11,10... | collective-permute-start | bytes 3080 | tf_op jit(solution)/shard_map/ppermute | solution.py:27
  14.6 9.8 %collective-permute-start = (f32[4,64]{1,0:T(4,128)S(1)}, f32[4,64]{1,0:T(4,128)S(1)}, u32[]{:S(2)}, u32[]{:S(2)}) collective-permute-start(f32[4,64]{1,0:T(4,128)S(1)} %get-tuple-element.324), channel_id=1, source_target_pairs={{0,1},{1,0},{2,3},{3,2},{4,5},{5,4},{6,7},{7,6},{8,9},{9,8},{10,11... | collective-permute-start | bytes 3080 | tf_op jit(solution)/shard_map/ppermute | solution.py:25
  24.8 39.9 %copy-start = (f32[3,256]{0,1:T(8,128)}, f32[3,256]{0,1:T(8,128)S(1)}, u32[]{:S(2)}) copy-start(f32[3,256]{0,1:T(8,128)S(1)} %get-tuple-element.566) | copy-start | bytes 9220 | tf_op jit(solution)/shard_map/while
  38.9 26.7 %copy-start.2 = (f32[32,128]{1,0:T(8,128)}, f32[32,128]{1,0:T(8,128)S(1)}, u32[]{:S(2)}) copy-start(f32[32,128]{1,0:T(8,128)S(1)} %get-tuple-element.494) | copy-start | bytes 49156 | tf_op jit(solution)/shard_map/while
  38.9 26.7 %copy-start.26 = (f32[25]{0:T(128)}, f32[25]{0:T(128)S(1)}, u32[]{:S(2)}) copy-start(f32[25]{0:T(128)S(1)} %get-tuple-element.492) | copy-start | bytes 304 | tf_op jit(solution)/shard_map/while
  38.9 26.7 %copy-start.28 = (f32[25]{0:T(128)}, f32[25]{0:T(128)S(1)}, u32[]{:S(2)}) copy-start(f32[25]{0:T(128)S(1)} %get-tuple-element.493) | copy-start | bytes 304 | tf_op jit(solution)/shard_map/while
  38.9 26.7 %copy-start.25 = (bf16[25,50]{1,0:T(8,128)(2,1)S(1)}, bf16[25,50]{1,0:T(8,128)(2,1)}, u32[]{:S(2)}) copy-start(bf16[25,50]{1,0:T(8,128)(2,1)} %get-tuple-element.575) | copy-start | bytes 7504 | tf_op jit(solution)/shard_map/while
  38.9 26.7 %copy-start.30 = (f32[50]{0:T(128)S(1)}, f32[50]{0:T(128)}, u32[]{:S(2)}) copy-start(f32[50]{0:T(128)} %get-tuple-element.576) | copy-start | bytes 604 | tf_op jit(solution)/shard_map/while
  129.2 39.9 %copy-start = (f32[3,256]{0,1:T(8,128)}, f32[3,256]{0,1:T(8,128)S(1)}, u32[]{:S(2)}) copy-start(f32[3,256]{0,1:T(8,128)S(1)} %get-tuple-element.566) | copy-start | bytes 9220 | tf_op jit(solution)/shard_map/while
  142.7 26.4 %copy-start.18 = (f32[32,128]{1,0:T(8,128)}, f32[32,128]{1,0:T(8,128)S(1)}, u32[]{:S(2)}) copy-start(f32[32,128]{1,0:T(8,128)S(1)} %multiply_reduce_fusion.5) | copy-start | bytes 49156 | tf_op jit(solution)/shard_map/while
  143.3 26.7 %copy-start.2 = (f32[32,128]{1,0:T(8,128)}, f32[32,128]{1,0:T(8,128)S(1)}, u32[]{:S(2)}) copy-start(f32[32,128]{1,0:T(8,128)S(1)} %get-tuple-element.494) | copy-start | bytes 49156 | tf_op jit(solution)/shard_map/while
  143.3 26.7 %copy-start.26 = (f32[25]{0:T(128)}, f32[25]{0:T(128)S(1)}, u32[]{:S(2)}) copy-start(f32[25]{0:T(128)S(1)} %get-tuple-element.492) | copy-start | bytes 304 | tf_op jit(solution)/shard_map/while
  143.3 26.7 %copy-start.28 = (f32[25]{0:T(128)}, f32[25]{0:T(128)S(1)}, u32[]{:S(2)}) copy-start(f32[25]{0:T(128)S(1)} %get-tuple-element.493) | copy-start | bytes 304 | tf_op jit(solution)/shard_map/while
  143.3 26.7 %copy-start.25 = (bf16[25,50]{1,0:T(8,128)(2,1)S(1)}, bf16[25,50]{1,0:T(8,128)(2,1)}, u32[]{:S(2)}) copy-start(bf16[25,50]{1,0:T(8,128)(2,1)} %get-tuple-element.575) | copy-start | bytes 7504 | tf_op jit(solution)/shard_map/while
  143.3 26.7 %copy-start.30 = (f32[50]{0:T(128)S(1)}, f32[50]{0:T(128)}, u32[]{:S(2)}) copy-start(f32[50]{0:T(128)} %get-tuple-element.576) | copy-start | bytes 604 | tf_op jit(solution)/shard_map/while
  209.5 27.4 %copy-start.1 = (f32[3,256]{0,1:T(8,128)S(1)}, f32[3,256]{0,1:T(8,128)}, u32[]{:S(2)}) copy-start(f32[3,256]{0,1:T(8,128)} %copy-done) | copy-start | bytes 9220 | tf_op jit(solution)/shard_map/while
  237.2 240.0 %copy-start.34 = (f32[16]{0:T(128)S(1)}, f32[16]{0:T(128)}, u32[]{:S(2)}) copy-start(f32[16]{0:T(128)} %get-tuple-element.330) | copy-start | bytes 196
  237.2 240.0 %copy-start.35 = (f32[16]{0:T(128)S(1)}, f32[16]{0:T(128)}, u32[]{:S(2)}) copy-start(f32[16]{0:T(128)} %get-tuple-element.331) | copy-start | bytes 196
  237.2 240.0 %copy-start.36 = (pred[16]{0:T(512)(128)(4,1)S(1)}, pred[16]{0:T(512)(128)(4,1)}, u32[]{:S(2)}) copy-start(pred[16]{0:T(512)(128)(4,1)} %get-tuple-element.332) | copy-start | bytes 52
  237.2 240.0 %copy-start.37 = (pred[16]{0:T(512)(128)(4,1)S(1)}, pred[16]{0:T(512)(128)(4,1)}, u32[]{:S(2)}) copy-start(pred[16]{0:T(512)(128)(4,1)} %get-tuple-element.333) | copy-start | bytes 52
  237.2 240.0 %copy-start.38 = (f32[16]{0:T(128)S(1)}, f32[16]{0:T(128)}, u32[]{:S(2)}) copy-start(f32[16]{0:T(128)} %iota_convert_fusion) | copy-start | bytes 196
  237.2 240.0 %copy-start.39 = (pred[16]{0:T(512)(128)(4,1)S(1)}, pred[16]{0:T(512)(128)(4,1)}, u32[]{:S(2)}) copy-start(pred[16]{0:T(512)(128)(4,1)} %iota_compare_fusion.2) | copy-start | bytes 52
  237.2 240.0 %copy-start.41 = (f32[16]{0:T(128)S(1)}, f32[16]{0:T(128)}, u32[]{:S(2)}) copy-start(f32[16]{0:T(128)} %divide_select_fusion) | copy-start | bytes 196
  237.2 250.8 %copy-start.40 = (f32[16]{0:T(128)S(1)}, f32[16]{0:T(128)}, u32[]{:S(2)}) copy-start(f32[16]{0:T(128)} %multiply_cosine_fusion) | copy-start | bytes 196
  237.3 206.5 %collective-permute-start.2 = (f32[3,64]{0,1:T(8,128)S(1)}, f32[3,64]{0,1:T(8,128)S(1)}, u32[]{:S(2)}, u32[]{:S(2)}) collective-permute-start(f32[3,64]{0,1:T(8,128)S(1)} %get-tuple-element.321), channel_id=1, source_target_pairs={{0,1},{1,0},{2,3},{3,2},{4,5},{5,4},{6,7},{7,6},{8,9},{9,8},{10,11... | collective-permute-start | bytes 2312 | tf_op jit(solution)/shard_map/ppermute | solution.py:25
  442.8 2.1 collective-permute-start.3
  447.3 14.4 %all-to-all-start.2 = ((f32[3,1,128]{0,1,2:T(1,128)}), f32[3,1,128]{0,1,2:T(1,128)S(1)}, u32[]{:S(2)}, u32[]{:S(2)}) async-start(f32[3,1,128]{0,1,2:T(1,128)} %bitcast.45), calls=%async_computation.2 | async-start | bytes 131072 | tf_op jit(solution)/shard_map/all_to_all | solution.py:188
  461.7 12.0 %all-to-all-start.1 = ((f32[3,16,8]{2,0,1:T(4,128)}), f32[3,16,8]{2,0,1:T(4,128)S(1)}, u32[]{:S(2)}, u32[]{:S(2)}) async-start(f32[3,16,8]{2,0,1:T(4,128)} %copy.99), calls=%async_computation.1 | async-start | bytes 65536 | tf_op jit(solution)/shard_map/all_to_all | solution.py:198
  473.7 10.9 %all-to-all-start.4 = ((f32[3,16,8]{2,0,1:T(4,128)}), f32[3,16,8]{2,0,1:T(4,128)S(1)}, u32[]{:S(2)}, u32[]{:S(2)}) async-start(f32[3,16,8]{2,0,1:T(4,128)} %copy.110), calls=%async_computation.4 | async-start | bytes 65536 | tf_op jit(solution)/shard_map/all_to_all | solution.py:199
  484.6 10.9 %all-to-all-start.3 = ((f32[3,16,8]{2,0,1:T(4,128)}), f32[3,16,8]{2,0,1:T(4,128)S(1)}, u32[]{:S(2)}, u32[]{:S(2)}) async-start(f32[3,16,8]{2,0,1:T(4,128)} %copy.108), calls=%async_computation.3 | async-start | bytes 65536 | tf_op jit(solution)/shard_map/all_to_all | solution.py:198
  495.4 10.9 %all-to-all-start.5 = ((f32[3,16,8]{2,0,1:T(4,128)}), f32[3,16,8]{2,0,1:T(4,128)S(1)}, u32[]{:S(2)}, u32[]{:S(2)}) async-start(f32[3,16,8]{2,0,1:T(4,128)} %copy.111), calls=%async_computation.5 | async-start | bytes 65536 | tf_op jit(solution)/shard_map/all_to_all | solution.py:199
  (56 other events, 220.5 us)
where the time goes:
time: 510 us; the launch traced here: 507 us
  starting transfers between devices  236 us (46%)
  local copies, waits for them, and re-layouts  112 us (22%)
  other arithmetic  72 us (14%)
  matrix products  55.8 us (11%)
  waiting for transfers between devices  27.5 us (5%)
    ppermute x2, starting transfers between devices, padded_2(): lax.ppermute(tail, axis, [(i, (i + 1) % count) for i in range(count)])  206 us
    gather x2, local copies, waits for them, and re-layouts, block_gradient(): around_hydrogen = wide_hydrogen[flat_rows].reshape(BLOCK, -1)  51.5 us
    scatter-add x2, other arithmetic, block_gradient(): gradient = gradient.at[:, flat_rows].add(grad_around.reshape(3, -1))  50.1 us
    gather x4, local copies, waits for them, and re-layouts, block_gradient(): beside_all = extended[:, flat_rows].reshape(3, BLOCK, -1)  22.8 us
    dot_general x6, matrix products, block_energy(): jnp.einsum('bke,cbk->bec', layer_three, environ, precision=highest)  18.7 us
    all_to_all x2, starting transfers between devices, exchange_apply(): lax.all_to_all(bead_field[:, None, :], 'bead', split_axis=2, concat_axis=...  15.2 us
    all_to_all x2, waiting for transfers between devices, exchange_apply(): lax.all_to_all(upper_part, 'bead', split_axis=1, concat_axis=2, tiled=True)  12.7 us
    all_to_all x2, waiting for transfers between devices, exchange_apply(): lax.all_to_all(lower_part, 'bead', split_axis=1, concat_axis=2, tiled=True)  12.4 us
  transfers between devices with their start and end apart: 10, of which 5 were waited for; matrix products, arithmetic and copies ran while one was open for 46% of the time, Pallas kernels for 0%

commit v1 on v0

v1 whole, which is shorter than its diff:
```python
import functools
import math

import jax
import jax.numpy as jnp
import numpy as np
from jax import lax
from jax.experimental import pallas as pl
from jax.experimental.pallas import tpu as pltpu
from jax.sharding import PartitionSpec as P

M2 = 16
step_size = 0.25
phase_rate = 1.2
cutoff_sq = 16.0
softening = 0.25
heavy_mass = 16.0

F32 = jnp.float32
BF16 = jnp.bfloat16
LANES = 128
OCTET = 8
CHUNK = 32
ONE_AT = 20.0
VMEM_LIMIT = 48 * 1024 * 1024


def bead_tables(count):
    index = np.arange(count)
    angles = 2.0 * np.pi * np.outer(index, index) / count
    norm = math.sqrt(2.0 / count)
    edge = 1.0 / math.sqrt(count)
    middle = count // 2
    basis = np.where(
        index[None, :] == 0,
        edge,
        np.where(
            index[None, :] < middle,
            norm * np.cos(angles),
            np.where(
                index[None, :] == middle, np.cos(np.pi * index)[:, None] * edge, norm * np.sin(angles)
            ),
        ),
    )
    sine = np.sin(np.pi * index / count)
    ratio = 2.0 * sine
    phases = phase_rate * count * sine
    travel = np.where(index == 0, 1.0, np.sin(phases) / np.where(index == 0, 1.0, ratio))

    def assemble(diagonal):
        return (basis * diagonal[None, :]) @ basis.T

    return np.concatenate(
        [assemble(np.cos(phases)), assemble(travel), assemble(ratio * np.sin(phases))], axis=1
    ).astype(np.float32)


def lookup(table, indices):
    return jnp.take_along_axis(table, indices, axis=1, mode="promise_in_bounds")


def outgoing_kernel(positions_ref, types_ref, rows_ref, own_ref, send_ref):
    hydrogen = (types_ref[...] == 1).astype(F32)
    atoms = hydrogen.shape[1]
    own = jnp.concatenate(
        [positions_ref[0], positions_ref[1], positions_ref[2], hydrogen]
        + [jnp.zeros((OCTET - 4, atoms), F32)],
        axis=0,
    )
    own_ref[...] = own
    send_ref[...] = lookup(own, jnp.broadcast_to(rows_ref[...], own.shape))


def force_kernel(
    live_ref,
    own_ref,
    halo_ref,
    listed_ref,
    scale_ref,
    shift_ref,
    two_ref,
    bias_two_ref,
    three_ref,
    bias_three_ref,
    first_ref,
    fit_bias_first_ref,
    second_ref,
    fit_bias_second_ref,
    third_ref,
    fit_bias_third_ref,
    readout_ref,
    out_ref,
    own_t,
    padded,
    two_in,
    two_out,
    three_in,
    three_out,
    consts,
    environ,
    offset,
    around,
    kept_one,
    kept_two,
    kept_three,
    kept_sum,
    features,
    features_t,
    descriptor,
    grad_descriptor,
    grad_environ,
    grad_strength,
    grad_terms,
    centre_terms,
    scattered,
):
    live = live_ref[0]
    octets = (live + (OCTET - 1)) // OCTET
    atoms, slots = listed_ref.shape
    e1 = scale_ref.shape[1]
    e2 = two_ref.shape[1]
    e3 = three_ref.shape[1]
    rows_one, rows_two, rows_three = two_in.shape[0], three_in.shape[0], three_out.shape[0]
    copies_two, copies_three = e2 // e1, e3 // e1

    def split_bias(bias):
        high = bias.astype(BF16).astype(F32)
        return high, bias - high

    padded[...] = jnp.zeros_like(padded)
    bias_high, bias_low = split_bias(bias_two_ref[...])
    for k in range(copies_two):
        cols = slice(k * e1, (k + 1) * e1)
        padded[0:e1, k * CHUNK : k * CHUNK + e1] = two_ref[:, cols].astype(F32)
        padded[e1 : e1 + 1, k * CHUNK : k * CHUNK + e1] = bias_high[:, cols]
        padded[e1 + 1 : e1 + 2, k * CHUNK : k * CHUNK + e1] = bias_low[:, cols]
    table = padded[...]
    two_in[...] = table[:rows_one, :rows_two].astype(BF16)
    two_out[...] = table.T[:rows_two, :rows_one].astype(BF16)

    padded[...] = jnp.zeros_like(padded)
    bias_high, bias_low = split_bias(bias_three_ref[...])
    for k in range(copies_three):
        cols = slice(k * e1, (k + 1) * e1)
        for m in range(copies_two):
            padded[m * CHUNK : m * CHUNK + e1, k * CHUNK : k * CHUNK + e1] = three_ref[
                m * e1 : (m + 1) * e1, cols
            ].astype(F32)
        padded[e1 : e1 + 1, k * CHUNK : k * CHUNK + e1] = bias_high[:, cols]
        padded[e1 + 1 : e1 + 2, k * CHUNK : k * CHUNK + e1] = bias_low[:, cols]
    table = padded[...]
    three_in[...] = table[:rows_two, :rows_three].astype(BF16)
    three_out[...] = table.T[:rows_three, :rows_two].astype(BF16)

    padded[...] = jnp.zeros_like(padded)
    padded[0:2, 0:e1] = scale_ref[...]
    padded[2:4, 0:e1] = shift_ref[...]
    padded[2:3, e1 : e1 + 2] = jnp.full((1, 2), ONE_AT, F32)
    padded[3:4, e1 : e1 + 2] = jnp.full((1, 2), ONE_AT, F32)
    table = padded[...].T
    for k in range(4):
        column = table[:CHUNK, k : k + 1]
        if k % 2 == 1:
            column = column - table[:CHUNK, k - 1 : k]
        consts[k] = jnp.broadcast_to(column, (CHUNK, slots))

    padded[...] = jnp.zeros_like(padded)
    padded[0:OCTET, :] = own_ref[...]
    own_t[...] = padded[...].T

    features[...] = jnp.zeros_like(features)
    upper = lax.broadcasted_iota(jnp.int32, (OCTET, LANES), 0) < 4

    def pair_blocks(tile):
        zero = jnp.zeros_like(tile)
        return jnp.concatenate(
            [jnp.where(upper, tile, zero), jnp.where(upper, zero, tile)], axis=1
        ).astype(BF16)

    def gather_octet(first):
        listed = listed_ref[pl.ds(first, OCTET), :]
        low = jnp.bitwise_and(listed, LANES - 1)
        is_own = listed < atoms
        centre = own_t[pl.ds(first, OCTET), :]
        fetched = []
        for c in range(4):
            near = lookup(jnp.broadcast_to(own_ref[c : c + 1, :], (OCTET, LANES)), low)
            far = lookup(jnp.broadcast_to(halo_ref[c : c + 1, :], (OCTET, LANES)), low)
            fetched.append(jnp.where(is_own, near, far))
        deltas = [fetched[c] - centre[:, c : c + 1] for c in range(3)]
        return listed, deltas, fetched[3]

    def geometry(listed, deltas):
        filled = (listed >= 0).astype(F32)
        dist_sq = deltas[0] * deltas[0] + deltas[1] * deltas[1] + deltas[2] * deltas[2]
        inverse = lax.rsqrt(dist_sq + softening)
        switch = jnp.maximum(1.0 - dist_sq * (1.0 / cutoff_sq), 0.0)
        base = filled * switch * inverse
        return inverse, switch, base, base * switch

    def forward(octet, carry):
        first = pl.multiple_of(octet * OCTET, OCTET)
        listed, deltas, hydrogen = gather_octet(first)
        inverse, _, _, strength = geometry(listed, deltas)
        around[pl.ds(first, OCTET), :] = hydrogen
        scaled = strength * inverse
        environ[pl.ds(first * 4, OCTET, stride=4), :] = strength
        for c in range(3):
            offset[c, pl.ds(first, OCTET), :] = deltas[c]
            environ[pl.ds(first * 4 + 1 + c, OCTET, stride=4), :] = scaled * deltas[c]
        for pair in range(OCTET // 2):
            halves = []
            for a in (2 * pair, 2 * pair + 1):
                row, kind = strength[a : a + 1], hydrogen[a : a + 1]
                halves.append(
                    row * consts[0] + consts[2] + kind * (row * consts[1] + consts[3])
                )
            one = jnp.tanh(jnp.concatenate(halves, axis=1))
            two = jnp.tanh(jnp.dot(two_out[...], one.astype(BF16), preferred_element_type=F32))
            sum_two = two + jnp.concatenate([one] * copies_two, axis=0)
            three = jnp.tanh(
                jnp.dot(three_out[...], sum_two.astype(BF16), preferred_element_type=F32)
            )
            sum_three = (three + jnp.concatenate([sum_two] * 2, axis=0)).astype(BF16)
            at = octet * (OCTET // 2) + pair
            kept_one[at] = one
            kept_two[at] = two
            kept_three[at] = three
            kept_sum[at] = sum_three
            rows = pl.ds(pl.multiple_of(first * 4 + OCTET * pair, OCTET), OCTET)
            features[rows, :] = lax.dot_general(
                pair_blocks(environ[rows, :]),
                sum_three,
                (((1,), (1,)), ((), ())),
                preferred_element_type=F32,
            )
        return carry

    lax.fori_loop(0, octets, forward, 0)

    for c in range(4):
        features_t[c] = features[pl.ds(c, atoms, stride=4), :].T * (1.0 / slots)

    def descriptor_rows(r, carry):
        for q in range(copies_three):
            total = None
            for c in range(4):
                term = features_t[c, pl.ds(q * CHUNK + r, 1), :] * features_t[c, 0:M2, :]
                total = term if total is None else total + term
            at = pl.multiple_of((q * e1 + r) * M2, M2)
            descriptor[pl.ds(at, M2), :] = total.astype(BF16)
        return carry

    lax.fori_loop(0, e1, descriptor_rows, 0)

    fit_one = jnp.tanh(
        lax.dot_general(
            descriptor[...], first_ref[...], (((0,), (0,)), ((), ())), preferred_element_type=F32
        )
        + fit_bias_first_ref[...]
    )
    tanh_two = jnp.tanh(
        jnp.dot(fit_one.astype(BF16), second_ref[...], preferred_element_type=F32)
        + fit_bias_second_ref[...]
    )
    fit_two = tanh_two + fit_one
    tanh_three = jnp.tanh(
        jnp.dot(fit_two.astype(BF16), third_ref[...], preferred_element_type=F32)
        + fit_bias_third_ref[...]
    )
    living = (lax.broadcasted_iota(jnp.int32, (atoms, 1), 0) < live).astype(F32)
    readout = readout_ref[0:1, :] + own_t[:, 3:4] * (readout_ref[1:2, :] - readout_ref[0:1, :])
    grad = living * readout
    contract_last = (((1,), (1,)), ((), ()))
    inner = (grad * (1.0 - tanh_three * tanh_three)).astype(BF16)
    grad = grad + lax.dot_general(inner, third_ref[...], contract_last, preferred_element_type=F32)
    inner = (grad * (1.0 - tanh_two * tanh_two)).astype(BF16)
    grad = grad + lax.dot_general(inner, second_ref[...], contract_last, preferred_element_type=F32)
    inner = (grad * (1.0 - fit_one * fit_one)).astype(BF16)
    grad_descriptor[0 : e3 * M2, :] = lax.dot_general(
        first_ref[...], inner, contract_last, preferred_element_type=F32
    )

    def second_factor(r, carry):
        totals = list(carry)
        for q in range(copies_three):
            at = pl.multiple_of((q * e1 + r) * M2, M2)
            rows = grad_descriptor[pl.ds(at, M2), :]
            for c in range(4):
                totals[c] = totals[c] + rows * features_t[c, pl.ds(q * CHUNK + r, 1), :]
        return tuple(totals)

    shared = lax.fori_loop(
        0, e1, second_factor, tuple(jnp.zeros((M2, atoms), F32) for _ in range(4))
    )
    valid = lax.broadcasted_iota(jnp.int32, (CHUNK, atoms), 0) < e1
    by_column = [[] for _ in range(4)]
    for q in range(copies_three):
        totals = [jnp.zeros((CHUNK, atoms), F32) for _ in range(4)]
        for f in range(M2):
            rows = grad_descriptor[pl.ds(q * e1 * M2 + f, CHUNK, stride=M2), :]
            for c in range(4):
                totals[c] = totals[c] + rows * features_t[c, f : f + 1, :]
        for c in range(4):
            part = jnp.where(valid, totals[c], 0.0)
            if q == 0:
                part = part + jnp.concatenate(
                    [shared[c], jnp.zeros((CHUNK - M2, atoms), F32)], axis=0
                )
            by_column[c].append(part)
    for c in range(4):
        features[pl.ds(c, atoms, stride=4), :] = (
            jnp.concatenate(by_column[c], axis=0) * (1.0 / slots)
        ).T

    scattered[...] = jnp.zeros_like(scattered)
    centre_terms[...] = jnp.zeros_like(centre_terms)
    entries = scattered.shape[1]
    lane = lax.broadcasted_iota(jnp.int32, (OCTET, LANES), 1)

    def backward(octet, carry):
        first = pl.multiple_of(octet * OCTET, OCTET)
        grad_rows = features[pl.ds(pl.multiple_of(first * 4, OCTET * 4), OCTET * 4), :]
        grad_cols = grad_rows.T.astype(BF16)
        grad_rows = grad_rows.astype(BF16)
        listed = listed_ref[pl.ds(first, OCTET), :]
        for pair in range(OCTET // 2):
            at = octet * (OCTET // 2) + pair
            rows = pl.ds(pl.multiple_of(first * 4 + OCTET * pair, OCTET), OCTET)
            blocks = pair_blocks(environ[rows, :])
            grad_three = jnp.dot(
                grad_cols[:, OCTET * pair : OCTET * (pair + 1)], blocks, preferred_element_type=F32
            )
            both = jnp.dot(
                grad_rows[OCTET * pair : OCTET * (pair + 1), :],
                kept_sum[at],
                preferred_element_type=F32,
            )
            grad_environ[rows, :] = jnp.where(upper, both[:, :LANES], both[:, LANES:])
            three = kept_three[at]
            inner = (grad_three * (1.0 - three * three)).astype(BF16)
            grad_two = (
                jnp.dot(three_in[...], inner, preferred_element_type=F32)
                + grad_three[:rows_two]
                + grad_three[rows_two:]
            )
            two = kept_two[at]
            inner = (grad_two * (1.0 - two * two)).astype(BF16)
            grad_one = jnp.dot(two_in[...], inner, preferred_element_type=F32)
            for k in range(copies_two):
                grad_one = grad_one + grad_two[k * CHUNK : (k + 1) * CHUNK]
            one = kept_one[at]
            grad_one = grad_one * (1.0 - one * one)
            for half in range(2):
                row = first + 2 * pair + half
                kind = around[pl.ds(row, 1), :]
                weighed = grad_one[:, half * LANES : (half + 1) * LANES] * (
                    consts[0] + kind * consts[1]
                )
                grad_strength[pl.ds(row, 1), :] = jnp.sum(weighed, axis=0, keepdims=True)

        deltas = [offset[c, pl.ds(first, OCTET), :] for c in range(3)]
        inverse, switch, base, strength = geometry(listed, deltas)
        by_environ = [
            grad_environ[pl.ds(first * 4 + c, OCTET, stride=4), :] for c in range(4)
        ]
        along = (
            by_environ[1] * deltas[0] + by_environ[2] * deltas[1] + by_environ[3] * deltas[2]
        )
        by_strength = (
            grad_strength[pl.ds(first, OCTET), :] + by_environ[0] + along * inverse
        )
        filled = (listed >= 0).astype(F32)
        by_inverse = strength * along + filled * switch * switch * by_strength
        by_dist = (-2.0 / cutoff_sq) * base * by_strength - (
            0.5 * inverse * inverse * inverse
        ) * by_inverse
        scaled = strength * inverse
        centre = jnp.zeros((OCTET, LANES), F32)
        for c in range(3):
            term = by_environ[1 + c] * scaled + 2.0 * deltas[c] * by_dist
            grad_terms[pl.ds(first * 4 + c, OCTET, stride=4), :] = term
            centre = jnp.where(lane == c, jnp.sum(term, axis=1, keepdims=True), centre)
        grad_terms[pl.ds(first * 4 + 3, OCTET, stride=4), :] = jnp.zeros((OCTET, LANES), F32)
        centre_terms[pl.ds(first, OCTET), :] = centre
        total = jnp.zeros((OCTET, entries), F32)
        numbers = lax.broadcasted_iota(jnp.int32, (entries, LANES), 0)
        for pair in range(OCTET // 2):
            rows = pl.ds(pl.multiple_of(first * 4 + OCTET * pair, OCTET), OCTET)
            hits = jnp.concatenate(
                [
                    (numbers == listed[a : a + 1, :]).astype(F32).astype(BF16)
                    for a in (2 * pair, 2 * pair + 1)
                ],
                axis=1,
            )
            total = total + lax.dot_general(
                pair_blocks(grad_terms[rows, :]), hits, contract_last, preferred_element_type=F32
            )
        scattered[...] += total
        return carry

    lax.fori_loop(0, octets, backward, 0)
    total = scattered[0:4, :] + scattered[4:8, :]
    centre = centre_terms[...].T[0:4, :]
    out_ref[0:4, 0:atoms] = centre - total[:, 0:atoms]
    out_ref[0:4, atoms:] = -total[:, atoms:]
    out_ref[4:8, :] = jnp.zeros((4, entries), F32)


def kick_kernel(part_ref, back_ref, rows_ref, types_ref, positions_ref, velocities_ref, forces_ref, out_ref):
    atoms = types_ref.shape[1]
    rows = rows_ref[...]
    hits = (
        lax.broadcasted_iota(jnp.int32, (atoms, rows.shape[1]), 0) == rows
    ).astype(F32)
    returned = lax.dot_general(
        back_ref[...],
        hits,
        (((1,), (1,)), ((), ())),
        preferred_element_type=F32,
        precision=lax.Precision.HIGHEST,
    )
    force = part_ref[:, 0:atoms] + returned
    inverse_mass = jnp.where(types_ref[...] == 1, 1.0, 1.0 / heavy_mass)
    rows = []
    for c in range(3):
        forces_ref[c] = force[c : c + 1]
        rows.append(positions_ref[c])
    for c in range(3):
        rows.append(velocities_ref[c] + step_size * inverse_mass * force[c : c + 1])
    tile = jnp.concatenate(rows + [jnp.zeros((2, atoms), F32)], axis=0)
    for b in range(out_ref.shape[0]):
        out_ref[b] = tile


def mix_kernel(bead_ref, table_ref, gathered_ref, positions_ref, velocities_ref):
    mine = bead_ref[0]
    count = gathered_ref.shape[0]
    tile_shape = gathered_ref.shape[1:]
    is_position = lax.broadcasted_iota(jnp.int32, tile_shape, 0) < 3
    turned = jnp.zeros(tile_shape, F32)
    crossed = jnp.zeros(tile_shape, F32)
    for b in range(count):
        tile = gathered_ref[b]
        turned = turned + table_ref[mine, b] * tile
        crossed = crossed + jnp.where(
            is_position, -table_ref[mine, 2 * count + b], table_ref[mine, count + b]
        ) * tile
    for c in range(3):
        positions_ref[c] = turned[c : c + 1] + crossed[3 + c : 4 + c]
        velocities_ref[c] = turned[3 + c : 4 + c] + crossed[c : c + 1]


VMEM_SPEC = pl.BlockSpec(memory_space=pltpu.VMEM)
SMEM_SPEC = pl.BlockSpec(memory_space=pltpu.SMEM)


def shape(*dims, dtype=F32):
    return jax.ShapeDtypeStruct(dims, dtype)


def call_force(live_atoms, own, halo, neighbours, weights):
    atoms, slots = neighbours.shape
    entries = atoms + halo.shape[1]
    e1 = weights[0].shape[1]
    e2 = weights[2].shape[1]
    e3 = weights[4].shape[1]
    rows_two = e2 // e1 * CHUNK
    rows_three = e3 // e1 * CHUNK
    assert slots == LANES and atoms == LANES and entries == 2 * LANES
    assert e3 == 2 * e2 and e2 == 2 * e1 and rows_three <= LANES and M2 <= e1
    pairs = atoms // 2
    return pl.pallas_call(
        force_kernel,
        out_shape=shape(OCTET, entries),
        in_specs=[SMEM_SPEC] + [VMEM_SPEC] * (3 + len(weights)),
        out_specs=VMEM_SPEC,
        scratch_shapes=[
            pltpu.VMEM((atoms, LANES), F32),
            pltpu.VMEM((LANES, LANES), F32),
            pltpu.VMEM((CHUNK, rows_two), BF16),
            pltpu.VMEM((rows_two, CHUNK), BF16),
            pltpu.VMEM((rows_two, rows_three), BF16),
            pltpu.VMEM((rows_three, rows_two), BF16),
            pltpu.VMEM((4, CHUNK, slots), F32),
            pltpu.VMEM((4 * atoms, slots), F32),
            pltpu.VMEM((3, atoms, slots), F32),
            pltpu.VMEM((atoms, slots), F32),
            pltpu.VMEM((pairs, CHUNK, 2 * slots), F32),
            pltpu.VMEM((pairs, rows_two, 2 * slots), F32),
            pltpu.VMEM((pairs, rows_three, 2 * slots), F32),
            pltpu.VMEM((pairs, rows_three, 2 * slots), BF16),
            pltpu.VMEM((4 * atoms, rows_three), F32),
            pltpu.VMEM((4, rows_three, atoms), F32),
            pltpu.VMEM((e3 * M2, atoms), BF16),
            pltpu.VMEM(((e3 + CHUNK) * M2, atoms), F32),
            pltpu.VMEM((4 * atoms, slots), F32),
            pltpu.VMEM((atoms, slots), F32),
            pltpu.VMEM((4 * atoms, slots), F32),
            pltpu.VMEM((atoms, LANES), F32),
            pltpu.VMEM((OCTET, entries), F32),
        ],
        compiler_params=pltpu.CompilerParams(vmem_limit_bytes=VMEM_LIMIT),
        name="force",
    )(live_atoms, own, halo, neighbours, *weights)


def row(array):
    return array.reshape(1, -1)


def local(
    positions,
    velocities,
    atom_types,
    live_atoms,
    halo_rows,
    neighbours,
    type_scale,
    type_shift,
    embed_two,
    embed_bias_two,
    embed_three,
    embed_bias_three,
    fit_first,
    fit_bias_first,
    fit_second,
    fit_bias_second,
    fit_third,
    fit_bias_third,
    fit_readout,
):
    weights = (
        type_scale,
        type_shift,
        embed_two,
        row(embed_bias_two),
        embed_three,
        row(embed_bias_three),
        fit_first,
        row(fit_bias_first),
        fit_second,
        row(fit_bias_second),
        fit_third,
        row(fit_bias_third),
        fit_readout,
    )
    atoms = positions.shape[2]
    half = halo_rows.shape[1] // 2
    beads = lax.axis_size("bead")
    slabs = lax.axis_size("slab")
    to_next = [(i, (i + 1) % slabs) for i in range(slabs)]
    to_last = [((i + 1) % slabs, i) for i in range(slabs)]

    def exchange(outgoing, up, down):
        if slabs == 2:
            return lax.ppermute(outgoing, "slab", to_next)
        return jnp.concatenate(
            [
                lax.ppermute(outgoing[:, up], "slab", to_next),
                lax.ppermute(outgoing[:, down], "slab", to_last),
            ],
            axis=1,
        )

    low, high = slice(0, half), slice(half, 2 * half)
    rows = jnp.concatenate([halo_rows[:, high], halo_rows[:, low]], axis=1)
    types = row(atom_types)
    own, sent = pl.pallas_call(
        outgoing_kernel,
        out_shape=(shape(OCTET, atoms), shape(OCTET, 2 * half)),
        in_specs=[VMEM_SPEC] * 3,
        out_specs=(VMEM_SPEC, VMEM_SPEC),
        name="outgoing",
    )(positions, types, rows)
    halo = exchange(sent, low, high)
    part = call_force(live_atoms, own, halo, neighbours, weights)
    back = exchange(part[:, atoms:], high, low)
    if slabs != 2:
        back = jnp.concatenate([back[:, high], back[:, low]], axis=1)
    forces, kicked = pl.pallas_call(
        kick_kernel,
        out_shape=(shape(*positions.shape), shape(beads, OCTET, atoms)),
        in_specs=[VMEM_SPEC] * 6,
        out_specs=(VMEM_SPEC, VMEM_SPEC),
        name="kick",
    )(part, back, rows, types, positions, velocities)
    gathered = lax.all_to_all(kicked, "bead", split_axis=0, concat_axis=0, tiled=True)
    table = jnp.asarray(bead_tables(beads))
    mine = lax.axis_index("bead").astype(jnp.int32).reshape(1)
    positions_new, velocities_new = pl.pallas_call(
        mix_kernel,
        out_shape=(shape(*positions.shape), shape(*positions.shape)),
        in_specs=[SMEM_SPEC, SMEM_SPEC, VMEM_SPEC],
        out_specs=(VMEM_SPEC, VMEM_SPEC),
        name="mix",
    )(mine, table, gathered)
    return positions_new, velocities_new, forces


def solution(mesh):
    sharded = P(None, "bead", "slab")
    return jax.shard_map(
        local,
        mesh=mesh,
        in_specs=(
            sharded,
            sharded,
            P("slab"),
            P("slab"),
            P("slab", None),
            P("slab", None),
        )
        + (P(),) * 13,
        out_specs=(sharded, sharded, sharded),
        check_vma=False,
    )
```

time: 510 us -> 75.8 us (0.15)
  starting transfers between devices: 236 us -> 8.52 us
  local copies, waits for them, and re-layouts: 112 us -> 4.21 us
  other arithmetic: 72 us -> 0.58 us
  matrix products: 55.8 us -> 0 us
  Pallas kernels: 0 us -> 52 us
  waiting for transfers between devices: 27.5 us -> 8.68 us
    ppermute x4 -> x2, starting transfers between devices: 206 us -> 0.57 us  [exchange(): return lax.ppermute(outgoing, 'slab', to_next)]
    gather x9 -> x0, local copies, waits for them, and re-layouts: 76.2 us -> none  [the longest x2 51.5 us: block_gradient(): around_hydrogen = wide_hydrogen[flat_rows].reshape(BLOCK, -1)]
    dot_general x33 -> x0, matrix products: 54.8 us -> none  [the longest x6 18.7 us: block_energy(): jnp.einsum('bke,cbk->bec', layer_three, environ, precision=highest)]
    scatter-add x4 -> x0, other arithmetic: 52.3 us -> none  [the longest x2 50.1 us: block_gradient(): gradient = gradient.at[:, flat_rows].add(grad_around.reshape(3, -1))]
    pallas_call x0 -> x4, Pallas kernels: none -> 52 us  [the longest x1 47.5 us: call_force(): pl.pallas_call(force_kernel, out_shape=shape(OCTET, entries), in_specs=[S...]
    all_to_all x6 -> x1, starting transfers between devices: 30.2 us -> 7.94 us  [local(): lax.all_to_all(kicked, 'bead', split_axis=0, concat_axis=0, tiled=True)]
    all_to_all x6 -> x1, waiting for transfers between devices: 27.5 us -> 7.53 us  [local(): lax.all_to_all(kicked, 'bead', split_axis=0, concat_axis=0, tiled=True)]
    while x143 -> x0, local copies, waits for them, and re-layouts: 9.45 us -> none
  transfers between devices with their start and end apart: 10 -> 3, of which waited for: 5 -> 2; matrix products, arithmetic and copies ran while one was open for 46% -> 2% of each run, Pallas kernels for 0% -> 0%
where the time goes in v1:
time: 75.8 us; the launch traced here: 75.5 us
  Pallas kernels  52 us (69%)
  waiting for transfers between devices  8.68 us (11%)
  starting transfers between devices  8.52 us (11%)
  local copies, waits for them, and re-layouts  4.21 us (6%)
  between operations  1.49 us (2%)
    pallas_call x1, Pallas kernels, call_force(): pl.pallas_call(force_kernel, out_shape=shape(OCTET, entries), in_specs=[S...  47.5 us
    all_to_all x1, starting transfers between devices, local(): lax.all_to_all(kicked, 'bead', split_axis=0, concat_axis=0, tiled=True)  7.94 us
    all_to_all x1, waiting for transfers between devices, local(): lax.all_to_all(kicked, 'bead', split_axis=0, concat_axis=0, tiled=True)  7.53 us
    unnamed x35, local copies, waits for them, and re-layouts  3.4 us
    pallas_call x1, Pallas kernels, local(): pl.pallas_call(kick_kernel, out_shape=(shape(*positions.shape), shape(bea...  1.61 us
  transfers between devices with their start and end apart: 3, of which 2 were waited for; matrix products, arithmetic and copies ran while one was open for 2% of the time, Pallas kernels for 0%

profile of v1, /device:TPU:0, one launch (start us, length us, event | category | flops | bytes accessed | tf_op | source)
XLA Modules:
  0.0 75.5 jit_solution(13164455104555859146)
XLA Ops:
  0.6 0.8 %fusion = (s32[1,64]{1,0:T(1,128)S(1)}, s32[1,64]{1,0:T(1,128)S(1)}) fusion(s32[1,128]{1,0:T(1,128)} %param.24), kind=kLoop, calls=%fused_computation.1 | loop fusion | bytes 1024 | tf_op jit(solution)/shard_map/slice | solution.py:568
  1.4 0.6 pad_add_fusion.rows_ref
  2.0 1.4 %outgoing.1 = (f32[8,128]{1,0:T(8,128)}, f32[8,128]{1,0:T(8,128)}) custom-call(f32[3,1,128]{2,1,0:T(1,128)} %positions_ref.3, s32[1,128]{1,0:T(1,128)} %bitcast.12, s32[1,128]{1,0:T(1,128)} %pad_add_fusion.rows_ref), custom_call_target="tpu_custom_call" | custom-call | tf_op jit(solution)/shard_map/outgoing/pallas_call | solution.py:570
  3.4 0.5 collective-permute-start
  3.9 0.0 copy-start.11
  3.9 0.0 copy-start.12
  3.9 0.0 copy-start.13
  3.9 0.0 copy-start.14
  4.0 1.6 %copy.23.first_ref = bf16[1600,240]{1,0:T(8,128)(2,1)S(1)} copy(bf16[1600,240]{0,1:T(8,128)(2,1)} %param.32) | data formatting | bytes 1536000 | tf_op args[12]
  5.5 0.0 copy-start.5
  6.2 0.0 collective-permute-done.halo_ref
  6.2 0.0 copy-start.6
  6.2 0.0 copy-start.8
  6.2 0.0 copy-done
  6.2 0.0 copy-done.1
  6.3 0.0 copy-done.2
  6.3 0.0 copy-done.4
  6.3 0.0 copy-done.7
  6.3 0.0 copy-done.9
  6.3 0.0 copy-done.10
  6.3 0.0 copy-done.11
  6.4 0.5 copy-done.6
  6.9 0.0 copy-done.8
  6.9 47.5 %force.1.part_ref = f32[8,256]{1,0:T(8,128)S(1)} custom-call(s32[1]{0:T(128)S(6)} %copy.24.live_ref, f32[8,128]{1,0:T(8,128)S(1)} %copy-done.6, f32[8,128]{1,0:T(8,128)S(1)} %collective-permute-done.halo_ref, s32[128,128]{1,0:T(8,128)S(1)} %copy-done.2, f32[2,25]{1,0:T(2,128)S(1)} %copy-done.8, f32[2,25]{1,0:T(2,128)S(1)} %copy-done.9, ...), custom_call_target="tpu_custom_call" | custom-call | tf_op jit(solution)/shard_map/force/pallas_call | solution.py:474
  54.5 0.1 collective-permute-start.1
  54.5 1.2 %collective-permute-done.1.back_ref = f32[8,128]{1,0:T(8,128)S(1)} collective-permute-done((f32[8,128]{1,0:T(8,128)S(1)}, f32[8,128]{1,0:T(8,128)S(1)}, u32[]{:S(2)}, u32[]{:S(2)}) %collective-permute-start.1) | collective-permute-done | bytes 4128 | tf_op jit(solution)/shard_map/ppermute | solution.py:558
  55.7 0.6 copy-done.16
  56.3 1.6 %kick.1 = (f32[3,1,128]{2,1,0:T(1,128)}, f32[16,8,128]{2,1,0:T(8,128)}) custom-call(f32[8,256]{1,0:T(8,128)} %copy-done.3, f32[8,128]{1,0:T(8,128)} %copy-done.16, s32[1,128]{1,0:T(1,128)} %pad_add_fusion.rows_ref, s32[1,128]{1,0:T(1,128)} %bitcast.13, f32[3,1,128]{2,1,0:T(1,128)} %positions_ref.3, f32[3,1,128]{2,1,0:T(1,128)} %velocities_ref.1), custom_call_target="tpu_custom_call" | custom-call | tf_op jit(solution)/shard_map/kick/pallas_call | solution.py:582
  57.9 7.9 %all-to-all-start = ((f32[16,8,128]{2,1,0:T(8,128)}), f32[16,8,128]{2,1,0:T(8,128)S(1)}, u32[]{:S(2)}, u32[]{:S(2)}) async-start(f32[16,8,128]{2,1,0:T(8,128)} %get-tuple-element.11), calls=%async_computation | async-start | bytes 131072 | tf_op jit(solution)/shard_map/all_to_all | solution.py:589
  65.8 7.5 %all-to-all-done.gathered_ref = f32[16,8,128]{2,1,0:T(8,128)S(1)} async-done(((f32[16,8,128]{2,1,0:T(8,128)}), f32[16,8,128]{2,1,0:T(8,128)S(1)}, u32[]{:S(2)}, u32[]{:S(2)}) %all-to-all-start) | async-done | bytes 65568 | tf_op jit(solution)/shard_map/all_to_all | solution.py:589
  73.4 0.6 copy-done.15
  74.0 1.5 %mix.1 = (f32[3,1,128]{2,1,0:T(1,128)}, f32[3,1,128]{2,1,0:T(1,128)}) custom-call(s32[1]{0:T(128)} %bitcast.bead_ref, f32[16,48]{1,0:T(8,128)} %constant.8.clone.table_ref, f32[16,8,128]{2,1,0:T(8,128)} %copy-done.15), custom_call_target="tpu_custom_call" | custom-call | tf_op jit(solution)/shard_map/mix/pallas_call | solution.py:592
  (16 shorter events, 0.0 us)
Async XLA Ops:
  3.4 2.9 %copy-start = (bf16[240,240]{1,0:T(8,128)(2,1)S(1)}, bf16[240,240]{1,0:T(8,128)(2,1)}, u32[]{:S(2)}) copy-start(bf16[240,240]{1,0:T(8,128)(2,1)} %second_ref.1) | copy-start | bytes 345604
  3.4 2.9 %copy-start.1 = (bf16[240,240]{1,0:T(8,128)(2,1)S(1)}, bf16[240,240]{1,0:T(8,128)(2,1)}, u32[]{:S(2)}) copy-start(bf16[240,240]{1,0:T(8,128)(2,1)} %third_ref.1) | copy-start | bytes 345604
  3.4 2.9 %copy-start.2 = (s32[128,128]{1,0:T(8,128)S(1)}, s32[128,128]{1,0:T(8,128)}, u32[]{:S(2)}) copy-start(s32[128,128]{1,0:T(8,128)} %listed_ref.1) | copy-start | bytes 196612
  3.4 2.8 %collective-permute-start = (f32[8,128]{1,0:T(8,128)}, f32[8,128]{1,0:T(8,128)S(1)}, u32[]{:S(2)}, u32[]{:S(2)}) collective-permute-start(f32[8,128]{1,0:T(8,128)} %get-tuple-element.10), channel_id=1, source_target_pairs={{0,1},{1,0},{2,3},{3,2},{4,5},{5,4},{6,7},{7,6},{8,9},{9,8},{10,11... | collective-permute-start | bytes 12296 | tf_op jit(solution)/shard_map/ppermute | solution.py:558
  3.9 2.4 %copy-start.4 = (bf16[50,100]{1,0:T(8,128)(2,1)S(1)}, bf16[50,100]{1,0:T(8,128)(2,1)}, u32[]{:S(2)}) copy-start(bf16[50,100]{1,0:T(8,128)(2,1)} %three_ref.1) | copy-start | bytes 30004
  3.9 2.4 %copy-start.7 = (f32[2,240]{1,0:T(2,128)S(1)}, f32[2,240]{1,0:T(2,128)}, u32[]{:S(2)}) copy-start(f32[2,240]{1,0:T(2,128)} %readout_ref.1) | copy-start | bytes 5764
  3.9 2.4 %copy-start.9 = (f32[2,25]{1,0:T(2,128)S(1)}, f32[2,25]{1,0:T(2,128)}, u32[]{:S(2)}) copy-start(f32[2,25]{1,0:T(2,128)} %shift_ref.1) | copy-start | bytes 604
  3.9 2.4 %copy-start.10 = (f32[240]{0:T(256)S(1)}, f32[240]{0:T(256)}, u32[]{:S(2)}) copy-start(f32[240]{0:T(256)} %param.33) | copy-start | bytes 2884
  3.9 2.4 %copy-start.11 = (f32[240]{0:T(256)S(1)}, f32[240]{0:T(256)}, u32[]{:S(2)}) copy-start(f32[240]{0:T(256)} %param.35) | copy-start | bytes 2884
  3.9 2.4 %copy-start.12 = (f32[240]{0:T(256)S(1)}, f32[240]{0:T(256)}, u32[]{:S(2)}) copy-start(f32[240]{0:T(256)} %param.37) | copy-start | bytes 2884
  3.9 2.4 %copy-start.13 = (f32[50]{0:T(128)S(1)}, f32[50]{0:T(128)}, u32[]{:S(2)}) copy-start(f32[50]{0:T(128)} %param.29) | copy-start | bytes 604
  3.9 2.4 %copy-start.14 = (f32[100]{0:T(128)S(1)}, f32[100]{0:T(128)}, u32[]{:S(2)}) copy-start(f32[100]{0:T(128)} %param.31) | copy-start | bytes 1204
  5.5 0.8 %copy-start.5 = (bf16[25,50]{1,0:T(8,128)(2,1)S(1)}, bf16[25,50]{1,0:T(8,128)(2,1)}, u32[]{:S(2)}) copy-start(bf16[25,50]{1,0:T(8,128)(2,1)} %two_ref.1) | copy-start | bytes 7504
  6.2 0.7 copy-start.6
  6.2 0.7 copy-start.8
  54.5 1.2 %copy-start.3 = (f32[8,256]{1,0:T(8,128)}, f32[8,256]{1,0:T(8,128)S(1)}, u32[]{:S(2)}) copy-start(f32[8,256]{1,0:T(8,128)S(1)} %force.1.part_ref) | copy-start | bytes 24580
  54.5 1.2 %collective-permute-start.1 = (f32[8,128]{1,0:T(8,128)S(1)}, f32[8,128]{1,0:T(8,128)S(1)}, u32[]{:S(2)}, u32[]{:S(2)}) collective-permute-start(f32[8,128]{1,0:T(8,128)S(1)} %slice.12), channel_id=1, source_target_pairs={{0,1},{1,0},{2,3},{3,2},{4,5},{5,4},{6,7},{7,6},{8,9},{9,8},{10,11... | collective-permute-start | bytes 12296 | tf_op jit(solution)/shard_map/ppermute | solution.py:558
  55.7 0.6 copy-start.16
  57.9 15.5 %all-to-all-start = ((f32[16,8,128]{2,1,0:T(8,128)}), f32[16,8,128]{2,1,0:T(8,128)S(1)}, u32[]{:S(2)}, u32[]{:S(2)}) async-start(f32[16,8,128]{2,1,0:T(8,128)} %get-tuple-element.11), calls=%async_computation | async-start | bytes 131072 | tf_op jit(solution)/shard_map/all_to_all | solution.py:589
  73.4 0.6 copy-start.15

commit v2 on v1

--- a/solution.py
+++ b/solution.py
@@ -20,9 +20,13 @@
 BF16 = jnp.bfloat16
 LANES = 128
 OCTET = 8
+UNROLL = 8
+DIGIT = 16
+GROUP = 8
 CHUNK = 32
 ONE_AT = 20.0
-VMEM_LIMIT = 48 * 1024 * 1024
+VMEM_LIMIT = 40 * 1024 * 1024
+SMALL_LIMIT = 4 * 1024 * 1024
 
 
 def bead_tables(count):
@@ -59,6 +63,12 @@
     return jnp.take_along_axis(table, indices, axis=1, mode="promise_in_bounds")
 
 
+def turned_rows(rows_ref):
+    rows = rows_ref[...]
+    half = rows.shape[1] // 2
+    return jnp.concatenate([rows[:, half:], rows[:, :half]], axis=1)
+
+
 def outgoing_kernel(positions_ref, types_ref, rows_ref, own_ref, send_ref):
     hydrogen = (types_ref[...] == 1).astype(F32)
     atoms = hydrogen.shape[1]
@@ -68,7 +78,7 @@
         axis=0,
     )
     own_ref[...] = own
-    send_ref[...] = lookup(own, jnp.broadcast_to(rows_ref[...], own.shape))
+    send_ref[...] = lookup(own, jnp.broadcast_to(turned_rows(rows_ref), own.shape))
 
 
 def force_kernel(
@@ -89,7 +99,9 @@
     third_ref,
     fit_bias_third_ref,
     readout_ref,
+    velocities_ref,
     out_ref,
+    parcels_ref,
     own_t,
     padded,
     two_in,
@@ -108,9 +120,10 @@
     features_t,
     descriptor,
     grad_descriptor,
+    first_rows,
+    products,
     grad_environ,
     grad_strength,
-    grad_terms,
     centre_terms,
     scattered,
 ):
@@ -122,6 +135,8 @@
     e3 = three_ref.shape[1]
     rows_one, rows_two, rows_three = two_in.shape[0], three_in.shape[0], three_out.shape[0]
     copies_two, copies_three = e2 // e1, e3 // e1
+
+    first_rows[...] = first_ref[...].T
 
     def split_bias(bias):
         high = bias.astype(BF16).astype(F32)
@@ -169,14 +184,6 @@
     own_t[...] = padded[...].T
 
     features[...] = jnp.zeros_like(features)
-    upper = lax.broadcasted_iota(jnp.int32, (OCTET, LANES), 0) < 4
-
-    def pair_blocks(tile):
-        zero = jnp.zeros_like(tile)
-        return jnp.concatenate(
-            [jnp.where(upper, tile, zero), jnp.where(upper, zero, tile)], axis=1
-        ).astype(BF16)
-
     def gather_octet(first):
         listed = listed_ref[pl.ds(first, OCTET), :]
         low = jnp.bitwise_and(listed, LANES - 1)
@@ -198,7 +205,15 @@
         base = filled * switch * inverse
         return inverse, switch, base, base * switch
 
-    def forward(octet, carry):
+    def run_octets(step, carry=0):
+        def body(turn, carry):
+            for u in range(UNROLL):
+                carry = step(turn * UNROLL + u, carry)
+            return carry
+
+        return lax.fori_loop(0, (octets + UNROLL - 1) // UNROLL, body, carry)
+
+    def surround(octet, carry):
         first = pl.multiple_of(octet * OCTET, OCTET)
         listed, deltas, hydrogen = gather_octet(first)
         inverse, _, _, strength = geometry(listed, deltas)
@@ -208,55 +223,68 @@
         for c in range(3):
             offset[c, pl.ds(first, OCTET), :] = deltas[c]
             environ[pl.ds(first * 4 + 1 + c, OCTET, stride=4), :] = scaled * deltas[c]
-        for pair in range(OCTET // 2):
-            halves = []
-            for a in (2 * pair, 2 * pair + 1):
-                row, kind = strength[a : a + 1], hydrogen[a : a + 1]
-                halves.append(
-                    row * consts[0] + consts[2] + kind * (row * consts[1] + consts[3])
+        return carry
+
+    run_octets(surround)
+
+    def forward(octet, carry):
+        first = pl.multiple_of(octet * OCTET, OCTET)
+        hydrogen = around[pl.ds(first, OCTET), :]
+        rows = pl.ds(pl.multiple_of(first * 4, OCTET * 4), OCTET * 4)
+        groups = range(OCTET // GROUP)
+        ones, twos, threes = [], [], []
+        for g in groups:
+            inputs = []
+            for a in range(g * GROUP, (g + 1) * GROUP):
+                line, kind = environ[pl.ds(first * 4 + 4 * a, 1), :], hydrogen[a : a + 1]
+                inputs.append(
+                    line * consts[0] + consts[2] + kind * (line * consts[1] + consts[3])
                 )
-            one = jnp.tanh(jnp.concatenate(halves, axis=1))
-            two = jnp.tanh(jnp.dot(two_out[...], one.astype(BF16), preferred_element_type=F32))
-            sum_two = two + jnp.concatenate([one] * copies_two, axis=0)
+            ones.append(jnp.tanh(jnp.concatenate(inputs, axis=1).astype(BF16)))
+        for g in groups:
+            kept_one[octet * len(groups) + g] = ones[g]
+            two = jnp.tanh(
+                jnp.dot(two_out[...], ones[g], preferred_element_type=F32).astype(BF16)
+            )
+            kept_two[octet * len(groups) + g] = two
+            twos.append(two + jnp.concatenate([ones[g]] * copies_two, axis=0))
+        by_slot = environ[rows, :].T.astype(BF16)
+        column = lax.broadcasted_iota(jnp.int32, by_slot.shape, 1) // 4
+        total = jnp.zeros((rows_three, OCTET * 4), F32)
+        for g in groups:
             three = jnp.tanh(
-                jnp.dot(three_out[...], sum_two.astype(BF16), preferred_element_type=F32)
+                jnp.dot(three_out[...], twos[g], preferred_element_type=F32).astype(BF16)
             )
-            sum_three = (three + jnp.concatenate([sum_two] * 2, axis=0)).astype(BF16)
-            at = octet * (OCTET // 2) + pair
-            kept_one[at] = one
-            kept_two[at] = two
-            kept_three[at] = three
-            kept_sum[at] = sum_three
-            rows = pl.ds(pl.multiple_of(first * 4 + OCTET * pair, OCTET), OCTET)
-            features[rows, :] = lax.dot_general(
-                pair_blocks(environ[rows, :]),
-                sum_three,
-                (((1,), (1,)), ((), ())),
-                preferred_element_type=F32,
+            kept_three[octet * len(groups) + g] = three
+            sum_three = three + jnp.concatenate([twos[g]] * 2, axis=0)
+            kept_sum[octet * len(groups) + g] = sum_three
+            blocks = jnp.concatenate(
+                [
+                    jnp.where(column == a, by_slot, jnp.zeros_like(by_slot))
+                    for a in range(g * GROUP, (g + 1) * GROUP)
+                ],
+                axis=0,
             )
+            total = total + jnp.dot(sum_three, blocks, preferred_element_type=F32)
+        features[rows, :] = total.T
         return carry
 
-    lax.fori_loop(0, octets, forward, 0)
+    run_octets(forward)
 
     for c in range(4):
         features_t[c] = features[pl.ds(c, atoms, stride=4), :].T * (1.0 / slots)
 
-    def descriptor_rows(r, carry):
-        for q in range(copies_three):
-            total = None
-            for c in range(4):
-                term = features_t[c, pl.ds(q * CHUNK + r, 1), :] * features_t[c, 0:M2, :]
-                total = term if total is None else total + term
-            at = pl.multiple_of((q * e1 + r) * M2, M2)
-            descriptor[pl.ds(at, M2), :] = total.astype(BF16)
-        return carry
-
-    lax.fori_loop(0, e1, descriptor_rows, 0)
+    unit_rows = [q * CHUNK + r for q in range(copies_three) for r in range(e1)]
+    leading = [features_t[c, 0:M2, :] for c in range(4)]
+    for e, at in enumerate(unit_rows):
+        total = None
+        for c in range(4):
+            term = features_t[c, at : at + 1, :] * leading[c]
+            total = term if total is None else total + term
+        descriptor[e * M2 : (e + 1) * M2, :] = total.astype(BF16)
 
     fit_one = jnp.tanh(
-        lax.dot_general(
-            descriptor[...], first_ref[...], (((0,), (0,)), ((), ())), preferred_element_type=F32
-        )
+        jnp.dot(first_ref[...], descriptor[...], preferred_element_type=F32).T
         + fit_bias_first_ref[...]
     )
     tanh_two = jnp.tanh(
@@ -277,45 +305,30 @@
     inner = (grad * (1.0 - tanh_two * tanh_two)).astype(BF16)
     grad = grad + lax.dot_general(inner, second_ref[...], contract_last, preferred_element_type=F32)
     inner = (grad * (1.0 - fit_one * fit_one)).astype(BF16)
-    grad_descriptor[0 : e3 * M2, :] = lax.dot_general(
-        first_ref[...], inner, contract_last, preferred_element_type=F32
-    )
-
-    def second_factor(r, carry):
-        totals = list(carry)
-        for q in range(copies_three):
-            at = pl.multiple_of((q * e1 + r) * M2, M2)
-            rows = grad_descriptor[pl.ds(at, M2), :]
-            for c in range(4):
-                totals[c] = totals[c] + rows * features_t[c, pl.ds(q * CHUNK + r, 1), :]
-        return tuple(totals)
-
-    shared = lax.fori_loop(
-        0, e1, second_factor, tuple(jnp.zeros((M2, atoms), F32) for _ in range(4))
-    )
-    valid = lax.broadcasted_iota(jnp.int32, (CHUNK, atoms), 0) < e1
-    by_column = [[] for _ in range(4)]
-    for q in range(copies_three):
-        totals = [jnp.zeros((CHUNK, atoms), F32) for _ in range(4)]
-        for f in range(M2):
-            rows = grad_descriptor[pl.ds(q * e1 * M2 + f, CHUNK, stride=M2), :]
-            for c in range(4):
-                totals[c] = totals[c] + rows * features_t[c, f : f + 1, :]
+    grad_descriptor[...] = lax.dot_general(
+        first_rows[...], inner, contract_last, preferred_element_type=F32
+    )
+
+    shared = [jnp.zeros((M2, atoms), F32) for _ in range(4)]
+    short = [tile.astype(BF16) for tile in leading]
+    for e, at in enumerate(unit_rows):
+        rows = grad_descriptor[e * M2 : (e + 1) * M2, :]
+        packed = rows.astype(BF16)
         for c in range(4):
-            part = jnp.where(valid, totals[c], 0.0)
-            if q == 0:
-                part = part + jnp.concatenate(
-                    [shared[c], jnp.zeros((CHUNK - M2, atoms), F32)], axis=0
-                )
-            by_column[c].append(part)
+            shared[c] = shared[c] + rows * features_t[c, at : at + 1, :]
+            products[e * M2 : (e + 1) * M2, c * atoms : (c + 1) * atoms] = packed * short[c]
+    unit = lax.broadcasted_iota(jnp.int32, (rows_three, e3 * M2), 0)
+    unit = jnp.where(unit % CHUNK < e1, unit // CHUNK * e1 + unit % CHUNK, -1)
+    gather = (lax.broadcasted_iota(jnp.int32, (rows_three, e3 * M2), 1) // M2 == unit).astype(F32)
+    sums = jnp.dot(gather.astype(BF16), products[...], preferred_element_type=F32)
     for c in range(4):
-        features[pl.ds(c, atoms, stride=4), :] = (
-            jnp.concatenate(by_column[c], axis=0) * (1.0 / slots)
-        ).T
+        total = sums[:, c * atoms : (c + 1) * atoms] + jnp.concatenate(
+            [shared[c], jnp.zeros((rows_three - M2, atoms), F32)], axis=0
+        )
+        features[pl.ds(c, atoms, stride=4), :] = (total * (1.0 / slots)).T
 
     scattered[...] = jnp.zeros_like(scattered)
     centre_terms[...] = jnp.zeros_like(centre_terms)
-    entries = scattered.shape[1]
     lane = lax.broadcasted_iota(jnp.int32, (OCTET, LANES), 1)
 
     def backward(octet, carry):
@@ -323,42 +336,68 @@
         grad_rows = features[pl.ds(pl.multiple_of(first * 4, OCTET * 4), OCTET * 4), :]
         grad_cols = grad_rows.T.astype(BF16)
         grad_rows = grad_rows.astype(BF16)
-        listed = listed_ref[pl.ds(first, OCTET), :]
-        for pair in range(OCTET // 2):
-            at = octet * (OCTET // 2) + pair
-            rows = pl.ds(pl.multiple_of(first * 4 + OCTET * pair, OCTET), OCTET)
-            blocks = pair_blocks(environ[rows, :])
-            grad_three = jnp.dot(
-                grad_cols[:, OCTET * pair : OCTET * (pair + 1)], blocks, preferred_element_type=F32
+        groups = range(OCTET // GROUP)
+        rows = pl.ds(pl.multiple_of(first * 4, OCTET * 4), OCTET * 4)
+        quads = environ[rows, :]
+        owner = lax.broadcasted_iota(jnp.int32, quads.shape, 0) // 4
+        by_quad = jnp.zeros_like(quads)
+        inners, grad_threes, grad_twos = [], [], []
+        for g in groups:
+            at = octet * len(groups) + g
+            blocks = jnp.concatenate(
+                [
+                    jnp.where(owner == a, quads, 0.0).astype(BF16)
+                    for a in range(g * GROUP, (g + 1) * GROUP)
+                ],
+                axis=1,
             )
-            both = jnp.dot(
-                grad_rows[OCTET * pair : OCTET * (pair + 1), :],
-                kept_sum[at],
-                preferred_element_type=F32,
-            )
-            grad_environ[rows, :] = jnp.where(upper, both[:, :LANES], both[:, LANES:])
+            grad_three = jnp.dot(grad_cols, blocks, preferred_element_type=F32).astype(BF16)
             three = kept_three[at]
-            inner = (grad_three * (1.0 - three * three)).astype(BF16)
+            inners.append(grad_three * (1.0 - three * three))
+            grad_threes.append(grad_three[:rows_two] + grad_three[rows_two:])
+        for g in groups:
+            at = octet * len(groups) + g
             grad_two = (
-                jnp.dot(three_in[...], inner, preferred_element_type=F32)
-                + grad_three[:rows_two]
-                + grad_three[rows_two:]
+                jnp.dot(three_in[...], inners[g], preferred_element_type=F32).astype(BF16)
+                + grad_threes[g]
             )
             two = kept_two[at]
-            inner = (grad_two * (1.0 - two * two)).astype(BF16)
-            grad_one = jnp.dot(two_in[...], inner, preferred_element_type=F32)
-            for k in range(copies_two):
-                grad_one = grad_one + grad_two[k * CHUNK : (k + 1) * CHUNK]
-            one = kept_one[at]
+            inners[g] = grad_two * (1.0 - two * two)
+            folded = grad_two[:CHUNK]
+            for k in range(1, copies_two):
+                folded = folded + grad_two[k * CHUNK : (k + 1) * CHUNK]
+            grad_twos.append(folded)
+            both = jnp.dot(grad_rows, kept_sum[at], preferred_element_type=F32)
+            for k in range(GROUP):
+                by_quad = jnp.where(
+                    owner == g * GROUP + k, both[:, k * LANES : (k + 1) * LANES], by_quad
+                )
+        grad_environ[rows, :] = by_quad
+        for g in groups:
+            at = octet * len(groups) + g
+            grad_one = jnp.dot(two_in[...], inners[g], preferred_element_type=F32) + grad_twos[g]
+            one = kept_one[at].astype(F32)
             grad_one = grad_one * (1.0 - one * one)
-            for half in range(2):
-                row = first + 2 * pair + half
-                kind = around[pl.ds(row, 1), :]
-                weighed = grad_one[:, half * LANES : (half + 1) * LANES] * (
+            for k in range(GROUP):
+                line = first + g * GROUP + k
+                kind = around[pl.ds(line, 1), :]
+                weighed = grad_one[:, k * LANES : (k + 1) * LANES] * (
                     consts[0] + kind * consts[1]
                 )
-                grad_strength[pl.ds(row, 1), :] = jnp.sum(weighed, axis=0, keepdims=True)
-
+                grad_strength[pl.ds(line, 1), :] = jnp.sum(weighed, axis=0, keepdims=True)
+
+        return carry
+
+    run_octets(backward)
+
+    numbers = lax.broadcasted_iota(jnp.int32, (DIGIT, LANES), 0).astype(F32).astype(BF16)
+
+    def tall(line):
+        return jnp.broadcast_to(line, (DIGIT, LANES)).astype(BF16)
+
+    def disperse(octet, total):
+        first = pl.multiple_of(octet * OCTET, OCTET)
+        listed = listed_ref[pl.ds(first, OCTET), :]
         deltas = [offset[c, pl.ds(first, OCTET), :] for c in range(3)]
         inverse, switch, base, strength = geometry(listed, deltas)
         by_environ = [
@@ -377,40 +416,58 @@
         ) * by_inverse
         scaled = strength * inverse
         centre = jnp.zeros((OCTET, LANES), F32)
+        terms = []
         for c in range(3):
             term = by_environ[1 + c] * scaled + 2.0 * deltas[c] * by_dist
-            grad_terms[pl.ds(first * 4 + c, OCTET, stride=4), :] = term
+            terms.append(term)
             centre = jnp.where(lane == c, jnp.sum(term, axis=1, keepdims=True), centre)
-        grad_terms[pl.ds(first * 4 + 3, OCTET, stride=4), :] = jnp.zeros((OCTET, LANES), F32)
         centre_terms[pl.ds(first, OCTET), :] = centre
-        total = jnp.zeros((OCTET, entries), F32)
-        numbers = lax.broadcasted_iota(jnp.int32, (entries, LANES), 0)
-        for pair in range(OCTET // 2):
-            rows = pl.ds(pl.multiple_of(first * 4 + OCTET * pair, OCTET), OCTET)
-            hits = jnp.concatenate(
-                [
-                    (numbers == listed[a : a + 1, :]).astype(F32).astype(BF16)
-                    for a in (2 * pair, 2 * pair + 1)
-                ],
-                axis=1,
+        upper_digit = (listed // DIGIT).astype(F32)
+        lower_digit = jnp.bitwise_and(listed, DIGIT - 1).astype(F32)
+        spread, hits = [], []
+        for a in range(OCTET):
+            here = numbers == tall(upper_digit[a : a + 1])
+            zero = jnp.zeros((DIGIT, LANES), BF16)
+            spread.append(
+                jnp.concatenate([jnp.where(here, tall(t[a : a + 1]), zero) for t in terms], axis=0)
             )
-            total = total + lax.dot_general(
-                pair_blocks(grad_terms[rows, :]), hits, contract_last, preferred_element_type=F32
+            hits.append(
+                jnp.where(numbers == tall(lower_digit[a : a + 1]), jnp.ones_like(zero), zero)
             )
-        scattered[...] += total
-        return carry
-
-    lax.fori_loop(0, octets, backward, 0)
-    total = scattered[0:4, :] + scattered[4:8, :]
-    centre = centre_terms[...].T[0:4, :]
-    out_ref[0:4, 0:atoms] = centre - total[:, 0:atoms]
-    out_ref[0:4, atoms:] = -total[:, atoms:]
-    out_ref[4:8, :] = jnp.zeros((4, entries), F32)
+        return total + lax.dot_general(
+            jnp.concatenate(spread, axis=1),
+            jnp.concatenate(hits, axis=1),
+            contract_last,
+            preferred_element_type=F32,
+        )
+
+    total = run_octets(disperse, jnp.zeros((3 * DIGIT, DIGIT), F32))
+    for c in range(3):
+        for d in range(DIGIT):
+            scattered[c : c + 1, d * DIGIT : (d + 1) * DIGIT] = total[
+                c * DIGIT + d : c * DIGIT + d + 1, :
+            ]
+    total = scattered[0:OCTET, :]
+    force = centre_terms[...].T[0:OCTET, :] - total[:, 0:atoms]
+    beyond = -total[:, atoms:]
+    out_ref[:, 0:atoms] = force
+    out_ref[:, atoms:] = beyond
+    if parcels_ref.shape[0] > 1:
+        mine = live_ref[1]
+        kick = step_size * jnp.where(own_ref[3:4, :] == 1.0, 1.0, 1.0 / heavy_mass)
+        moving = [own_ref[c : c + 1, :] for c in range(3)] + [
+            velocities_ref[c] + kick * force[c : c + 1] for c in range(3)
+        ]
+        moving = jnp.concatenate(moving + [jnp.zeros((OCTET - 6, atoms), F32)], axis=0)
+        for s in range(2):
+            tile = jnp.where(mine == s, moving, beyond)
+            for b in range(parcels_ref.shape[0] // 2):
+                parcels_ref[2 * b + s] = tile
 
 
 def kick_kernel(part_ref, back_ref, rows_ref, types_ref, positions_ref, velocities_ref, forces_ref, out_ref):
     atoms = types_ref.shape[1]
-    rows = rows_ref[...]
+    rows = turned_rows(rows_ref)
     hits = (
         lax.broadcasted_iota(jnp.int32, (atoms, rows.shape[1]), 0) == rows
     ).astype(F32)
@@ -434,8 +491,8 @@
         out_ref[b] = tile
 
 
-def mix_kernel(bead_ref, table_ref, gathered_ref, positions_ref, velocities_ref):
-    mine = bead_ref[0]
+def mix_kernel(place_ref, table_ref, gathered_ref, positions_ref, velocities_ref):
+    mine = place_ref[0]
     count = gathered_ref.shape[0]
     tile_shape = gathered_ref.shape[1:]
     is_position = lax.broadcasted_iota(jnp.int32, tile_shape, 0) < 3
@@ -452,15 +509,58 @@
         velocities_ref[c] = turned[3 + c : 4 + c] + crossed[c : c + 1]
 
 
+def settle_kernel(
+    place_ref, table_ref, part_ref, gathered_ref, rows_ref, types_ref, positions_ref, velocities_ref, forces_ref
+):
+    mine, slab = place_ref[0], place_ref[1]
+    count = gathered_ref.shape[0] // 2
+    tile_shape = gathered_ref.shape[1:]
+    is_position = lax.broadcasted_iota(jnp.int32, tile_shape, 0) < 3
+    zero = jnp.zeros(tile_shape, F32)
+    turned, crossed, halo_turned, halo_travel = zero, zero, zero, zero
+    for b in range(count):
+        tile = gathered_ref[2 * b + slab]
+        beyond = gathered_ref[2 * b + 1 - slab]
+        cosine, travel = table_ref[mine, b], table_ref[mine, count + b]
+        spring = table_ref[mine, 2 * count + b]
+        turned = turned + cosine * tile
+        crossed = crossed + jnp.where(is_position, -spring, travel) * tile
+        halo_turned = halo_turned + cosine * beyond
+        halo_travel = halo_travel + travel * beyond
+    rows = turned_rows(rows_ref)
+    atoms = types_ref.shape[1]
+    hits = (lax.broadcasted_iota(jnp.int32, (atoms, rows.shape[1]), 0) == rows).astype(F32)
+    own_beyond = gathered_ref[2 * mine + 1 - slab]
+    returned = lax.dot_general(
+        jnp.concatenate([halo_travel, halo_turned, own_beyond], axis=0),
+        hits,
+        (((1,), (1,)), ((), ())),
+        preferred_element_type=F32,
+        precision=lax.Precision.HIGHEST,
+    )
+    kick = step_size * jnp.where(types_ref[...] == 1, 1.0, 1.0 / heavy_mass)
+    for c in range(3):
+        positions_ref[c] = (
+            turned[c : c + 1] + crossed[3 + c : 4 + c] + kick * returned[c : c + 1]
+        )
+        velocities_ref[c] = (
+            turned[3 + c : 4 + c]
+            + crossed[c : c + 1]
+            + kick * returned[OCTET + c : OCTET + c + 1]
+        )
+        forces_ref[c] = part_ref[c : c + 1, 0:atoms] + returned[2 * OCTET + c : 2 * OCTET + c + 1]
+
+
 VMEM_SPEC = pl.BlockSpec(memory_space=pltpu.VMEM)
 SMEM_SPEC = pl.BlockSpec(memory_space=pltpu.SMEM)
+SMALL = pltpu.CompilerParams(vmem_limit_bytes=SMALL_LIMIT)
 
 
 def shape(*dims, dtype=F32):
     return jax.ShapeDtypeStruct(dims, dtype)
 
 
-def call_force(live_atoms, own, halo, neighbours, weights):
+def call_force(live_atoms, own, halo, neighbours, weights, velocities, parcels=1):
     atoms, slots = neighbours.shape
     entries = atoms + halo.shape[1]
     e1 = weights[0].shape[1]
@@ -468,14 +568,14 @@
     e3 = weights[4].shape[1]
     rows_two = e2 // e1 * CHUNK
     rows_three = e3 // e1 * CHUNK
-    assert slots == LANES and atoms == LANES and entries == 2 * LANES
+    assert entries <= DIGIT * DIGIT and slots == LANES and atoms == LANES and entries == 2 * LANES
     assert e3 == 2 * e2 and e2 == 2 * e1 and rows_three <= LANES and M2 <= e1
-    pairs = atoms // 2
+    groups = atoms // GROUP
     return pl.pallas_call(
         force_kernel,
-        out_shape=shape(OCTET, entries),
-        in_specs=[SMEM_SPEC] + [VMEM_SPEC] * (3 + len(weights)),
-        out_specs=VMEM_SPEC,
+        out_shape=(shape(OCTET, entries), shape(parcels, OCTET, atoms)),
+        in_specs=[SMEM_SPEC] + [VMEM_SPEC] * (4 + len(weights)),
+        out_specs=(VMEM_SPEC, VMEM_SPEC),
         scratch_shapes=[
             pltpu.VMEM((atoms, LANES), F32),
             pltpu.VMEM((LANES, LANES), F32),
@@ -487,23 +587,24 @@
             pltpu.VMEM((4 * atoms, slots), F32),
             pltpu.VMEM((3, atoms, slots), F32),
             pltpu.VMEM((atoms, slots), F32),
-            pltpu.VMEM((pairs, CHUNK, 2 * slots), F32),
-            pltpu.VMEM((pairs, rows_two, 2 * slots), F32),
-            pltpu.VMEM((pairs, rows_three, 2 * slots), F32),
-            pltpu.VMEM((pairs, rows_three, 2 * slots), BF16),
+            pltpu.VMEM((groups, CHUNK, GROUP * slots), BF16),
+            pltpu.VMEM((groups, rows_two, GROUP * slots), BF16),
+            pltpu.VMEM((groups, rows_three, GROUP * slots), BF16),
+            pltpu.VMEM((groups, rows_three, GROUP * slots), BF16),
             pltpu.VMEM((4 * atoms, rows_three), F32),
             pltpu.VMEM((4, rows_three, atoms), F32),
             pltpu.VMEM((e3 * M2, atoms), BF16),
-            pltpu.VMEM(((e3 + CHUNK) * M2, atoms), F32),
+            pltpu.VMEM((e3 * M2, atoms), F32),
+            pltpu.VMEM(weights[6].shape[::-1], BF16),
+            pltpu.VMEM((e3 * M2, 4 * atoms), BF16),
             pltpu.VMEM((4 * atoms, slots), F32),
             pltpu.VMEM((atoms, slots), F32),
-            pltpu.VMEM((4 * atoms, slots), F32),
             pltpu.VMEM((atoms, LANES), F32),
             pltpu.VMEM((OCTET, entries), F32),
         ],
         compiler_params=pltpu.CompilerParams(vmem_limit_bytes=VMEM_LIMIT),
         name="force",
-    )(live_atoms, own, halo, neighbours, *weights)
+    )(live_atoms, own, halo, neighbours, *weights, velocities)
 
 
 def row(array):
@@ -538,7 +639,7 @@
         row(embed_bias_two),
         embed_three,
         row(embed_bias_three),
-        fit_first,
+        fit_first.T,
         row(fit_bias_first),
         fit_second,
         row(fit_bias_second),
@@ -565,37 +666,55 @@
         )
 
     low, high = slice(0, half), slice(half, 2 * half)
-    rows = jnp.concatenate([halo_rows[:, high], halo_rows[:, low]], axis=1)
     types = row(atom_types)
     own, sent = pl.pallas_call(
         outgoing_kernel,
         out_shape=(shape(OCTET, atoms), shape(OCTET, 2 * half)),
         in_specs=[VMEM_SPEC] * 3,
         out_specs=(VMEM_SPEC, VMEM_SPEC),
+        compiler_params=SMALL,
         name="outgoing",
-    )(positions, types, rows)
+    )(positions, types, halo_rows)
     halo = exchange(sent, low, high)
-    part = call_force(live_atoms, own, halo, neighbours, weights)
+    place = jnp.stack([lax.axis_index("bead"), lax.axis_index("slab")]).astype(jnp.int32)
+    scalars = jnp.concatenate([live_atoms, place[1:]])
+    table = jnp.asarray(bead_tables(beads))
+    sharded_shape = shape(*positions.shape)
+    if slabs == 2:
+        part, parcels = call_force(
+            scalars, own, halo, neighbours, weights, velocities, beads * slabs
+        )
+        gathered = lax.all_to_all(
+            parcels, ("bead", "slab"), split_axis=0, concat_axis=0, tiled=True
+        )
+        return pl.pallas_call(
+            settle_kernel,
+            out_shape=(sharded_shape,) * 3,
+            in_specs=[SMEM_SPEC] * 2 + [VMEM_SPEC] * 4,
+            out_specs=(VMEM_SPEC,) * 3,
+            compiler_params=SMALL,
+            name="settle",
+        )(place, table, part, gathered, halo_rows, types)
+    part, _ = call_force(scalars, own, halo, neighbours, weights, velocities)
     back = exchange(part[:, atoms:], high, low)
-    if slabs != 2:
-        back = jnp.concatenate([back[:, high], back[:, low]], axis=1)
+    back = jnp.concatenate([back[:, high], back[:, low]], axis=1)
     forces, kicked = pl.pallas_call(
         kick_kernel,
-        out_shape=(shape(*positions.shape), shape(beads, OCTET, atoms)),
+        out_shape=(sharded_shape, shape(beads, OCTET, atoms)),
         in_specs=[VMEM_SPEC] * 6,
         out_specs=(VMEM_SPEC, VMEM_SPEC),
+        compiler_params=SMALL,
         name="kick",
-    )(part, back, rows, types, positions, velocities)
+    )(part, back, halo_rows, types, positions, velocities)
     gathered = lax.all_to_all(kicked, "bead", split_axis=0, concat_axis=0, tiled=True)
-    table = jnp.asarray(bead_tables(beads))
-    mine = lax.axis_index("bead").astype(jnp.int32).reshape(1)
     positions_new, velocities_new = pl.pallas_call(
         mix_kernel,
-        out_shape=(shape(*positions.shape), shape(*positions.shape)),
+        out_shape=(sharded_shape, sharded_shape),
         in_specs=[SMEM_SPEC, SMEM_SPEC, VMEM_SPEC],
         out_specs=(VMEM_SPEC, VMEM_SPEC),
+        compiler_params=SMALL,
         name="mix",
-    )(mine, table, gathered)
+    )(place, table, gathered)
     return positions_new, velocities_new, forces
 
 

time: 75.8 us -> 44.7 us (0.59)
  Pallas kernels: 52 us -> 13 us
  starting transfers between devices: 8.52 us -> 14.2 us
  local copies, waits for them, and re-layouts: 4.21 us -> 7.2 us
    pallas_call x3 -> x2, Pallas kernels: 50.6 us -> 12.9 us  [the longest x1 11.3 us: call_force(): pl.pallas_call(force_kernel, out_shape=(shape(OCTET, entries), shape(parc...]
    all_to_all x1, starting transfers between devices: 7.94 us -> 13.7 us  [local(): lax.all_to_all(parcels, ('bead', 'slab'), split_axis=0, concat_axis=0, ti...]
    unnamed x35 -> x38, local copies, waits for them, and re-layouts: 3.4 us -> 7.2 us
    pallas_call x1, Pallas kernels: 1.36 us -> 0.14 us  [local(): pl.pallas_call(outgoing_kernel, out_shape=(shape(OCTET, atoms), shape(OCT...]
    ppermute x2 -> x1, waiting for transfers between devices: 1.16 us -> 0.08 us  [exchange(): return lax.ppermute(outgoing, 'slab', to_next)]
    slice x2 -> x0, local copies, waits for them, and re-layouts: 0.8 us -> none  [the longest x1 0.8 us: local(): rows = jnp.concatenate([halo_rows[:, high], halo_rows[:, low]], axis=1)]
  transfers between devices with their start and end apart: 3 -> 2, of which waited for: 2 -> 2; matrix products, arithmetic and copies ran while one was open for 2% -> 0% of each run, Pallas kernels for 0% -> 0%
where the time goes in v2:
time: 44.7 us; the launch traced here: 44.1 us
  starting transfers between devices  14.2 us (32%)
  Pallas kernels  13 us (29%)
  waiting for transfers between devices  8.22 us (18%)
  local copies, waits for them, and re-layouts  7.2 us (16%)
  between operations  1.38 us (3%)
    all_to_all x1, starting transfers between devices, local(): lax.all_to_all(parcels, ('bead', 'slab'), split_axis=0, concat_axis=0, ti...  13.7 us
    pallas_call x1, Pallas kernels, call_force(): pl.pallas_call(force_kernel, out_shape=(shape(OCTET, entries), shape(parc...  11.3 us
    all_to_all x1, waiting for transfers between devices, local(): lax.all_to_all(parcels, ('bead', 'slab'), split_axis=0, concat_axis=0, ti...  8.14 us
    unnamed x38, local copies, waits for them, and re-layouts  7.2 us
    pallas_call x1, Pallas kernels, local(): pl.pallas_call(settle_kernel, out_shape=(sharded_shape,) * 3, in_specs=[S...  1.53 us
  transfers between devices with their start and end apart: 2, of which 2 were waited for; matrix products, arithmetic and copies ran while one was open for 0% of the time, Pallas kernels for 0%

profile of v2, /device:TPU:0, one launch (start us, length us, event | category | flops | bytes accessed | tf_op | source)
XLA Modules:
  0.0 44.1 jit_solution(9646772486626435405)
XLA Ops:
  0.6 0.0 copy-start.9
  0.6 0.0 copy-start.8
  0.7 0.0 copy-start.18
  0.7 0.6 %copy-done.9 = s32[1,128]{1,0:T(1,128)S(1)} copy-done((s32[1,128]{1,0:T(1,128)S(1)}, s32[1,128]{1,0:T(1,128)}, u32[]{:S(2)}) %copy-start.9) | copy-done | bytes 536
  1.3 0.0 copy-done.8
  1.3 0.7 %copy-done.11 = f32[3,1,128]{2,1,0:T(1,128)S(1)} copy-done((f32[3,1,128]{2,1,0:T(1,128)S(1)}, f32[3,1,128]{2,1,0:T(1,128)}, u32[]{:S(2)}) %copy-start.11) | copy-done | bytes 1560
  2.0 0.1 outgoing.1
  2.1 0.5 %collective-permute-start = (f32[8,128]{1,0:T(8,128)S(1)}, f32[8,128]{1,0:T(8,128)S(1)}, u32[]{:S(2)}, u32[]{:S(2)}) collective-permute-start(f32[8,128]{1,0:T(8,128)S(1)} %get-tuple-element.8), channel_id=1, source_target_pairs={{0,1},{1,0},{2,3},{3,2},{4,5},{5,4},{6,7},{7,6},{8,9},{9,8},{10,11... | collective-permute-start | bytes 12296 | tf_op jit(solution)/shard_map/ppermute | solution.py:659
  3.2 0.0 copy-start.5
  3.2 0.1 pad_add_fusion.1.live_ref
  3.3 0.1 collective-permute-done.halo_ref
  3.4 0.0 copy-start.10
  3.4 0.0 copy-done.18
  3.5 0.5 %copy-done.5 = bf16[25,50]{1,0:T(8,128)(2,1)S(1)} copy-done((bf16[25,50]{1,0:T(8,128)(2,1)S(1)}, bf16[25,50]{1,0:T(8,128)(2,1)}, u32[]{:S(2)}) %copy-start.5) | copy-done | bytes 2524
  3.9 0.2 copy-done.14
  4.1 0.0 copy-done.17
  4.1 0.0 copy-done.12
  4.1 0.0 copy-done.13
  4.1 0.0 copy-done.7
  4.2 0.0 copy-done.10
  4.2 1.1 %copy-done = bf16[1600,240]{0,1:T(8,128)(2,1)S(1)} copy-done((bf16[1600,240]{0,1:T(8,128)(2,1)S(1)}, bf16[1600,240]{0,1:T(8,128)(2,1)}, u32[]{:S(2)}) %copy-start) | copy-done | bytes 768024
  5.3 0.9 %copy-done.1 = bf16[240,240]{1,0:T(8,128)(2,1)S(1)} copy-done((bf16[240,240]{1,0:T(8,128)(2,1)S(1)}, bf16[240,240]{1,0:T(8,128)(2,1)}, u32[]{:S(2)}) %copy-start.1) | copy-done | bytes 115224
  6.2 0.9 %copy-done.2 = bf16[240,240]{1,0:T(8,128)(2,1)S(1)} copy-done((bf16[240,240]{1,0:T(8,128)(2,1)S(1)}, bf16[240,240]{1,0:T(8,128)(2,1)}, u32[]{:S(2)}) %copy-start.2) | copy-done | bytes 115224
  7.1 0.8 %copy-done.3 = s32[128,128]{1,0:T(8,128)S(1)} copy-done((s32[128,128]{1,0:T(8,128)S(1)}, s32[128,128]{1,0:T(8,128)}, u32[]{:S(2)}) %copy-start.3) | copy-done | bytes 65560
  8.0 0.7 %copy-done.15 = f32[240]{0:T(256)S(1)} copy-done((f32[240]{0:T(256)S(1)}, f32[240]{0:T(256)}, u32[]{:S(2)}) %copy-start.15) | copy-done | bytes 984
  8.6 0.7 %copy-done.16 = f32[240]{0:T(256)S(1)} copy-done((f32[240]{0:T(256)S(1)}, f32[240]{0:T(256)}, u32[]{:S(2)}) %copy-start.16) | copy-done | bytes 984
  9.3 11.3 %force.1 = (f32[8,256]{1,0:T(8,128)S(1)}, f32[32,8,128]{2,1,0:T(8,128)}) custom-call(s32[2]{0:T(128)S(1)} %pad_add_fusion.1.live_ref, f32[8,128]{1,0:T(8,128)S(1)} %get-tuple-element.7.own_ref, f32[8,128]{1,0:T(8,128)S(1)} %collective-permute-done.halo_ref, s32[128,128]{1,0:T(8,128)S(1)} %copy-done.3, f32[2,25]{1,0:T(2,128)S(1)} %copy-done.12, ...), custom_call_target="tpu_custom_call" | custom-call | tf_op jit(solution)/shard_map/force/pallas_call | solution.py:574
  20.6 13.7 %all-to-all-start = ((f32[32,8,128]{2,1,0:T(8,128)}), f32[32,8,128]{2,1,0:T(8,128)S(1)}, u32[]{:S(2)}, u32[]{:S(2)}) async-start(f32[32,8,128]{2,1,0:T(8,128)} %get-tuple-element.10), calls=%async_computation | async-start | bytes 262144 | tf_op jit(solution)/shard_map/all_to_all | solution.py:687
  34.4 0.0 copy-start.6
  34.4 0.1 pad_add_fusion.place_ref
  34.5 8.1 %all-to-all-done.gathered_ref = f32[32,8,128]{2,1,0:T(8,128)S(1)} async-done(((f32[32,8,128]{2,1,0:T(8,128)}), f32[32,8,128]{2,1,0:T(8,128)S(1)}, u32[]{:S(2)}, u32[]{:S(2)}) %all-to-all-start) | async-done | bytes 131104 | tf_op jit(solution)/shard_map/all_to_all | solution.py:687
  42.6 1.5 %settle.1 = (f32[3,1,128]{2,1,0:T(1,128)}, f32[3,1,128]{2,1,0:T(1,128)}, f32[3,1,128]{2,1,0:T(1,128)}) custom-call(s32[2]{0:T(128)S(1)} %pad_add_fusion.place_ref, f32[16,48]{1,0:T(8,128)S(1)} %copy-done.6, f32[8,256]{1,0:T(8,128)S(1)} %get-tuple-element.9.part_ref, f32[32,8,128]{2,1,0:T(8,128)S(1)} %all-to-all-done.gathered_ref, s32[1,128]{1,0:T(1,128)S(1)} %copy-done.9, ...), custom_call_target="tpu_custom_call" | custom-call | tf_op jit(solution)/shard_map/settle/pallas_call | solution.py:690
  (15 shorter events, 0.0 us)
Async XLA Ops:
  0.6 0.7 %copy-start.9 = (s32[1,128]{1,0:T(1,128)S(1)}, s32[1,128]{1,0:T(1,128)}, u32[]{:S(2)}) copy-start(s32[1,128]{1,0:T(1,128)} %rows_ref.3) | copy-start | bytes 1540
  0.6 0.7 %copy-start.8 = (s32[128]{0:T(128)S(1)}, s32[128]{0:T(128)}, u32[]{:S(2)}) copy-start(s32[128]{0:T(128)} %param.22) | copy-start | bytes 1540
  0.7 2.8 %copy-start.18 = (f32[100]{0:T(128)S(1)}, f32[100]{0:T(128)}, u32[]{:S(2)}) copy-start(f32[100]{0:T(128)} %param.31) | copy-start | bytes 1204
  1.3 0.7 %copy-start.11 = (f32[3,1,128]{2,1,0:T(1,128)S(1)}, f32[3,1,128]{2,1,0:T(1,128)}, u32[]{:S(2)}) copy-start(f32[3,1,128]{2,1,0:T(1,128)} %positions_ref.1) | copy-start | bytes 4612
  2.0 1.5 %copy-start.4 = (bf16[50,100]{1,0:T(8,128)(2,1)S(1)}, bf16[50,100]{1,0:T(8,128)(2,1)}, u32[]{:S(2)}) copy-start(bf16[50,100]{1,0:T(8,128)(2,1)} %three_ref.1) | copy-start | bytes 30004
  2.1 1.3 %collective-permute-start = (f32[8,128]{1,0:T(8,128)S(1)}, f32[8,128]{1,0:T(8,128)S(1)}, u32[]{:S(2)}, u32[]{:S(2)}) collective-permute-start(f32[8,128]{1,0:T(8,128)S(1)} %get-tuple-element.8), channel_id=1, source_target_pairs={{0,1},{1,0},{2,3},{3,2},{4,5},{5,4},{6,7},{7,6},{8,9},{9,8},{10,11... | collective-permute-start | bytes 12296 | tf_op jit(solution)/shard_map/ppermute | solution.py:659
  3.2 0.7 %copy-start.5 = (bf16[25,50]{1,0:T(8,128)(2,1)S(1)}, bf16[25,50]{1,0:T(8,128)(2,1)}, u32[]{:S(2)}) copy-start(bf16[25,50]{1,0:T(8,128)(2,1)} %two_ref.1) | copy-start | bytes 7504
  3.4 0.7 %copy-start.14 = (f32[240]{0:T(256)S(1)}, f32[240]{0:T(256)}, u32[]{:S(2)}) copy-start(f32[240]{0:T(256)} %param.33) | copy-start | bytes 2884
  3.4 0.7 %copy-start.17 = (f32[50]{0:T(128)S(1)}, f32[50]{0:T(128)}, u32[]{:S(2)}) copy-start(f32[50]{0:T(128)} %param.29) | copy-start | bytes 604
  3.4 0.7 %copy-start.12 = (f32[2,25]{1,0:T(2,128)S(1)}, f32[2,25]{1,0:T(2,128)}, u32[]{:S(2)}) copy-start(f32[2,25]{1,0:T(2,128)} %scale_ref.1) | copy-start | bytes 604
  3.4 0.7 %copy-start.13 = (f32[2,25]{1,0:T(2,128)S(1)}, f32[2,25]{1,0:T(2,128)}, u32[]{:S(2)}) copy-start(f32[2,25]{1,0:T(2,128)} %shift_ref.1) | copy-start | bytes 604
  3.4 0.7 %copy-start.7 = (f32[2,240]{1,0:T(2,128)S(1)}, f32[2,240]{1,0:T(2,128)}, u32[]{:S(2)}) copy-start(f32[2,240]{1,0:T(2,128)} %readout_ref.1) | copy-start | bytes 5764
  3.4 0.7 %copy-start.10 = (f32[3,1,128]{2,1,0:T(1,128)S(1)}, f32[3,1,128]{2,1,0:T(1,128)}, u32[]{:S(2)}) copy-start(f32[3,1,128]{2,1,0:T(1,128)} %velocities_ref.1) | copy-start | bytes 4612
  4.2 1.1 %copy-start = (bf16[1600,240]{0,1:T(8,128)(2,1)S(1)}, bf16[1600,240]{0,1:T(8,128)(2,1)}, u32[]{:S(2)}) copy-start(bf16[1600,240]{0,1:T(8,128)(2,1)} %param.32) | copy-start | bytes 2304004
  5.3 0.9 %copy-start.1 = (bf16[240,240]{1,0:T(8,128)(2,1)S(1)}, bf16[240,240]{1,0:T(8,128)(2,1)}, u32[]{:S(2)}) copy-start(bf16[240,240]{1,0:T(8,128)(2,1)} %second_ref.1) | copy-start | bytes 345604
  6.2 0.9 %copy-start.2 = (bf16[240,240]{1,0:T(8,128)(2,1)S(1)}, bf16[240,240]{1,0:T(8,128)(2,1)}, u32[]{:S(2)}) copy-start(bf16[240,240]{1,0:T(8,128)(2,1)} %third_ref.1) | copy-start | bytes 345604
  7.1 0.8 %copy-start.3 = (s32[128,128]{1,0:T(8,128)S(1)}, s32[128,128]{1,0:T(8,128)}, u32[]{:S(2)}) copy-start(s32[128,128]{1,0:T(8,128)} %listed_ref.1) | copy-start | bytes 196612
  7.9 0.7 %copy-start.15 = (f32[240]{0:T(256)S(1)}, f32[240]{0:T(256)}, u32[]{:S(2)}) copy-start(f32[240]{0:T(256)} %param.35) | copy-start | bytes 2884
  8.6 0.7 %copy-start.16 = (f32[240]{0:T(256)S(1)}, f32[240]{0:T(256)}, u32[]{:S(2)}) copy-start(f32[240]{0:T(256)} %param.37) | copy-start | bytes 2884
  20.6 22.0 %all-to-all-start = ((f32[32,8,128]{2,1,0:T(8,128)}), f32[32,8,128]{2,1,0:T(8,128)S(1)}, u32[]{:S(2)}, u32[]{:S(2)}) async-start(f32[32,8,128]{2,1,0:T(8,128)} %get-tuple-element.10), calls=%async_computation | async-start | bytes 262144 | tf_op jit(solution)/shard_map/all_to_all | solution.py:687
  34.4 8.2 %copy-start.6 = (f32[16,48]{1,0:T(8,128)S(1)}, f32[16,48]{1,0:T(8,128)}, u32[]{:S(2)}) copy-start(f32[16,48]{1,0:T(8,128)} %constant.10.clone.table_ref) | copy-start | bytes 9220

commit v3 on v2

--- a/solution.py
+++ b/solution.py
@@ -20,12 +20,13 @@
 BF16 = jnp.bfloat16
 LANES = 128
 OCTET = 8
-UNROLL = 8
+UNROLL = 16
+SKEW = 2
 DIGIT = 16
-GROUP = 8
+GROUP = 2
 CHUNK = 32
 ONE_AT = 20.0
-VMEM_LIMIT = 40 * 1024 * 1024
+VMEM_LIMIT = 55168 * 1024
 SMALL_LIMIT = 4 * 1024 * 1024
 
 
@@ -92,13 +93,13 @@
     bias_two_ref,
     three_ref,
     bias_three_ref,
-    first_ref,
-    fit_bias_first_ref,
-    second_ref,
-    fit_bias_second_ref,
-    third_ref,
-    fit_bias_third_ref,
-    readout_ref,
+    first_hbm,
+    fit_bias_first_hbm,
+    second_hbm,
+    fit_bias_second_hbm,
+    third_hbm,
+    fit_bias_third_hbm,
+    readout_hbm,
     velocities_ref,
     out_ref,
     parcels_ref,
@@ -126,6 +127,14 @@
     grad_strength,
     centre_terms,
     scattered,
+    first_ref,
+    fit_bias_first_ref,
+    second_ref,
+    fit_bias_second_ref,
+    third_ref,
+    fit_bias_third_ref,
+    readout_ref,
+    arrived,
 ):
     live = live_ref[0]
     octets = (live + (OCTET - 1)) // OCTET
@@ -136,7 +145,22 @@
     rows_one, rows_two, rows_three = two_in.shape[0], three_in.shape[0], three_out.shape[0]
     copies_two, copies_three = e2 // e1, e3 // e1
 
-    first_rows[...] = first_ref[...].T
+    late = [
+        pltpu.make_async_copy(source, target, arrived.at[k])
+        for k, (source, target) in enumerate(
+            (
+                (first_hbm, first_ref),
+                (fit_bias_first_hbm, fit_bias_first_ref),
+                (second_hbm, second_ref),
+                (fit_bias_second_hbm, fit_bias_second_ref),
+                (third_hbm, third_ref),
+                (fit_bias_third_hbm, fit_bias_third_ref),
+                (readout_hbm, readout_ref),
+            )
+        )
+    ]
+    for copy in late:
+        copy.start()
 
     def split_bias(bias):
         high = bias.astype(BF16).astype(F32)
@@ -213,6 +237,29 @@
 
         return lax.fori_loop(0, (octets + UNROLL - 1) // UNROLL, body, carry)
 
+    def run_skewed(stages, skew):
+        def body(turn, carry):
+            waiting = [stages(turn * UNROLL + u) for u in range(UNROLL)]
+            begun = 0
+            active = []
+            step = 0
+            while begun < UNROLL or active:
+                if begun < UNROLL and step % skew == 0:
+                    active.append(waiting[begun])
+                    begun += 1
+                still = []
+                for one in active:
+                    try:
+                        next(one)
+                        still.append(one)
+                    except StopIteration:
+                        pass
+                active = still
+                step += 1
+            return carry
+
+        lax.fori_loop(0, (octets + UNROLL - 1) // UNROLL, body, 0)
+
     def surround(octet, carry):
         first = pl.multiple_of(octet * OCTET, OCTET)
         listed, deltas, hydrogen = gather_octet(first)
@@ -227,7 +274,7 @@
 
     run_octets(surround)
 
-    def forward(octet, carry):
+    def forward(octet):
         first = pl.multiple_of(octet * OCTET, OCTET)
         hydrogen = around[pl.ds(first, OCTET), :]
         rows = pl.ds(pl.multiple_of(first * 4, OCTET * 4), OCTET * 4)
@@ -241,6 +288,7 @@
                     line * consts[0] + consts[2] + kind * (line * consts[1] + consts[3])
                 )
             ones.append(jnp.tanh(jnp.concatenate(inputs, axis=1).astype(BF16)))
+            yield
         for g in groups:
             kept_one[octet * len(groups) + g] = ones[g]
             two = jnp.tanh(
@@ -248,6 +296,7 @@
             )
             kept_two[octet * len(groups) + g] = two
             twos.append(two + jnp.concatenate([ones[g]] * copies_two, axis=0))
+            yield
         by_slot = environ[rows, :].T.astype(BF16)
         column = lax.broadcasted_iota(jnp.int32, by_slot.shape, 1) // 4
         total = jnp.zeros((rows_three, OCTET * 4), F32)
@@ -266,11 +315,14 @@
                 axis=0,
             )
             total = total + jnp.dot(sum_three, blocks, preferred_element_type=F32)
+            yield
         features[rows, :] = total.T
-        return carry
-
-    run_octets(forward)
-
+
+    run_skewed(forward, SKEW)
+
+    for copy in late:
+        copy.wait()
+    first_rows[...] = first_ref[...].T
     for c in range(4):
         features_t[c] = features[pl.ds(c, atoms, stride=4), :].T * (1.0 / slots)
 
@@ -331,7 +383,7 @@
     centre_terms[...] = jnp.zeros_like(centre_terms)
     lane = lax.broadcasted_iota(jnp.int32, (OCTET, LANES), 1)
 
-    def backward(octet, carry):
+    def backward(octet):
         first = pl.multiple_of(octet * OCTET, OCTET)
         grad_rows = features[pl.ds(pl.multiple_of(first * 4, OCTET * 4), OCTET * 4), :]
         grad_cols = grad_rows.T.astype(BF16)
@@ -355,6 +407,7 @@
             three = kept_three[at]
             inners.append(grad_three * (1.0 - three * three))
             grad_threes.append(grad_three[:rows_two] + grad_three[rows_two:])
+            yield
         for g in groups:
             at = octet * len(groups) + g
             grad_two = (
@@ -372,6 +425,7 @@
                 by_quad = jnp.where(
                     owner == g * GROUP + k, both[:, k * LANES : (k + 1) * LANES], by_quad
                 )
+            yield
         grad_environ[rows, :] = by_quad
         for g in groups:
             at = octet * len(groups) + g
@@ -386,9 +440,8 @@
                 )
                 grad_strength[pl.ds(line, 1), :] = jnp.sum(weighed, axis=0, keepdims=True)
 
-        return carry
-
-    run_octets(backward)
+
+    run_skewed(backward, SKEW)
 
     numbers = lax.broadcasted_iota(jnp.int32, (DIGIT, LANES), 0).astype(F32).astype(BF16)
 
@@ -552,6 +605,7 @@
 
 
 VMEM_SPEC = pl.BlockSpec(memory_space=pltpu.VMEM)
+HBM_SPEC = pl.BlockSpec(memory_space=pltpu.HBM)
 SMEM_SPEC = pl.BlockSpec(memory_space=pltpu.SMEM)
 SMALL = pltpu.CompilerParams(vmem_limit_bytes=SMALL_LIMIT)
 
@@ -574,7 +628,10 @@
     return pl.pallas_call(
         force_kernel,
         out_shape=(shape(OCTET, entries), shape(parcels, OCTET, atoms)),
-        in_specs=[SMEM_SPEC] + [VMEM_SPEC] * (4 + len(weights)),
+        in_specs=[SMEM_SPEC]
+        + [VMEM_SPEC] * 9
+        + [HBM_SPEC] * (len(weights) - 6)
+        + [VMEM_SPEC],
         out_specs=(VMEM_SPEC, VMEM_SPEC),
         scratch_shapes=[
             pltpu.VMEM((atoms, LANES), F32),
@@ -601,7 +658,9 @@
             pltpu.VMEM((atoms, slots), F32),
             pltpu.VMEM((atoms, LANES), F32),
             pltpu.VMEM((OCTET, entries), F32),
-        ],
+        ]
+        + [pltpu.VMEM(w.shape, w.dtype) for w in weights[6:]]
+        + [pltpu.SemaphoreType.DMA((len(weights) - 6,))],
         compiler_params=pltpu.CompilerParams(vmem_limit_bytes=VMEM_LIMIT),
         name="force",
     )(live_atoms, own, halo, neighbours, *weights, velocities)

time: 44.7 us -> 35.3 us (0.79)
  starting transfers between devices: 14.2 us -> 7.64 us
  local copies, waits for them, and re-layouts: 7.2 us -> 2.09 us
  Pallas kernels: 13 us -> 15.5 us
    all_to_all x1, starting transfers between devices: 13.7 us -> 7.19 us  [local(): lax.all_to_all(parcels, ('bead', 'slab'), split_axis=0, concat_axis=0, ti...]
    unnamed x38 -> x28, local copies, waits for them, and re-layouts: 7.2 us -> 2.09 us
    pallas_call x1, Pallas kernels: 11.3 us -> 13.9 us  [call_force(): pl.pallas_call(force_kernel, out_shape=(shape(OCTET, entries), shape(parc...]
  transfers between devices with their start and end apart: 2 -> 2, of which waited for: 2 -> 1; matrix products, arithmetic and copies ran while one was open for 0% -> 0% of each run, Pallas kernels for 0% -> 0%
where the time goes in v3:
time: 35.3 us; the launch traced here: 35 us
  Pallas kernels  15.5 us (44%)
  waiting for transfers between devices  8.18 us (23%)
  starting transfers between devices  7.64 us (22%)
  local copies, waits for them, and re-layouts  2.09 us (6%)
  between operations  1.4 us (4%)
    pallas_call x1, Pallas kernels, call_force(): pl.pallas_call(force_kernel, out_shape=(shape(OCTET, entries), shape(parc...  13.9 us
    all_to_all x1, waiting for transfers between devices, local(): lax.all_to_all(parcels, ('bead', 'slab'), split_axis=0, concat_axis=0, ti...  8.14 us
    all_to_all x1, starting transfers between devices, local(): lax.all_to_all(parcels, ('bead', 'slab'), split_axis=0, concat_axis=0, ti...  7.19 us
    unnamed x28, local copies, waits for them, and re-layouts  2.09 us
    pallas_call x1, Pallas kernels, local(): pl.pallas_call(settle_kernel, out_shape=(sharded_shape,) * 3, in_specs=[S...  1.53 us
  transfers between devices with their start and end apart: 2, of which 1 were waited for; matrix products, arithmetic and copies ran while one was open for 0% of the time, Pallas kernels for 0%

profile of v3, /device:TPU:0, one launch (start us, length us, event | category | flops | bytes accessed | tf_op | source)
XLA Modules:
  0.0 35.0 jit_solution(9278811434487166168)
XLA Ops:
  0.6 0.0 copy-start.4
  0.6 0.0 copy-start.3
  0.7 0.6 %copy-done.4 = s32[1,128]{1,0:T(1,128)S(1)} copy-done((s32[1,128]{1,0:T(1,128)S(1)}, s32[1,128]{1,0:T(1,128)}, u32[]{:S(2)}) %copy-start.4) | copy-done | bytes 536
  1.3 0.0 copy-done.3
  1.3 0.0 copy-start.6
  1.3 0.7 %copy-done.6 = f32[3,1,128]{2,1,0:T(1,128)S(1)} copy-done((f32[3,1,128]{2,1,0:T(1,128)S(1)}, f32[3,1,128]{2,1,0:T(1,128)}, u32[]{:S(2)}) %copy-start.6) | copy-done | bytes 1560
  2.0 0.1 outgoing.1
  2.1 0.5 %collective-permute-start = (f32[8,128]{1,0:T(8,128)S(1)}, f32[8,128]{1,0:T(8,128)S(1)}, u32[]{:S(2)}, u32[]{:S(2)}) collective-permute-start(f32[8,128]{1,0:T(8,128)S(1)} %get-tuple-element.8), channel_id=1, source_target_pairs={{0,1},{1,0},{2,3},{3,2},{4,5},{5,4},{6,7},{7,6},{8,9},{9,8},{10,11... | collective-permute-start | bytes 12296 | tf_op jit(solution)/shard_map/ppermute | solution.py:718
  2.6 0.0 copy-start.13
  3.2 0.0 copy-start.10
  3.3 0.0 copy-start.11
  3.3 0.0 copy-start
  3.3 0.1 pad_add_fusion.1.live_ref
  3.4 0.0 collective-permute-done.halo_ref
  3.4 0.0 copy-start.5
  3.4 0.0 copy-done.13
  3.4 0.5 %copy-done.10 = f32[240]{0:T(256)S(1)} copy-done((f32[240]{0:T(256)S(1)}, f32[240]{0:T(256)}, u32[]{:S(2)}) %copy-start.10) | copy-done | bytes 984
  3.9 0.0 copy-done.11
  3.9 0.0 copy-done
  4.0 0.1 copy-done.9
  4.1 0.0 copy-done.12
  4.1 0.0 copy-done.7
  4.1 0.0 copy-done.8
  4.1 0.0 copy-done.2
  4.1 0.0 copy-done.5
  4.2 13.9 %force.1 = (f32[8,256]{1,0:T(8,128)S(1)}, f32[32,8,128]{2,1,0:T(8,128)}) custom-call(s32[2]{0:T(128)S(1)} %pad_add_fusion.1.live_ref, f32[8,128]{1,0:T(8,128)S(1)} %get-tuple-element.7.own_ref, f32[8,128]{1,0:T(8,128)S(1)} %collective-permute-done.halo_ref, s32[128,128]{1,0:T(8,128)} %listed_ref.1, f32[2,25]{1,0:T(2,128)S(1)} %copy-done.7, ...), custom_call_target="tpu_custom_call" | custom-call | tf_op jit(solution)/shard_map/force/pallas_call | solution.py:628
  18.0 7.2 %all-to-all-start = ((f32[32,8,128]{2,1,0:T(8,128)}), f32[32,8,128]{2,1,0:T(8,128)S(1)}, u32[]{:S(2)}, u32[]{:S(2)}) async-start(f32[32,8,128]{2,1,0:T(8,128)} %get-tuple-element.10), calls=%async_computation | async-start | bytes 262144 | tf_op jit(solution)/shard_map/all_to_all | solution.py:746
  25.2 0.0 copy-start.1
  25.3 0.1 pad_add_fusion.place_ref
  25.3 8.1 %all-to-all-done.gathered_ref = f32[32,8,128]{2,1,0:T(8,128)S(1)} async-done(((f32[32,8,128]{2,1,0:T(8,128)}), f32[32,8,128]{2,1,0:T(8,128)S(1)}, u32[]{:S(2)}, u32[]{:S(2)}) %all-to-all-start) | async-done | bytes 131104 | tf_op jit(solution)/shard_map/all_to_all | solution.py:746
  33.5 0.0 copy-done.1
  33.5 1.5 %settle.1 = (f32[3,1,128]{2,1,0:T(1,128)}, f32[3,1,128]{2,1,0:T(1,128)}, f32[3,1,128]{2,1,0:T(1,128)}) custom-call(s32[2]{0:T(128)S(1)} %pad_add_fusion.place_ref, f32[16,48]{1,0:T(8,128)S(1)} %copy-done.1, f32[8,256]{1,0:T(8,128)S(1)} %get-tuple-element.9.part_ref, f32[32,8,128]{2,1,0:T(8,128)S(1)} %all-to-all-done.gathered_ref, s32[1,128]{1,0:T(1,128)S(1)} %copy-done.4, ...), custom_call_target="tpu_custom_call" | custom-call | tf_op jit(solution)/shard_map/settle/pallas_call | solution.py:749
  (5 shorter events, 0.0 us)
Async XLA Ops:
  0.6 0.7 %copy-start.4 = (s32[1,128]{1,0:T(1,128)S(1)}, s32[1,128]{1,0:T(1,128)}, u32[]{:S(2)}) copy-start(s32[1,128]{1,0:T(1,128)} %rows_ref.3) | copy-start | bytes 1540
  0.6 0.7 %copy-start.3 = (s32[128]{0:T(128)S(1)}, s32[128]{0:T(128)}, u32[]{:S(2)}) copy-start(s32[128]{0:T(128)} %param.22) | copy-start | bytes 1540
  1.3 0.7 %copy-start.6 = (f32[3,1,128]{2,1,0:T(1,128)S(1)}, f32[3,1,128]{2,1,0:T(1,128)}, u32[]{:S(2)}) copy-start(f32[3,1,128]{2,1,0:T(1,128)} %positions_ref.1) | copy-start | bytes 4612
  2.1 1.3 %collective-permute-start = (f32[8,128]{1,0:T(8,128)S(1)}, f32[8,128]{1,0:T(8,128)S(1)}, u32[]{:S(2)}, u32[]{:S(2)}) collective-permute-start(f32[8,128]{1,0:T(8,128)S(1)} %get-tuple-element.8), channel_id=1, source_target_pairs={{0,1},{1,0},{2,3},{3,2},{4,5},{5,4},{6,7},{7,6},{8,9},{9,8},{10,11... | collective-permute-start | bytes 12296 | tf_op jit(solution)/shard_map/ppermute | solution.py:718
  2.6 0.9 %copy-start.13 = (f32[100]{0:T(128)S(1)}, f32[100]{0:T(128)}, u32[]{:S(2)}) copy-start(f32[100]{0:T(128)} %param.31) | copy-start | bytes 1204
  3.2 0.7 %copy-start.10 = (f32[240]{0:T(256)S(1)}, f32[240]{0:T(256)}, u32[]{:S(2)}) copy-start(f32[240]{0:T(256)} %param.35) | copy-start | bytes 2884
  3.3 0.7 %copy-start.11 = (f32[240]{0:T(256)S(1)}, f32[240]{0:T(256)}, u32[]{:S(2)}) copy-start(f32[240]{0:T(256)} %param.37) | copy-start | bytes 2884
  3.3 0.7 %copy-start = (bf16[25,50]{1,0:T(8,128)(2,1)S(1)}, bf16[25,50]{1,0:T(8,128)(2,1)}, u32[]{:S(2)}) copy-start(bf16[25,50]{1,0:T(8,128)(2,1)} %two_ref.1) | copy-start | bytes 7504
  3.4 0.7 %copy-start.9 = (f32[240]{0:T(256)S(1)}, f32[240]{0:T(256)}, u32[]{:S(2)}) copy-start(f32[240]{0:T(256)} %param.33) | copy-start | bytes 2884
  3.4 0.7 %copy-start.12 = (f32[50]{0:T(128)S(1)}, f32[50]{0:T(128)}, u32[]{:S(2)}) copy-start(f32[50]{0:T(128)} %param.29) | copy-start | bytes 604
  3.4 0.7 %copy-start.7 = (f32[2,25]{1,0:T(2,128)S(1)}, f32[2,25]{1,0:T(2,128)}, u32[]{:S(2)}) copy-start(f32[2,25]{1,0:T(2,128)} %scale_ref.1) | copy-start | bytes 604
  3.4 0.7 %copy-start.8 = (f32[2,25]{1,0:T(2,128)S(1)}, f32[2,25]{1,0:T(2,128)}, u32[]{:S(2)}) copy-start(f32[2,25]{1,0:T(2,128)} %shift_ref.1) | copy-start | bytes 604
  3.4 0.7 %copy-start.2 = (f32[2,240]{1,0:T(2,128)S(1)}, f32[2,240]{1,0:T(2,128)}, u32[]{:S(2)}) copy-start(f32[2,240]{1,0:T(2,128)} %readout_hbm.1) | copy-start | bytes 5764
  3.4 0.7 %copy-start.5 = (f32[3,1,128]{2,1,0:T(1,128)S(1)}, f32[3,1,128]{2,1,0:T(1,128)}, u32[]{:S(2)}) copy-start(f32[3,1,128]{2,1,0:T(1,128)} %velocities_ref.1) | copy-start | bytes 4612
  18.0 15.4 %all-to-all-start = ((f32[32,8,128]{2,1,0:T(8,128)}), f32[32,8,128]{2,1,0:T(8,128)S(1)}, u32[]{:S(2)}, u32[]{:S(2)}) async-start(f32[32,8,128]{2,1,0:T(8,128)} %get-tuple-element.10), calls=%async_computation | async-start | bytes 262144 | tf_op jit(solution)/shard_map/all_to_all | solution.py:746
  25.2 8.2 %copy-start.1 = (f32[16,48]{1,0:T(8,128)S(1)}, f32[16,48]{1,0:T(8,128)}, u32[]{:S(2)}) copy-start(f32[16,48]{1,0:T(8,128)} %constant.10.clone.table_ref) | copy-start | bytes 9220

commit v4 on v3

--- a/solution.py
+++ b/solution.py
@@ -21,7 +21,6 @@
 LANES = 128
 OCTET = 8
 UNROLL = 16
-SKEW = 2
 DIGIT = 16
 GROUP = 2
 CHUNK = 32
@@ -318,7 +317,7 @@
             yield
         features[rows, :] = total.T
 
-    run_skewed(forward, SKEW)
+    run_skewed(forward, 2)
 
     for copy in late:
         copy.wait()
@@ -369,9 +368,9 @@
         for c in range(4):
             shared[c] = shared[c] + rows * features_t[c, at : at + 1, :]
             products[e * M2 : (e + 1) * M2, c * atoms : (c + 1) * atoms] = packed * short[c]
-    unit = lax.broadcasted_iota(jnp.int32, (rows_three, e3 * M2), 0)
+    unit = lax.broadcasted_iota(jnp.int32, (rows_three, 1), 0)
     unit = jnp.where(unit % CHUNK < e1, unit // CHUNK * e1 + unit % CHUNK, -1)
-    gather = (lax.broadcasted_iota(jnp.int32, (rows_three, e3 * M2), 1) // M2 == unit).astype(F32)
+    gather = (lax.broadcasted_iota(jnp.int32, (1, e3 * M2), 1) // M2 == unit).astype(F32)
     sums = jnp.dot(gather.astype(BF16), products[...], preferred_element_type=F32)
     for c in range(4):
         total = sums[:, c * atoms : (c + 1) * atoms] + jnp.concatenate(
@@ -441,7 +440,7 @@
                 grad_strength[pl.ds(line, 1), :] = jnp.sum(weighed, axis=0, keepdims=True)
 
 
-    run_skewed(backward, SKEW)
+    run_skewed(backward, 1)
 
     numbers = lax.broadcasted_iota(jnp.int32, (DIGIT, LANES), 0).astype(F32).astype(BF16)
 
@@ -582,15 +581,21 @@
         halo_travel = halo_travel + travel * beyond
     rows = turned_rows(rows_ref)
     atoms = types_ref.shape[1]
-    hits = (lax.broadcasted_iota(jnp.int32, (atoms, rows.shape[1]), 0) == rows).astype(F32)
+    hits = lax.broadcasted_iota(jnp.int32, (atoms, rows.shape[1]), 0) == rows
     own_beyond = gathered_ref[2 * mine + 1 - slab]
-    returned = lax.dot_general(
-        jnp.concatenate([halo_travel, halo_turned, own_beyond], axis=0),
-        hits,
+    rest = jnp.concatenate([halo_travel, halo_turned, own_beyond], axis=0)
+    parts = []
+    for _ in range(3):
+        parts.append(rest.astype(BF16))
+        rest = rest - parts[-1].astype(F32)
+    sums = lax.dot_general(
+        jnp.concatenate(parts, axis=0),
+        hits.astype(F32).astype(BF16),
         (((1,), (1,)), ((), ())),
         preferred_element_type=F32,
-        precision=lax.Precision.HIGHEST,
-    )
+    )
+    tall = 3 * OCTET
+    returned = sums[:tall] + sums[tall : 2 * tall] + sums[2 * tall :]
     kick = step_size * jnp.where(types_ref[...] == 1, 1.0, 1.0 / heavy_mass)
     for c in range(3):
         positions_ref[c] = (

time: 35.3 us -> 34.9 us (0.989)
  Pallas kernels: 15.5 us -> 15.1 us
where the time goes in v4:
time: 34.9 us; the launch traced here: 34.6 us
  Pallas kernels  15.1 us (43%)
  waiting for transfers between devices  8.18 us (23%)
  starting transfers between devices  7.65 us (22%)
  local copies, waits for them, and re-layouts  2.09 us (6%)
  between operations  1.4 us (4%)
    pallas_call x1, Pallas kernels, call_force(): pl.pallas_call(force_kernel, out_shape=(shape(OCTET, entries), shape(parc...  13.5 us
    all_to_all x1, waiting for transfers between devices, local(): lax.all_to_all(parcels, ('bead', 'slab'), split_axis=0, concat_axis=0, ti...  8.14 us
    all_to_all x1, starting transfers between devices, local(): lax.all_to_all(parcels, ('bead', 'slab'), split_axis=0, concat_axis=0, ti...  7.19 us
    unnamed x28, local copies, waits for them, and re-layouts  2.09 us
    pallas_call x1, Pallas kernels, local(): pl.pallas_call(settle_kernel, out_shape=(sharded_shape,) * 3, in_specs=[S...  1.47 us
  transfers between devices with their start and end apart: 2, of which 1 were waited for; matrix products, arithmetic and copies ran while one was open for 0% of the time, Pallas kernels for 0%

profile of v4, /device:TPU:0, one launch (start us, length us, event | category | flops | bytes accessed | tf_op | source)
XLA Modules:
  0.0 34.6 jit_solution(9308062332815130155)
XLA Ops:
  0.6 0.0 copy-start.4
  0.6 0.0 copy-start.3
  0.7 0.6 %copy-done.4 = s32[1,128]{1,0:T(1,128)S(1)} copy-done((s32[1,128]{1,0:T(1,128)S(1)}, s32[1,128]{1,0:T(1,128)}, u32[]{:S(2)}) %copy-start.4) | copy-done | bytes 536
  1.3 0.0 copy-done.3
  1.3 0.0 copy-start.6
  1.3 0.7 %copy-done.6 = f32[3,1,128]{2,1,0:T(1,128)S(1)} copy-done((f32[3,1,128]{2,1,0:T(1,128)S(1)}, f32[3,1,128]{2,1,0:T(1,128)}, u32[]{:S(2)}) %copy-start.6) | copy-done | bytes 1560
  2.0 0.1 outgoing.1
  2.1 0.5 %collective-permute-start = (f32[8,128]{1,0:T(8,128)S(1)}, f32[8,128]{1,0:T(8,128)S(1)}, u32[]{:S(2)}, u32[]{:S(2)}) collective-permute-start(f32[8,128]{1,0:T(8,128)S(1)} %get-tuple-element.8), channel_id=1, source_target_pairs={{0,1},{1,0},{2,3},{3,2},{4,5},{5,4},{6,7},{7,6},{8,9},{9,8},{10,11... | collective-permute-start | bytes 12296 | tf_op jit(solution)/shard_map/ppermute | solution.py:723
  2.6 0.0 copy-start.13
  3.2 0.0 copy-start.10
  3.3 0.0 copy-start.11
  3.3 0.0 copy-start
  3.3 0.1 pad_add_fusion.1.live_ref
  3.4 0.0 collective-permute-done.halo_ref
  3.4 0.0 copy-start.5
  3.4 0.0 copy-done.13
  3.4 0.5 %copy-done.10 = f32[240]{0:T(256)S(1)} copy-done((f32[240]{0:T(256)S(1)}, f32[240]{0:T(256)}, u32[]{:S(2)}) %copy-start.10) | copy-done | bytes 984
  3.9 0.0 copy-done.11
  3.9 0.0 copy-done
  4.0 0.1 copy-done.9
  4.1 0.0 copy-done.12
  4.1 0.0 copy-done.7
  4.1 0.0 copy-done.8
  4.1 0.0 copy-done.2
  4.1 0.0 copy-done.5
  4.2 13.5 %force.1 = (f32[8,256]{1,0:T(8,128)S(1)}, f32[32,8,128]{2,1,0:T(8,128)}) custom-call(s32[2]{0:T(128)S(1)} %pad_add_fusion.1.live_ref, f32[8,128]{1,0:T(8,128)S(1)} %get-tuple-element.7.own_ref, f32[8,128]{1,0:T(8,128)S(1)} %collective-permute-done.halo_ref, s32[128,128]{1,0:T(8,128)} %listed_ref.1, f32[2,25]{1,0:T(2,128)S(1)} %copy-done.7, ...), custom_call_target="tpu_custom_call" | custom-call | tf_op jit(solution)/shard_map/force/pallas_call | solution.py:633
  17.7 7.2 %all-to-all-start = ((f32[32,8,128]{2,1,0:T(8,128)}), f32[32,8,128]{2,1,0:T(8,128)S(1)}, u32[]{:S(2)}, u32[]{:S(2)}) async-start(f32[32,8,128]{2,1,0:T(8,128)} %get-tuple-element.10), calls=%async_computation | async-start | bytes 262144 | tf_op jit(solution)/shard_map/all_to_all | solution.py:751
  24.9 0.0 copy-start.1
  24.9 0.1 pad_add_fusion.place_ref
  25.0 8.1 %all-to-all-done.gathered_ref = f32[32,8,128]{2,1,0:T(8,128)S(1)} async-done(((f32[32,8,128]{2,1,0:T(8,128)}), f32[32,8,128]{2,1,0:T(8,128)S(1)}, u32[]{:S(2)}, u32[]{:S(2)}) %all-to-all-start) | async-done | bytes 131104 | tf_op jit(solution)/shard_map/all_to_all | solution.py:751
  33.1 0.0 copy-done.1
  33.1 1.5 %settle.1 = (f32[3,1,128]{2,1,0:T(1,128)}, f32[3,1,128]{2,1,0:T(1,128)}, f32[3,1,128]{2,1,0:T(1,128)}) custom-call(s32[2]{0:T(128)S(1)} %pad_add_fusion.place_ref, f32[16,48]{1,0:T(8,128)S(1)} %copy-done.1, f32[8,256]{1,0:T(8,128)S(1)} %get-tuple-element.9.part_ref, f32[32,8,128]{2,1,0:T(8,128)S(1)} %all-to-all-done.gathered_ref, s32[1,128]{1,0:T(1,128)S(1)} %copy-done.4, ...), custom_call_target="tpu_custom_call" | custom-call | tf_op jit(solution)/shard_map/settle/pallas_call | solution.py:754
  (5 shorter events, 0.0 us)
Async XLA Ops:
  0.6 0.7 %copy-start.4 = (s32[1,128]{1,0:T(1,128)S(1)}, s32[1,128]{1,0:T(1,128)}, u32[]{:S(2)}) copy-start(s32[1,128]{1,0:T(1,128)} %rows_ref.3) | copy-start | bytes 1540
  0.6 0.7 %copy-start.3 = (s32[128]{0:T(128)S(1)}, s32[128]{0:T(128)}, u32[]{:S(2)}) copy-start(s32[128]{0:T(128)} %param.22) | copy-start | bytes 1540
  1.3 0.7 %copy-start.6 = (f32[3,1,128]{2,1,0:T(1,128)S(1)}, f32[3,1,128]{2,1,0:T(1,128)}, u32[]{:S(2)}) copy-start(f32[3,1,128]{2,1,0:T(1,128)} %positions_ref.1) | copy-start | bytes 4612
  2.1 1.3 %collective-permute-start = (f32[8,128]{1,0:T(8,128)S(1)}, f32[8,128]{1,0:T(8,128)S(1)}, u32[]{:S(2)}, u32[]{:S(2)}) collective-permute-start(f32[8,128]{1,0:T(8,128)S(1)} %get-tuple-element.8), channel_id=1, source_target_pairs={{0,1},{1,0},{2,3},{3,2},{4,5},{5,4},{6,7},{7,6},{8,9},{9,8},{10,11... | collective-permute-start | bytes 12296 | tf_op jit(solution)/shard_map/ppermute | solution.py:723
  2.6 0.9 %copy-start.13 = (f32[100]{0:T(128)S(1)}, f32[100]{0:T(128)}, u32[]{:S(2)}) copy-start(f32[100]{0:T(128)} %param.31) | copy-start | bytes 1204
  3.2 0.7 %copy-start.10 = (f32[240]{0:T(256)S(1)}, f32[240]{0:T(256)}, u32[]{:S(2)}) copy-start(f32[240]{0:T(256)} %param.35) | copy-start | bytes 2884
  3.3 0.7 %copy-start.11 = (f32[240]{0:T(256)S(1)}, f32[240]{0:T(256)}, u32[]{:S(2)}) copy-start(f32[240]{0:T(256)} %param.37) | copy-start | bytes 2884
  3.3 0.7 %copy-start = (bf16[25,50]{1,0:T(8,128)(2,1)S(1)}, bf16[25,50]{1,0:T(8,128)(2,1)}, u32[]{:S(2)}) copy-start(bf16[25,50]{1,0:T(8,128)(2,1)} %two_ref.1) | copy-start | bytes 7504
  3.4 0.7 %copy-start.9 = (f32[240]{0:T(256)S(1)}, f32[240]{0:T(256)}, u32[]{:S(2)}) copy-start(f32[240]{0:T(256)} %param.33) | copy-start | bytes 2884
  3.4 0.7 %copy-start.12 = (f32[50]{0:T(128)S(1)}, f32[50]{0:T(128)}, u32[]{:S(2)}) copy-start(f32[50]{0:T(128)} %param.29) | copy-start | bytes 604
  3.4 0.7 %copy-start.7 = (f32[2,25]{1,0:T(2,128)S(1)}, f32[2,25]{1,0:T(2,128)}, u32[]{:S(2)}) copy-start(f32[2,25]{1,0:T(2,128)} %scale_ref.1) | copy-start | bytes 604
  3.4 0.7 %copy-start.8 = (f32[2,25]{1,0:T(2,128)S(1)}, f32[2,25]{1,0:T(2,128)}, u32[]{:S(2)}) copy-start(f32[2,25]{1,0:T(2,128)} %shift_ref.1) | copy-start | bytes 604
  3.4 0.7 %copy-start.2 = (f32[2,240]{1,0:T(2,128)S(1)}, f32[2,240]{1,0:T(2,128)}, u32[]{:S(2)}) copy-start(f32[2,240]{1,0:T(2,128)} %readout_hbm.1) | copy-start | bytes 5764
  3.4 0.7 %copy-start.5 = (f32[3,1,128]{2,1,0:T(1,128)S(1)}, f32[3,1,128]{2,1,0:T(1,128)}, u32[]{:S(2)}) copy-start(f32[3,1,128]{2,1,0:T(1,128)} %velocities_ref.1) | copy-start | bytes 4612
  17.7 15.4 %all-to-all-start = ((f32[32,8,128]{2,1,0:T(8,128)}), f32[32,8,128]{2,1,0:T(8,128)S(1)}, u32[]{:S(2)}, u32[]{:S(2)}) async-start(f32[32,8,128]{2,1,0:T(8,128)} %get-tuple-element.10), calls=%async_computation | async-start | bytes 262144 | tf_op jit(solution)/shard_map/all_to_all | solution.py:751
  24.9 8.2 %copy-start.1 = (f32[16,48]{1,0:T(8,128)S(1)}, f32[16,48]{1,0:T(8,128)}, u32[]{:S(2)}) copy-start(f32[16,48]{1,0:T(8,128)} %constant.10.clone.table_ref) | copy-start | bytes 9220

commit v5 on v4

--- a/solution.py
+++ b/solution.py
@@ -69,22 +69,25 @@
     return jnp.concatenate([rows[:, half:], rows[:, :half]], axis=1)
 
 
+def field_table(positions_ref, types_ref):
+    hydrogen = (types_ref[...] == 1).astype(F32)
+    return jnp.concatenate(
+        [positions_ref[0], positions_ref[1], positions_ref[2], hydrogen]
+        + [jnp.zeros((OCTET - 4, hydrogen.shape[1]), F32)],
+        axis=0,
+    )
+
+
 def outgoing_kernel(positions_ref, types_ref, rows_ref, own_ref, send_ref):
-    hydrogen = (types_ref[...] == 1).astype(F32)
-    atoms = hydrogen.shape[1]
-    own = jnp.concatenate(
-        [positions_ref[0], positions_ref[1], positions_ref[2], hydrogen]
-        + [jnp.zeros((OCTET - 4, atoms), F32)],
-        axis=0,
-    )
+    own = field_table(positions_ref, types_ref)
     own_ref[...] = own
     send_ref[...] = lookup(own, jnp.broadcast_to(turned_rows(rows_ref), own.shape))
 
 
 def force_kernel(
     live_ref,
-    own_ref,
-    halo_ref,
+    near_refs,
+    far_refs,
     listed_ref,
     scale_ref,
     shift_ref,
@@ -133,17 +136,10 @@
     third_ref,
     fit_bias_third_ref,
     readout_ref,
+    own_ref,
+    halo_ref,
     arrived,
 ):
-    live = live_ref[0]
-    octets = (live + (OCTET - 1)) // OCTET
-    atoms, slots = listed_ref.shape
-    e1 = scale_ref.shape[1]
-    e2 = two_ref.shape[1]
-    e3 = three_ref.shape[1]
-    rows_one, rows_two, rows_three = two_in.shape[0], three_in.shape[0], three_out.shape[0]
-    copies_two, copies_three = e2 // e1, e3 // e1
-
     late = [
         pltpu.make_async_copy(source, target, arrived.at[k])
         for k, (source, target) in enumerate(
@@ -160,6 +156,21 @@
     ]
     for copy in late:
         copy.start()
+    if len(near_refs) > 1:
+        own_ref[...] = field_table(*near_refs)
+        table = field_table(*far_refs[:2])
+        halo_ref[...] = lookup(table, jnp.broadcast_to(turned_rows(far_refs[2]), table.shape))
+    else:
+        own_ref[...] = near_refs[0][...]
+        halo_ref[...] = far_refs[0][...]
+    live = live_ref[0]
+    octets = (live + (OCTET - 1)) // OCTET
+    atoms, slots = listed_ref.shape
+    e1 = scale_ref.shape[1]
+    e2 = two_ref.shape[1]
+    e3 = three_ref.shape[1]
+    rows_one, rows_two, rows_three = two_in.shape[0], three_in.shape[0], three_out.shape[0]
+    copies_two, copies_three = e2 // e1, e3 // e1
 
     def split_bias(bias):
         high = bias.astype(BF16).astype(F32)
@@ -619,9 +630,9 @@
     return jax.ShapeDtypeStruct(dims, dtype)
 
 
-def call_force(live_atoms, own, halo, neighbours, weights, velocities, parcels=1):
+def call_force(live_atoms, near, far, neighbours, weights, velocities, parcels=1):
     atoms, slots = neighbours.shape
-    entries = atoms + halo.shape[1]
+    entries = atoms + far[-1].shape[1]
     e1 = weights[0].shape[1]
     e2 = weights[2].shape[1]
     e3 = weights[4].shape[1]
@@ -633,10 +644,10 @@
     return pl.pallas_call(
         force_kernel,
         out_shape=(shape(OCTET, entries), shape(parcels, OCTET, atoms)),
-        in_specs=[SMEM_SPEC]
-        + [VMEM_SPEC] * 9
-        + [HBM_SPEC] * (len(weights) - 6)
-        + [VMEM_SPEC],
+        in_specs=(SMEM_SPEC, (VMEM_SPEC,) * len(near), (VMEM_SPEC,) * len(far))
+        + (VMEM_SPEC,) * 7
+        + (HBM_SPEC,) * (len(weights) - 6)
+        + (VMEM_SPEC,),
         out_specs=(VMEM_SPEC, VMEM_SPEC),
         scratch_shapes=[
             pltpu.VMEM((atoms, LANES), F32),
@@ -665,10 +676,11 @@
             pltpu.VMEM((OCTET, entries), F32),
         ]
         + [pltpu.VMEM(w.shape, w.dtype) for w in weights[6:]]
+        + [pltpu.VMEM((OCTET, atoms), F32), pltpu.VMEM((OCTET, entries - atoms), F32)]
         + [pltpu.SemaphoreType.DMA((len(weights) - 6,))],
         compiler_params=pltpu.CompilerParams(vmem_limit_bytes=VMEM_LIMIT),
         name="force",
-    )(live_atoms, own, halo, neighbours, *weights, velocities)
+    )(live_atoms, near, far, neighbours, *weights, velocities)
 
 
 def row(array):
@@ -719,8 +731,6 @@
     to_last = [((i + 1) % slabs, i) for i in range(slabs)]
 
     def exchange(outgoing, up, down):
-        if slabs == 2:
-            return lax.ppermute(outgoing, "slab", to_next)
         return jnp.concatenate(
             [
                 lax.ppermute(outgoing[:, up], "slab", to_next),
@@ -731,6 +741,26 @@
 
     low, high = slice(0, half), slice(half, 2 * half)
     types = row(atom_types)
+    place = jnp.stack([lax.axis_index("bead"), lax.axis_index("slab")]).astype(jnp.int32)
+    scalars = jnp.concatenate([live_atoms, place[1:]])
+    table = jnp.asarray(bead_tables(beads))
+    sharded_shape = shape(*positions.shape)
+    if slabs == 2:
+        far = tuple(lax.ppermute(a, "slab", to_next) for a in (positions, types, halo_rows))
+        part, parcels = call_force(
+            scalars, (positions, types), far, neighbours, weights, velocities, beads * slabs
+        )
+        gathered = lax.all_to_all(
+            parcels, ("bead", "slab"), split_axis=0, concat_axis=0, tiled=True
+        )
+        return pl.pallas_call(
+            settle_kernel,
+            out_shape=(sharded_shape,) * 3,
+            in_specs=[SMEM_SPEC] * 2 + [VMEM_SPEC] * 4,
+            out_specs=(VMEM_SPEC,) * 3,
+            compiler_params=SMALL,
+            name="settle",
+        )(place, table, part, gathered, halo_rows, types)
     own, sent = pl.pallas_call(
         outgoing_kernel,
         out_shape=(shape(OCTET, atoms), shape(OCTET, 2 * half)),
@@ -740,26 +770,7 @@
         name="outgoing",
     )(positions, types, halo_rows)
     halo = exchange(sent, low, high)
-    place = jnp.stack([lax.axis_index("bead"), lax.axis_index("slab")]).astype(jnp.int32)
-    scalars = jnp.concatenate([live_atoms, place[1:]])
-    table = jnp.asarray(bead_tables(beads))
-    sharded_shape = shape(*positions.shape)
-    if slabs == 2:
-        part, parcels = call_force(
-            scalars, own, halo, neighbours, weights, velocities, beads * slabs
-        )
-        gathered = lax.all_to_all(
-            parcels, ("bead", "slab"), split_axis=0, concat_axis=0, tiled=True
-        )
-        return pl.pallas_call(
-            settle_kernel,
-            out_shape=(sharded_shape,) * 3,
-            in_specs=[SMEM_SPEC] * 2 + [VMEM_SPEC] * 4,
-            out_specs=(VMEM_SPEC,) * 3,
-            compiler_params=SMALL,
-            name="settle",
-        )(place, table, part, gathered, halo_rows, types)
-    part, _ = call_force(scalars, own, halo, neighbours, weights, velocities)
+    part, _ = call_force(scalars, (own,), (halo,), neighbours, weights, velocities)
     back = exchange(part[:, atoms:], high, low)
     back = jnp.concatenate([back[:, high], back[:, low]], axis=1)
     forces, kicked = pl.pallas_call(

time: 34.9 us -> 34.3 us (0.983)
  Pallas kernels: 15.1 us -> 14.4 us
  local copies, waits for them, and re-layouts: 2.09 us -> 1.42 us
  starting transfers between devices: 7.65 us -> 8.14 us
    unnamed x28, local copies, waits for them, and re-layouts: 2.09 us -> 1.42 us
    pallas_call x1, Pallas kernels: 13.5 us -> 13 us  [call_force(): pl.pallas_call(force_kernel, out_shape=(shape(OCTET, entries), shape(parc...]
    ppermute x1 -> x3, starting transfers between devices: 0.45 us -> 0.96 us  [local(): lax.ppermute(a, 'slab', to_next)]
  transfers between devices with their start and end apart: 2 -> 4, of which waited for: 1 -> 2; matrix products, arithmetic and copies ran while one was open for 0% -> 0% of each run, Pallas kernels for 0% -> 0%
where the time goes in v5:
time: 34.3 us; the launch traced here: 34 us
  Pallas kernels  14.4 us (42%)
  waiting for transfers between devices  8.44 us (25%)
  starting transfers between devices  8.14 us (24%)
  local copies, waits for them, and re-layouts  1.42 us (4%)
  between operations  1.39 us (4%)
    pallas_call x1, Pallas kernels, call_force(): pl.pallas_call(force_kernel, out_shape=(shape(OCTET, entries), shape(parc...  13 us
    all_to_all x1, waiting for transfers between devices, local(): lax.all_to_all(parcels, ('bead', 'slab'), split_axis=0, concat_axis=0, ti...  8.14 us
    all_to_all x1, starting transfers between devices, local(): lax.all_to_all(parcels, ('bead', 'slab'), split_axis=0, concat_axis=0, ti...  7.18 us
    pallas_call x1, Pallas kernels, local(): pl.pallas_call(settle_kernel, out_shape=(sharded_shape,) * 3, in_specs=[S...  1.47 us
    unnamed x28, local copies, waits for them, and re-layouts  1.42 us
    ppermute x3, starting transfers between devices, local(): lax.ppermute(a, 'slab', to_next)  0.96 us
  transfers between devices with their start and end apart: 4, of which 2 were waited for; matrix products, arithmetic and copies ran while one was open for 0% of the time, Pallas kernels for 0%

profile of v5, /device:TPU:0, one launch (start us, length us, event | category | flops | bytes accessed | tf_op | source)
XLA Modules:
  0.0 34.0 jit_solution(17032501472169915832)
XLA Ops:
  0.6 0.0 copy-start.3
  0.6 0.0 copy-start.13
  0.7 0.6 %copy-done.3 = s32[128]{0:T(128)S(1)} copy-done((s32[128]{0:T(128)S(1)}, s32[128]{0:T(128)}, u32[]{:S(2)}) %copy-start.3) | copy-done | bytes 536
  1.3 0.5 %collective-permute-start.1 = (s32[1,128]{1,0:T(1,128)S(1)}, s32[1,128]{1,0:T(1,128)S(1)}, u32[]{:S(2)}, u32[]{:S(2)}) collective-permute-start(s32[1,128]{1,0:T(1,128)S(1)} %bitcast.9), channel_id=1, source_target_pairs={{0,1},{1,0},{2,3},{3,2},{4,5},{5,4},{6,7},{7,6},{8,9},{9,8},{10,11... | collective-permute-start | bytes 1544 | tf_op jit(solution)/shard_map/ppermute | solution.py:749
  1.7 0.0 copy-done.13
  1.7 0.1 collective-permute-start.2
  1.8 0.5 %collective-permute-start = (f32[3,1,128]{2,1,0:T(1,128)}, f32[3,1,128]{2,1,0:T(1,128)S(1)}, u32[]{:S(2)}, u32[]{:S(2)}) collective-permute-start(f32[3,1,128]{2,1,0:T(1,128)} %near_refs_0_.1), channel_id=1, source_target_pairs={{0,1},{1,0},{2,3},{3,2},{4,5},{5,4},{6,7},{7,6},{8,9},{9,8},{10,11... | collective-permute-start | bytes 4616 | tf_op jit(solution)/shard_map/ppermute | solution.py:749
  2.9 0.1 pad_add_fusion.1.live_ref
  3.0 0.0 collective-permute-done.1.far_refs_1_
  3.0 0.0 collective-permute-done.2.far_refs_2_
  3.0 0.3 collective-permute-done.far_refs_0_
  3.3 0.0 copy-start.6
  3.3 0.0 copy-start.7
  3.3 0.0 copy-start.5
  3.3 0.0 copy-start.2
  3.3 0.0 copy-start.4
  3.4 0.6 %copy-done.10 = f32[240]{0:T(256)S(1)} copy-done((f32[240]{0:T(256)S(1)}, f32[240]{0:T(256)}, u32[]{:S(2)}) %copy-start.10) | copy-done | bytes 984
  4.0 0.0 copy-done.11
  4.0 0.0 copy-done.12
  4.0 0.0 copy-done.8
  4.0 0.0 copy-done.9
  4.0 0.0 copy-done.6
  4.0 0.0 copy-done.7
  4.1 0.0 copy-done.5
  4.1 0.0 copy-done.2
  4.1 0.0 copy-done.4
  4.1 13.0 %force.1 = (f32[8,256]{1,0:T(8,128)}, f32[32,8,128]{2,1,0:T(8,128)}) custom-call(s32[2]{0:T(128)S(1)} %pad_add_fusion.1.live_ref, f32[3,1,128]{2,1,0:T(1,128)S(1)} %copy-done.4, s32[1,128]{1,0:T(1,128)S(1)} %bitcast.10, f32[3,1,128]{2,1,0:T(1,128)S(1)} %collective-permute-done.far_refs_0_, s32[1,128]{1,0:T(1,128)S(1)} %collective-permute-done.1.far_refs_1_, ...), custom_call_target="tpu_custom_call" | custom-call | tf_op jit(solution)/shard_map/force/pallas_call | solution.py:644
  17.1 7.2 %all-to-all-start = ((f32[32,8,128]{2,1,0:T(8,128)}), f32[32,8,128]{2,1,0:T(8,128)S(1)}, u32[]{:S(2)}, u32[]{:S(2)}) async-start(f32[32,8,128]{2,1,0:T(8,128)} %get-tuple-element.6), calls=%async_computation | async-start | bytes 262144 | tf_op jit(solution)/shard_map/all_to_all | solution.py:753
  24.3 0.0 copy-start
  24.3 0.1 pad_add_fusion.place_ref
  24.4 8.1 %all-to-all-done.gathered_ref = f32[32,8,128]{2,1,0:T(8,128)S(1)} async-done(((f32[32,8,128]{2,1,0:T(8,128)}), f32[32,8,128]{2,1,0:T(8,128)S(1)}, u32[]{:S(2)}, u32[]{:S(2)}) %all-to-all-start) | async-done | bytes 131104 | tf_op jit(solution)/shard_map/all_to_all | solution.py:753
  32.5 1.5 %settle.1 = (f32[3,1,128]{2,1,0:T(1,128)}, f32[3,1,128]{2,1,0:T(1,128)}, f32[3,1,128]{2,1,0:T(1,128)}) custom-call(s32[2]{0:T(128)S(1)} %pad_add_fusion.place_ref, f32[16,48]{1,0:T(8,128)S(1)} %copy-done, f32[8,256]{1,0:T(8,128)S(1)} %copy-done.1, f32[32,8,128]{2,1,0:T(8,128)S(1)} %all-to-all-done.gathered_ref, s32[1,128]{1,0:T(1,128)S(1)} %copy-done.13, ...), custom_call_target="tpu_custom_call" | custom-call | tf_op jit(solution)/shard_map/settle/pallas_call | solution.py:756
  (8 shorter events, 0.0 us)
Async XLA Ops:
  0.6 0.7 %copy-start.3 = (s32[128]{0:T(128)S(1)}, s32[128]{0:T(128)}, u32[]{:S(2)}) copy-start(s32[128]{0:T(128)} %param.22) | copy-start | bytes 1540
  0.6 1.1 %copy-start.13 = (s32[1,128]{1,0:T(1,128)S(1)}, s32[1,128]{1,0:T(1,128)}, u32[]{:S(2)}) copy-start(s32[1,128]{1,0:T(1,128)} %rows_ref.1) | copy-start | bytes 1540
  1.3 1.7 %collective-permute-start.1 = (s32[1,128]{1,0:T(1,128)S(1)}, s32[1,128]{1,0:T(1,128)S(1)}, u32[]{:S(2)}, u32[]{:S(2)}) collective-permute-start(s32[1,128]{1,0:T(1,128)S(1)} %bitcast.9), channel_id=1, source_target_pairs={{0,1},{1,0},{2,3},{3,2},{4,5},{5,4},{6,7},{7,6},{8,9},{9,8},{10,11... | collective-permute-start | bytes 1544 | tf_op jit(solution)/shard_map/ppermute | solution.py:749
  1.7 1.2 %collective-permute-start.2 = (s32[1,128]{1,0:T(1,128)S(1)}, s32[1,128]{1,0:T(1,128)S(1)}, u32[]{:S(2)}, u32[]{:S(2)}) collective-permute-start(s32[1,128]{1,0:T(1,128)S(1)} %copy-done.13), channel_id=1, source_target_pairs={{0,1},{1,0},{2,3},{3,2},{4,5},{5,4},{6,7},{7,6},{8,9},{9,8},{10,11... | collective-permute-start | bytes 1544 | tf_op jit(solution)/shard_map/ppermute | solution.py:749
  1.8 1.5 %collective-permute-start = (f32[3,1,128]{2,1,0:T(1,128)}, f32[3,1,128]{2,1,0:T(1,128)S(1)}, u32[]{:S(2)}, u32[]{:S(2)}) collective-permute-start(f32[3,1,128]{2,1,0:T(1,128)} %near_refs_0_.1), channel_id=1, source_target_pairs={{0,1},{1,0},{2,3},{3,2},{4,5},{5,4},{6,7},{7,6},{8,9},{9,8},{10,11... | collective-permute-start | bytes 4616 | tf_op jit(solution)/shard_map/ppermute | solution.py:749
  3.3 0.7 %copy-start.10 = (f32[240]{0:T(256)S(1)}, f32[240]{0:T(256)}, u32[]{:S(2)}) copy-start(f32[240]{0:T(256)} %param.37) | copy-start | bytes 2884
  3.3 0.7 %copy-start.11 = (f32[50]{0:T(128)S(1)}, f32[50]{0:T(128)}, u32[]{:S(2)}) copy-start(f32[50]{0:T(128)} %param.29) | copy-start | bytes 604
  3.3 0.7 %copy-start.12 = (f32[100]{0:T(128)S(1)}, f32[100]{0:T(128)}, u32[]{:S(2)}) copy-start(f32[100]{0:T(128)} %param.31) | copy-start | bytes 1204
  3.3 0.7 %copy-start.8 = (f32[240]{0:T(256)S(1)}, f32[240]{0:T(256)}, u32[]{:S(2)}) copy-start(f32[240]{0:T(256)} %param.33) | copy-start | bytes 2884
  3.3 0.7 %copy-start.9 = (f32[240]{0:T(256)S(1)}, f32[240]{0:T(256)}, u32[]{:S(2)}) copy-start(f32[240]{0:T(256)} %param.35) | copy-start | bytes 2884
  3.3 0.7 %copy-start.6 = (f32[2,25]{1,0:T(2,128)S(1)}, f32[2,25]{1,0:T(2,128)}, u32[]{:S(2)}) copy-start(f32[2,25]{1,0:T(2,128)} %scale_ref.1) | copy-start | bytes 604
  3.3 0.7 %copy-start.7 = (f32[2,25]{1,0:T(2,128)S(1)}, f32[2,25]{1,0:T(2,128)}, u32[]{:S(2)}) copy-start(f32[2,25]{1,0:T(2,128)} %shift_ref.1) | copy-start | bytes 604
  3.3 0.8 %copy-start.5 = (f32[3,1,128]{2,1,0:T(1,128)S(1)}, f32[3,1,128]{2,1,0:T(1,128)}, u32[]{:S(2)}) copy-start(f32[3,1,128]{2,1,0:T(1,128)} %velocities_ref.1) | copy-start | bytes 4612
  3.3 0.8 %copy-start.2 = (f32[2,240]{1,0:T(2,128)S(1)}, f32[2,240]{1,0:T(2,128)}, u32[]{:S(2)}) copy-start(f32[2,240]{1,0:T(2,128)} %readout_hbm.1) | copy-start | bytes 5764
  3.3 0.8 %copy-start.4 = (f32[3,1,128]{2,1,0:T(1,128)S(1)}, f32[3,1,128]{2,1,0:T(1,128)}, u32[]{:S(2)}) copy-start(f32[3,1,128]{2,1,0:T(1,128)} %near_refs_0_.1) | copy-start | bytes 4612
  17.1 15.4 %copy-start.1 = (f32[8,256]{1,0:T(8,128)S(1)}, f32[8,256]{1,0:T(8,128)}, u32[]{:S(2)}) copy-start(f32[8,256]{1,0:T(8,128)} %get-tuple-element.5.part_ref) | copy-start | bytes 24580
  17.1 15.4 %all-to-all-start = ((f32[32,8,128]{2,1,0:T(8,128)}), f32[32,8,128]{2,1,0:T(8,128)S(1)}, u32[]{:S(2)}, u32[]{:S(2)}) async-start(f32[32,8,128]{2,1,0:T(8,128)} %get-tuple-element.6), calls=%async_computation | async-start | bytes 262144 | tf_op jit(solution)/shard_map/all_to_all | solution.py:753
  24.3 8.2 %copy-start = (f32[16,48]{1,0:T(8,128)S(1)}, f32[16,48]{1,0:T(8,128)}, u32[]{:S(2)}) copy-start(f32[16,48]{1,0:T(8,128)} %constant.10.clone.table_ref) | copy-start | bytes 9220

commit v6 on v5

--- a/solution.py
+++ b/solution.py
@@ -157,7 +157,7 @@
     for copy in late:
         copy.start()
     if len(near_refs) > 1:
-        own_ref[...] = field_table(*near_refs)
+        own_ref[...] = field_table(*near_refs[:2])
         table = field_table(*far_refs[:2])
         halo_ref[...] = lookup(table, jnp.broadcast_to(turned_rows(far_refs[2]), table.shape))
     else:
@@ -522,6 +522,8 @@
             velocities_ref[c] + kick * force[c : c + 1] for c in range(3)
         ]
         moving = jnp.concatenate(moving + [jnp.zeros((OCTET - 6, atoms), F32)], axis=0)
+        out_ref[3:4, 0:atoms] = kick
+        out_ref[4:5, 0:atoms] = turned_rows(near_refs[2]).astype(F32)
         for s in range(2):
             tile = jnp.where(mine == s, moving, beyond)
             for b in range(parcels_ref.shape[0] // 2):
@@ -573,7 +575,7 @@
 
 
 def settle_kernel(
-    place_ref, table_ref, part_ref, gathered_ref, rows_ref, types_ref, positions_ref, velocities_ref, forces_ref
+    place_ref, table_ref, part_ref, gathered_ref, positions_ref, velocities_ref, forces_ref
 ):
     mine, slab = place_ref[0], place_ref[1]
     count = gathered_ref.shape[0] // 2
@@ -590,8 +592,8 @@
         crossed = crossed + jnp.where(is_position, -spring, travel) * tile
         halo_turned = halo_turned + cosine * beyond
         halo_travel = halo_travel + travel * beyond
-    rows = turned_rows(rows_ref)
-    atoms = types_ref.shape[1]
+    atoms = part_ref.shape[1] - gathered_ref.shape[2]
+    rows = part_ref[4:5, 0:atoms].astype(jnp.int32)
     hits = lax.broadcasted_iota(jnp.int32, (atoms, rows.shape[1]), 0) == rows
     own_beyond = gathered_ref[2 * mine + 1 - slab]
     rest = jnp.concatenate([halo_travel, halo_turned, own_beyond], axis=0)
@@ -607,7 +609,7 @@
     )
     tall = 3 * OCTET
     returned = sums[:tall] + sums[tall : 2 * tall] + sums[2 * tall :]
-    kick = step_size * jnp.where(types_ref[...] == 1, 1.0, 1.0 / heavy_mass)
+    kick = part_ref[3:4, 0:atoms]
     for c in range(3):
         positions_ref[c] = (
             turned[c : c + 1] + crossed[3 + c : 4 + c] + kick * returned[c : c + 1]
@@ -748,7 +750,7 @@
     if slabs == 2:
         far = tuple(lax.ppermute(a, "slab", to_next) for a in (positions, types, halo_rows))
         part, parcels = call_force(
-            scalars, (positions, types), far, neighbours, weights, velocities, beads * slabs
+            scalars, (positions, types, halo_rows), far, neighbours, weights, velocities, beads * slabs
         )
         gathered = lax.all_to_all(
             parcels, ("bead", "slab"), split_axis=0, concat_axis=0, tiled=True
@@ -756,11 +758,11 @@
         return pl.pallas_call(
             settle_kernel,
             out_shape=(sharded_shape,) * 3,
-            in_specs=[SMEM_SPEC] * 2 + [VMEM_SPEC] * 4,
+            in_specs=[SMEM_SPEC] * 2 + [VMEM_SPEC] * 2,
             out_specs=(VMEM_SPEC,) * 3,
             compiler_params=SMALL,
             name="settle",
-        )(place, table, part, gathered, halo_rows, types)
+        )(place, table, part, gathered)
     own, sent = pl.pallas_call(
         outgoing_kernel,
         out_shape=(shape(OCTET, atoms), shape(OCTET, 2 * half)),

time: 34.3 us -> 34 us (level)
  local copies, waits for them, and re-layouts: 1.42 us -> 0.86 us
  Pallas kernels: 14.4 us -> 14.8 us
    unnamed x28, local copies, waits for them, and re-layouts: 1.42 us -> 0.86 us
    pallas_call x1, Pallas kernels: 13 us -> 13.4 us  [call_force(): pl.pallas_call(force_kernel, out_shape=(shape(OCTET, entries), shape(parc...]
where the time goes in v6:
time: 34 us; the launch traced here: 33.7 us
  Pallas kernels  14.8 us (44%)
  starting transfers between devices  8.23 us (24%)
  waiting for transfers between devices  8.23 us (24%)
  between operations  1.39 us (4%)
  local copies, waits for them, and re-layouts  0.86 us (3%)
    pallas_call x1, Pallas kernels, call_force(): pl.pallas_call(force_kernel, out_shape=(shape(OCTET, entries), shape(parc...  13.4 us
    all_to_all x1, waiting for transfers between devices, local(): lax.all_to_all(parcels, ('bead', 'slab'), split_axis=0, concat_axis=0, ti...  8.14 us
    all_to_all x1, starting transfers between devices, local(): lax.all_to_all(parcels, ('bead', 'slab'), split_axis=0, concat_axis=0, ti...  7.18 us
    pallas_call x1, Pallas kernels, local(): pl.pallas_call(settle_kernel, out_shape=(sharded_shape,) * 3, in_specs=[S...  1.41 us
    ppermute x3, starting transfers between devices, local(): lax.ppermute(a, 'slab', to_next)  1.05 us
    unnamed x28, local copies, waits for them, and re-layouts  0.86 us
  transfers between devices with their start and end apart: 4, of which 2 were waited for; matrix products, arithmetic and copies ran while one was open for 0% of the time, Pallas kernels for 0%

profile of v6, /device:TPU:0, one launch (start us, length us, event | category | flops | bytes accessed | tf_op | source)
XLA Modules:
  0.0 33.7 jit_solution(621716713301505804)
XLA Ops:
  0.6 0.5 %collective-permute-start.1 = (s32[1,128]{1,0:T(1,128)}, s32[1,128]{1,0:T(1,128)S(1)}, u32[]{:S(2)}, u32[]{:S(2)}) collective-permute-start(s32[1,128]{1,0:T(1,128)} %bitcast.12), channel_id=1, source_target_pairs={{0,1},{1,0},{2,3},{3,2},{4,5},{5,4},{6,7},{7,6},{8,9},{9,8},{10,11... | collective-permute-start | bytes 1544 | tf_op jit(solution)/shard_map/ppermute | solution.py:751
  1.2 0.1 collective-permute-start.2
  1.2 0.1 copy-done.3
  1.3 0.5 %collective-permute-start = (f32[3,1,128]{2,1,0:T(1,128)S(1)}, f32[3,1,128]{2,1,0:T(1,128)S(1)}, u32[]{:S(2)}, u32[]{:S(2)}) collective-permute-start(f32[3,1,128]{2,1,0:T(1,128)S(1)} %copy-done.3), channel_id=1, source_target_pairs={{0,1},{1,0},{2,3},{3,2},{4,5},{5,4},{6,7},{7,6},{8,9},{9,8},{10,11... | collective-permute-start | bytes 4616 | tf_op jit(solution)/shard_map/ppermute | solution.py:751
  2.4 0.1 pad_add_fusion.1.live_ref
  2.5 0.0 collective-permute-done.1.far_refs_1_
  2.5 0.0 collective-permute-done.2.far_refs_2_
  2.5 0.1 collective-permute-done.far_refs_0_
  2.6 0.0 copy-start.7
  2.6 0.0 copy-start.8
  2.6 0.0 copy-start.5
  2.6 0.0 copy-start.6
  2.6 0.0 copy-start.2
  2.7 0.0 copy-start.4
  2.7 0.6 %copy-done.11 = s32[1,128]{1,0:T(1,128)S(1)} copy-done((s32[1,128]{1,0:T(1,128)S(1)}, s32[1,128]{1,0:T(1,128)}, u32[]{:S(2)}) %copy-start.11) | copy-done | bytes 536
  3.2 0.0 copy-done.12
  3.3 0.0 copy-done.13
  3.3 0.0 copy-done.9
  3.3 0.0 copy-done.10
  3.3 0.0 copy-done.7
  3.3 0.0 copy-done.8
  3.4 0.0 copy-done.5
  3.4 0.0 copy-done.6
  3.4 0.0 copy-done.2
  3.4 0.0 copy-done.4
  3.4 13.4 %force.1 = (f32[8,256]{1,0:T(8,128)}, f32[32,8,128]{2,1,0:T(8,128)}) custom-call(s32[2]{0:T(128)S(1)} %pad_add_fusion.1.live_ref, f32[3,1,128]{2,1,0:T(1,128)S(1)} %copy-done.3, s32[1,128]{1,0:T(1,128)S(1)} %bitcast.13, s32[1,128]{1,0:T(1,128)S(1)} %copy-done.11, f32[3,1,128]{2,1,0:T(1,128)S(1)} %collective-permute-done.far_refs_0_, ...), custom_call_target="tpu_custom_call" | custom-call | tf_op jit(solution)/shard_map/force/pallas_call | solution.py:646
  16.8 7.2 %all-to-all-start = ((f32[32,8,128]{2,1,0:T(8,128)}), f32[32,8,128]{2,1,0:T(8,128)S(1)}, u32[]{:S(2)}, u32[]{:S(2)}) async-start(f32[32,8,128]{2,1,0:T(8,128)} %get-tuple-element.6), calls=%async_computation | async-start | bytes 262144 | tf_op jit(solution)/shard_map/all_to_all | solution.py:755
  24.0 0.0 copy-start
  24.0 0.1 pad_add_fusion.place_ref
  24.1 8.1 %all-to-all-done.gathered_ref = f32[32,8,128]{2,1,0:T(8,128)S(1)} async-done(((f32[32,8,128]{2,1,0:T(8,128)}), f32[32,8,128]{2,1,0:T(8,128)S(1)}, u32[]{:S(2)}, u32[]{:S(2)}) %all-to-all-start) | async-done | bytes 131104 | tf_op jit(solution)/shard_map/all_to_all | solution.py:755
  32.2 0.0 copy-done.1
  32.2 1.4 %settle.1 = (f32[3,1,128]{2,1,0:T(1,128)}, f32[3,1,128]{2,1,0:T(1,128)}, f32[3,1,128]{2,1,0:T(1,128)}) custom-call(s32[2]{0:T(128)S(1)} %pad_add_fusion.place_ref, f32[16,48]{1,0:T(8,128)S(1)} %copy-done, f32[8,256]{1,0:T(8,128)S(1)} %copy-done.1, f32[32,8,128]{2,1,0:T(8,128)S(1)} %all-to-all-done.gathered_ref), custom_call_target="tpu_custom_call" | custom-call | tf_op jit(solution)/shard_map/settle/pallas_call | solution.py:758
  (8 shorter events, 0.0 us)
Async XLA Ops:
  0.6 0.7 %copy-start.3 = (f32[3,1,128]{2,1,0:T(1,128)S(1)}, f32[3,1,128]{2,1,0:T(1,128)}, u32[]{:S(2)}) copy-start(f32[3,1,128]{2,1,0:T(1,128)} %near_refs_0_.1) | copy-start | bytes 4612
  0.6 1.9 %collective-permute-start.1 = (s32[1,128]{1,0:T(1,128)}, s32[1,128]{1,0:T(1,128)S(1)}, u32[]{:S(2)}, u32[]{:S(2)}) collective-permute-start(s32[1,128]{1,0:T(1,128)} %bitcast.12), channel_id=1, source_target_pairs={{0,1},{1,0},{2,3},{3,2},{4,5},{5,4},{6,7},{7,6},{8,9},{9,8},{10,11... | collective-permute-start | bytes 1544 | tf_op jit(solution)/shard_map/ppermute | solution.py:751
  1.2 1.3 %collective-permute-start.2 = (s32[1,128]{1,0:T(1,128)}, s32[1,128]{1,0:T(1,128)S(1)}, u32[]{:S(2)}, u32[]{:S(2)}) collective-permute-start(s32[1,128]{1,0:T(1,128)} %near_refs_2_.1), channel_id=1, source_target_pairs={{0,1},{1,0},{2,3},{3,2},{4,5},{5,4},{6,7},{7,6},{8,9},{9,8},{10,11... | collective-permute-start | bytes 1544 | tf_op jit(solution)/shard_map/ppermute | solution.py:751
  1.3 1.3 %collective-permute-start = (f32[3,1,128]{2,1,0:T(1,128)S(1)}, f32[3,1,128]{2,1,0:T(1,128)S(1)}, u32[]{:S(2)}, u32[]{:S(2)}) collective-permute-start(f32[3,1,128]{2,1,0:T(1,128)S(1)} %copy-done.3), channel_id=1, source_target_pairs={{0,1},{1,0},{2,3},{3,2},{4,5},{5,4},{6,7},{7,6},{8,9},{9,8},{10,11... | collective-permute-start | bytes 4616 | tf_op jit(solution)/shard_map/ppermute | solution.py:751
  2.6 0.7 %copy-start.11 = (s32[1,128]{1,0:T(1,128)S(1)}, s32[1,128]{1,0:T(1,128)}, u32[]{:S(2)}) copy-start(s32[1,128]{1,0:T(1,128)} %near_refs_2_.1) | copy-start | bytes 1540
  2.6 0.7 %copy-start.12 = (f32[50]{0:T(128)S(1)}, f32[50]{0:T(128)}, u32[]{:S(2)}) copy-start(f32[50]{0:T(128)} %param.29) | copy-start | bytes 604
  2.6 0.7 %copy-start.13 = (f32[100]{0:T(128)S(1)}, f32[100]{0:T(128)}, u32[]{:S(2)}) copy-start(f32[100]{0:T(128)} %param.31) | copy-start | bytes 1204
  2.6 0.7 %copy-start.9 = (f32[240]{0:T(256)S(1)}, f32[240]{0:T(256)}, u32[]{:S(2)}) copy-start(f32[240]{0:T(256)} %param.37) | copy-start | bytes 2884
  2.6 0.7 %copy-start.10 = (s32[128]{0:T(128)S(1)}, s32[128]{0:T(128)}, u32[]{:S(2)}) copy-start(s32[128]{0:T(128)} %param.22) | copy-start | bytes 1540
  2.6 0.7 %copy-start.7 = (f32[240]{0:T(256)S(1)}, f32[240]{0:T(256)}, u32[]{:S(2)}) copy-start(f32[240]{0:T(256)} %param.33) | copy-start | bytes 2884
  2.6 0.7 %copy-start.8 = (f32[240]{0:T(256)S(1)}, f32[240]{0:T(256)}, u32[]{:S(2)}) copy-start(f32[240]{0:T(256)} %param.35) | copy-start | bytes 2884
  2.6 0.7 %copy-start.5 = (f32[2,25]{1,0:T(2,128)S(1)}, f32[2,25]{1,0:T(2,128)}, u32[]{:S(2)}) copy-start(f32[2,25]{1,0:T(2,128)} %scale_ref.1) | copy-start | bytes 604
  2.6 0.8 %copy-start.6 = (f32[2,25]{1,0:T(2,128)S(1)}, f32[2,25]{1,0:T(2,128)}, u32[]{:S(2)}) copy-start(f32[2,25]{1,0:T(2,128)} %shift_ref.1) | copy-start | bytes 604
  2.6 0.8 %copy-start.2 = (f32[2,240]{1,0:T(2,128)S(1)}, f32[2,240]{1,0:T(2,128)}, u32[]{:S(2)}) copy-start(f32[2,240]{1,0:T(2,128)} %readout_hbm.1) | copy-start | bytes 5764
  2.7 0.8 %copy-start.4 = (f32[3,1,128]{2,1,0:T(1,128)S(1)}, f32[3,1,128]{2,1,0:T(1,128)}, u32[]{:S(2)}) copy-start(f32[3,1,128]{2,1,0:T(1,128)} %velocities_ref.1) | copy-start | bytes 4612
  16.8 15.4 %copy-start.1 = (f32[8,256]{1,0:T(8,128)S(1)}, f32[8,256]{1,0:T(8,128)}, u32[]{:S(2)}) copy-start(f32[8,256]{1,0:T(8,128)} %get-tuple-element.5.part_ref) | copy-start | bytes 24580
  16.8 15.4 %all-to-all-start = ((f32[32,8,128]{2,1,0:T(8,128)}), f32[32,8,128]{2,1,0:T(8,128)S(1)}, u32[]{:S(2)}, u32[]{:S(2)}) async-start(f32[32,8,128]{2,1,0:T(8,128)} %get-tuple-element.6), calls=%async_computation | async-start | bytes 262144 | tf_op jit(solution)/shard_map/all_to_all | solution.py:755
  24.0 8.2 %copy-start = (f32[16,48]{1,0:T(8,128)S(1)}, f32[16,48]{1,0:T(8,128)}, u32[]{:S(2)}) copy-start(f32[16,48]{1,0:T(8,128)} %constant.10.clone.table_ref) | copy-start | bytes 9220

commit v7 on v6

--- a/solution.py
+++ b/solution.py
@@ -189,12 +189,13 @@
 
     padded[...] = jnp.zeros_like(padded)
     bias_high, bias_low = split_bias(bias_three_ref[...])
+    three = three_ref[...].astype(F32)
     for k in range(copies_three):
         cols = slice(k * e1, (k + 1) * e1)
         for m in range(copies_two):
-            padded[m * CHUNK : m * CHUNK + e1, k * CHUNK : k * CHUNK + e1] = three_ref[
+            padded[m * CHUNK : m * CHUNK + e1, k * CHUNK : k * CHUNK + e1] = three[
                 m * e1 : (m + 1) * e1, cols
-            ].astype(F32)
+            ]
         padded[e1 : e1 + 1, k * CHUNK : k * CHUNK + e1] = bias_high[:, cols]
         padded[e1 + 1 : e1 + 2, k * CHUNK : k * CHUNK + e1] = bias_low[:, cols]
     table = padded[...]

time: 34 us -> 34 us (level)
  no operation moved by 1% of the time
where the time goes in v7:
time: 34 us; the launch traced here: 33.7 us
  Pallas kernels  14.8 us (44%)
  starting transfers between devices  8.24 us (24%)
  waiting for transfers between devices  8.23 us (24%)
  between operations  1.39 us (4%)
  local copies, waits for them, and re-layouts  0.86 us (3%)
    pallas_call x1, Pallas kernels, call_force(): pl.pallas_call(force_kernel, out_shape=(shape(OCTET, entries), shape(parc...  13.4 us
    all_to_all x1, waiting for transfers between devices, local(): lax.all_to_all(parcels, ('bead', 'slab'), split_axis=0, concat_axis=0, ti...  8.14 us
    all_to_all x1, starting transfers between devices, local(): lax.all_to_all(parcels, ('bead', 'slab'), split_axis=0, concat_axis=0, ti...  7.18 us
    pallas_call x1, Pallas kernels, local(): pl.pallas_call(settle_kernel, out_shape=(sharded_shape,) * 3, in_specs=[S...  1.41 us
    ppermute x3, starting transfers between devices, local(): lax.ppermute(a, 'slab', to_next)  1.05 us
    unnamed x28, local copies, waits for them, and re-layouts  0.86 us
  transfers between devices with their start and end apart: 4, of which 2 were waited for; matrix products, arithmetic and copies ran while one was open for 0% of the time, Pallas kernels for 0%

profile of v7, /device:TPU:0, one launch (start us, length us, event | category | flops | bytes accessed | tf_op | source)
XLA Modules:
  0.0 33.7 jit_solution(13082432504302619106)
XLA Ops:
  0.6 0.5 %collective-permute-start.1 = (s32[1,128]{1,0:T(1,128)}, s32[1,128]{1,0:T(1,128)S(1)}, u32[]{:S(2)}, u32[]{:S(2)}) collective-permute-start(s32[1,128]{1,0:T(1,128)} %bitcast.12), channel_id=1, source_target_pairs={{0,1},{1,0},{2,3},{3,2},{4,5},{5,4},{6,7},{7,6},{8,9},{9,8},{10,11... | collective-permute-start | bytes 1544 | tf_op jit(solution)/shard_map/ppermute | solution.py:752
  1.2 0.1 collective-permute-start.2
  1.2 0.1 copy-done.3
  1.3 0.5 %collective-permute-start = (f32[3,1,128]{2,1,0:T(1,128)S(1)}, f32[3,1,128]{2,1,0:T(1,128)S(1)}, u32[]{:S(2)}, u32[]{:S(2)}) collective-permute-start(f32[3,1,128]{2,1,0:T(1,128)S(1)} %copy-done.3), channel_id=1, source_target_pairs={{0,1},{1,0},{2,3},{3,2},{4,5},{5,4},{6,7},{7,6},{8,9},{9,8},{10,11... | collective-permute-start | bytes 4616 | tf_op jit(solution)/shard_map/ppermute | solution.py:752
  2.4 0.1 pad_add_fusion.1.live_ref
  2.5 0.0 collective-permute-done.1.far_refs_1_
  2.5 0.0 collective-permute-done.2.far_refs_2_
  2.5 0.1 collective-permute-done.far_refs_0_
  2.6 0.0 copy-start.7
  2.6 0.0 copy-start.8
  2.6 0.0 copy-start.5
  2.6 0.0 copy-start.6
  2.6 0.0 copy-start.2
  2.7 0.0 copy-start.4
  2.7 0.6 %copy-done.11 = s32[1,128]{1,0:T(1,128)S(1)} copy-done((s32[1,128]{1,0:T(1,128)S(1)}, s32[1,128]{1,0:T(1,128)}, u32[]{:S(2)}) %copy-start.11) | copy-done | bytes 536
  3.2 0.0 copy-done.12
  3.3 0.0 copy-done.13
  3.3 0.0 copy-done.9
  3.3 0.0 copy-done.10
  3.3 0.0 copy-done.7
  3.3 0.0 copy-done.8
  3.4 0.0 copy-done.5
  3.4 0.0 copy-done.6
  3.4 0.0 copy-done.2
  3.4 0.0 copy-done.4
  3.4 13.4 %force.1 = (f32[8,256]{1,0:T(8,128)}, f32[32,8,128]{2,1,0:T(8,128)}) custom-call(s32[2]{0:T(128)S(1)} %pad_add_fusion.1.live_ref, f32[3,1,128]{2,1,0:T(1,128)S(1)} %copy-done.3, s32[1,128]{1,0:T(1,128)S(1)} %bitcast.13, s32[1,128]{1,0:T(1,128)S(1)} %copy-done.11, f32[3,1,128]{2,1,0:T(1,128)S(1)} %collective-permute-done.far_refs_0_, ...), custom_call_target="tpu_custom_call" | custom-call | tf_op jit(solution)/shard_map/force/pallas_call | solution.py:647
  16.8 7.2 %all-to-all-start = ((f32[32,8,128]{2,1,0:T(8,128)}), f32[32,8,128]{2,1,0:T(8,128)S(1)}, u32[]{:S(2)}, u32[]{:S(2)}) async-start(f32[32,8,128]{2,1,0:T(8,128)} %get-tuple-element.6), calls=%async_computation | async-start | bytes 262144 | tf_op jit(solution)/shard_map/all_to_all | solution.py:756
  24.0 0.0 copy-start
  24.0 0.1 pad_add_fusion.place_ref
  24.1 8.1 %all-to-all-done.gathered_ref = f32[32,8,128]{2,1,0:T(8,128)S(1)} async-done(((f32[32,8,128]{2,1,0:T(8,128)}), f32[32,8,128]{2,1,0:T(8,128)S(1)}, u32[]{:S(2)}, u32[]{:S(2)}) %all-to-all-start) | async-done | bytes 131104 | tf_op jit(solution)/shard_map/all_to_all | solution.py:756
  32.2 0.0 copy-done.1
  32.2 1.4 %settle.1 = (f32[3,1,128]{2,1,0:T(1,128)}, f32[3,1,128]{2,1,0:T(1,128)}, f32[3,1,128]{2,1,0:T(1,128)}) custom-call(s32[2]{0:T(128)S(1)} %pad_add_fusion.place_ref, f32[16,48]{1,0:T(8,128)S(1)} %copy-done, f32[8,256]{1,0:T(8,128)S(1)} %copy-done.1, f32[32,8,128]{2,1,0:T(8,128)S(1)} %all-to-all-done.gathered_ref), custom_call_target="tpu_custom_call" | custom-call | tf_op jit(solution)/shard_map/settle/pallas_call | solution.py:759
  (8 shorter events, 0.0 us)
Async XLA Ops:
  0.6 0.7 %copy-start.3 = (f32[3,1,128]{2,1,0:T(1,128)S(1)}, f32[3,1,128]{2,1,0:T(1,128)}, u32[]{:S(2)}) copy-start(f32[3,1,128]{2,1,0:T(1,128)} %near_refs_0_.1) | copy-start | bytes 4612
  0.6 1.9 %collective-permute-start.1 = (s32[1,128]{1,0:T(1,128)}, s32[1,128]{1,0:T(1,128)S(1)}, u32[]{:S(2)}, u32[]{:S(2)}) collective-permute-start(s32[1,128]{1,0:T(1,128)} %bitcast.12), channel_id=1, source_target_pairs={{0,1},{1,0},{2,3},{3,2},{4,5},{5,4},{6,7},{7,6},{8,9},{9,8},{10,11... | collective-permute-start | bytes 1544 | tf_op jit(solution)/shard_map/ppermute | solution.py:752
  1.2 1.3 %collective-permute-start.2 = (s32[1,128]{1,0:T(1,128)}, s32[1,128]{1,0:T(1,128)S(1)}, u32[]{:S(2)}, u32[]{:S(2)}) collective-permute-start(s32[1,128]{1,0:T(1,128)} %near_refs_2_.1), channel_id=1, source_target_pairs={{0,1},{1,0},{2,3},{3,2},{4,5},{5,4},{6,7},{7,6},{8,9},{9,8},{10,11... | collective-permute-start | bytes 1544 | tf_op jit(solution)/shard_map/ppermute | solution.py:752
  1.3 1.3 %collective-permute-start = (f32[3,1,128]{2,1,0:T(1,128)S(1)}, f32[3,1,128]{2,1,0:T(1,128)S(1)}, u32[]{:S(2)}, u32[]{:S(2)}) collective-permute-start(f32[3,1,128]{2,1,0:T(1,128)S(1)} %copy-done.3), channel_id=1, source_target_pairs={{0,1},{1,0},{2,3},{3,2},{4,5},{5,4},{6,7},{7,6},{8,9},{9,8},{10,11... | collective-permute-start | bytes 4616 | tf_op jit(solution)/shard_map/ppermute | solution.py:752
  2.6 0.7 %copy-start.11 = (s32[1,128]{1,0:T(1,128)S(1)}, s32[1,128]{1,0:T(1,128)}, u32[]{:S(2)}) copy-start(s32[1,128]{1,0:T(1,128)} %near_refs_2_.1) | copy-start | bytes 1540
  2.6 0.7 %copy-start.12 = (f32[50]{0:T(128)S(1)}, f32[50]{0:T(128)}, u32[]{:S(2)}) copy-start(f32[50]{0:T(128)} %param.29) | copy-start | bytes 604
  2.6 0.7 %copy-start.13 = (f32[100]{0:T(128)S(1)}, f32[100]{0:T(128)}, u32[]{:S(2)}) copy-start(f32[100]{0:T(128)} %param.31) | copy-start | bytes 1204
  2.6 0.7 %copy-start.9 = (f32[240]{0:T(256)S(1)}, f32[240]{0:T(256)}, u32[]{:S(2)}) copy-start(f32[240]{0:T(256)} %param.37) | copy-start | bytes 2884
  2.6 0.7 %copy-start.10 = (s32[128]{0:T(128)S(1)}, s32[128]{0:T(128)}, u32[]{:S(2)}) copy-start(s32[128]{0:T(128)} %param.22) | copy-start | bytes 1540
  2.6 0.7 %copy-start.7 = (f32[240]{0:T(256)S(1)}, f32[240]{0:T(256)}, u32[]{:S(2)}) copy-start(f32[240]{0:T(256)} %param.33) | copy-start | bytes 2884
  2.6 0.7 %copy-start.8 = (f32[240]{0:T(256)S(1)}, f32[240]{0:T(256)}, u32[]{:S(2)}) copy-start(f32[240]{0:T(256)} %param.35) | copy-start | bytes 2884
  2.6 0.7 %copy-start.5 = (f32[2,25]{1,0:T(2,128)S(1)}, f32[2,25]{1,0:T(2,128)}, u32[]{:S(2)}) copy-start(f32[2,25]{1,0:T(2,128)} %scale_ref.1) | copy-start | bytes 604
  2.6 0.8 %copy-start.6 = (f32[2,25]{1,0:T(2,128)S(1)}, f32[2,25]{1,0:T(2,128)}, u32[]{:S(2)}) copy-start(f32[2,25]{1,0:T(2,128)} %shift_ref.1) | copy-start | bytes 604
  2.6 0.8 %copy-start.2 = (f32[2,240]{1,0:T(2,128)S(1)}, f32[2,240]{1,0:T(2,128)}, u32[]{:S(2)}) copy-start(f32[2,240]{1,0:T(2,128)} %readout_hbm.1) | copy-start | bytes 5764
  2.7 0.8 %copy-start.4 = (f32[3,1,128]{2,1,0:T(1,128)S(1)}, f32[3,1,128]{2,1,0:T(1,128)}, u32[]{:S(2)}) copy-start(f32[3,1,128]{2,1,0:T(1,128)} %velocities_ref.1) | copy-start | bytes 4612
  16.8 15.4 %copy-start.1 = (f32[8,256]{1,0:T(8,128)S(1)}, f32[8,256]{1,0:T(8,128)}, u32[]{:S(2)}) copy-start(f32[8,256]{1,0:T(8,128)} %get-tuple-element.5.part_ref) | copy-start | bytes 24580
  16.8 15.4 %all-to-all-start = ((f32[32,8,128]{2,1,0:T(8,128)}), f32[32,8,128]{2,1,0:T(8,128)S(1)}, u32[]{:S(2)}, u32[]{:S(2)}) async-start(f32[32,8,128]{2,1,0:T(8,128)} %get-tuple-element.6), calls=%async_computation | async-start | bytes 262144 | tf_op jit(solution)/shard_map/all_to_all | solution.py:756
  24.0 8.2 %copy-start = (f32[16,48]{1,0:T(8,128)S(1)}, f32[16,48]{1,0:T(8,128)}, u32[]{:S(2)}) copy-start(f32[16,48]{1,0:T(8,128)} %constant.10.clone.table_ref) | copy-start | bytes 9220
